TPU v7x, 512 devices: a whole 4x8x8 slice. The times are simulated.
512 devices in a mesh: slab: 16 (over x, z_hi), tile: 32 (over z_lo, y, core).
Axes of the slice: x: 4, y: 8, z: 8 (z_hi: 4, z_lo: 2; z = z_hi * 2 + z_lo), core: 2. Of those that a mesh axis runs over, the one named last changes fastest.
Arguments:
- embed: bfloat16 [16, 64, 128, 128], P('slab', 'tile'), may hold values from -12 to 12
- tissue: int32 [16, 64, 128], P('slab', 'tile'), may hold values 0 or 1
- whiten0: bfloat16 [64, 128, 128], replicated, may hold values from -0.2 to 1.2, as said below
- means0: float32 [64, 128], replicated, may hold values from -0.3 to 0.3
- weights0: float32 [64], replicated, may hold values from 1 to 4
Outputs:
- resp_final: float32 [64, 16, 64, 128], P(None, 'slab', 'tile')
- new_means: float32 [64, 128], P('tile')
- score: float32 [], replicated
Inputs may be any that keep to these rules, and one draw needn't show every extreme that they name: `whiten0`: every whitening matrix is lower triangular with a positive diagonal.
All inputs are finite; a program needn't handle non-finite values. No bound on the sum of `tissue` on one device may be relied on, other than what follows from the above.
Results may differ from a plain program's by a relative error of at most 0.015.
The roundings to bfloat16 on the way count: a program that leaves them out, or rounds other values in their place, can miss the bound.
Values sent between devices are 32-bit elements; how exact they have to be, the bound alone decides.
No kernel may reach another device: no remote copies, remote signals or barrier semaphores. Data moves between devices by JAX's collectives and lax.ppermute only.
A program may use at most 128 MiB of HBM per device.

v0:
```python
import jax
import jax.numpy as jnp
from jax import lax
from jax.sharding import PartitionSpec as P

SWEEPS = 2


BETA_POTTS = 1.0
COV_RIDGE = 0.01
GROUP_SIZE = 8


def extended(cells, sides, width):
    for axis, dim in sides:
        count = lax.axis_size(axis)
        ends = count - 1
        head = lax.slice_in_dim(cells, 0, width, axis=dim)
        tail = lax.slice_in_dim(cells, cells.shape[dim] - width, cells.shape[dim], axis=dim)
        cells = jnp.concatenate(
            [
                lax.ppermute(tail, axis, [(i, (i + 1) % count) for i in range(ends)]),
                cells,
                lax.ppermute(head, axis, [((i + 1) % count, i) for i in range(ends)]),
            ],
            axis=dim,
        )
    return cells


def normalise(scores):
    top = jnp.max(scores, axis=0, keepdims=True)
    expon = jnp.exp(scores - top)
    return expon / jnp.sum(expon, axis=0, keepdims=True)


def neighbour_sum(resp):
    padded = extended(resp, (("slab", 1), ("tile", 2)), 1)
    total = padded[:, 2:, 1:-1, :] + padded[:, :-2, 1:-1, :]
    total = total + padded[:, 1:-1, 2:, :] + padded[:, 1:-1, :-2, :]
    after = jnp.pad(resp[:, :, :, 1:], ((0, 0), (0, 0), (0, 0), (0, 1)))
    before = jnp.pad(resp[:, :, :, :-1], ((0, 0), (0, 0), (0, 0), (1, 0)))
    return total + after + before


def likelihood(flat, whiten_half, shift, offset):
    count = whiten_half.shape[0]
    width = whiten_half.shape[1]

    def per_block(pair):
        matrices, centres = pair
        proj = jnp.einsum("kde,ne->knd", matrices, flat, preferred_element_type=jnp.float32)
        proj = proj - centres[:, None, :]
        return jnp.sum(proj * proj, axis=2)

    quad = lax.map(
        per_block,
        (
            whiten_half.reshape(count // GROUP_SIZE, GROUP_SIZE, width, width),
            shift.reshape(count // GROUP_SIZE, GROUP_SIZE, width),
        ),
    )
    return offset[:, None] - 0.5 * quad.reshape(count, -1)


def mean_field(scores, tissue_f):
    resp = normalise(scores) * tissue_f[None]
    for sweep in range(SWEEPS):
        resp = normalise(scores + BETA_POTTS * neighbour_sum(resp)) * tissue_f[None]
    return resp


def factor(second, first_moment, counts):
    centre = first_moment / counts[:, None]
    ident = jnp.eye(second.shape[1], dtype=jnp.float32)
    sym = 0.5 * (second + jnp.swapaxes(second, 1, 2))
    cov = sym / counts[:, None, None] - centre[:, :, None] * centre[:, None, :] + COV_RIDGE * ident
    lower = jnp.linalg.cholesky(cov)

    def solve_one(lower_one):
        return jax.scipy.linalg.solve_triangular(lower_one, ident, lower=True)

    whiten = jax.vmap(solve_one)(lower)
    logdet = -jnp.sum(jnp.log(jnp.diagonal(lower, axis1=1, axis2=2)), axis=1)
    return (whiten, logdet)


def offsets(whiten_full, centre, logdet, counts):
    shift = jnp.einsum("kde,ke->kd", whiten_full, centre, precision=lax.Precision.HIGHEST)
    return (shift, jnp.log(counts / jnp.sum(counts)) + logdet)


def owned_factor(owned, first_all, counts_all, start):
    share = owned.shape[0]
    first_own = lax.dynamic_slice_in_dim(first_all, start, share, 0)
    counts_own = lax.dynamic_slice_in_dim(counts_all, start, share, 0)
    return factor(owned, first_own, counts_own)


def shards(embed, tissue, whiten0, means0, weights0):
    depth, rows_sec, length, width = embed.shape
    count = whiten0.shape[0]
    cells = depth * rows_sec * length
    flat = embed.reshape(cells, width)
    tissue_f = tissue.astype(jnp.float32)
    grid = (count, depth, rows_sec, length)
    start_full = whiten0.astype(jnp.float32)
    logdet0 = jnp.sum(jnp.log(jnp.diagonal(start_full, axis1=1, axis2=2)), axis=1)
    shift0, offset0 = offsets(start_full, means0, logdet0, weights0)
    resp = mean_field(likelihood(flat, whiten0, shift0, offset0).reshape(grid), tissue_f)
    flat_resp = resp.reshape(count, cells)

    def moments(block):
        weighted = (block[:, :, None] * flat[None].astype(jnp.float32)).astype(jnp.bfloat16)
        second_part = jnp.einsum("knd,ne->kde", weighted, flat, preferred_element_type=jnp.float32)
        return (second_part, jnp.sum(weighted.astype(jnp.float32), axis=1))

    second, first_moment = lax.map(
        moments, flat_resp.reshape(count // GROUP_SIZE, GROUP_SIZE, cells)
    )
    second = second.reshape(count, width, width)
    first_moment = first_moment.reshape(count, width)
    counts = jnp.sum(flat_resp, axis=1)
    counts_all, first_all = lax.psum((counts, first_moment), ("slab", "tile"))
    centre = first_all / counts_all[:, None]
    owned = lax.psum_scatter(second, "tile", scatter_dimension=0, tiled=True)
    owned = lax.psum(owned, "slab")
    whiten_own, logdet_own = owned_factor(
        owned, first_all, counts_all, lax.axis_index("tile") * owned.shape[0]
    )
    whiten, logdet = (
        lax.all_gather(whiten_own, "tile", axis=0, tiled=True),
        lax.all_gather(logdet_own, "tile", axis=0, tiled=True),
    )
    shift, offset = offsets(whiten, centre, logdet, counts_all)
    scores = likelihood(flat, whiten.astype(jnp.bfloat16), shift, offset)
    top = jnp.max(scores, axis=0)
    lse = top + jnp.log(jnp.sum(jnp.exp(scores - top[None]), axis=0))
    local_total = jnp.sum(lse * tissue_f.reshape(cells))
    score = lax.psum(local_total, ("slab", "tile")) / (
        cells * lax.axis_size("slab") * lax.axis_size("tile")
    )
    resp_final = mean_field(scores.reshape(grid), tissue_f)
    share = count // lax.axis_size("tile")
    means_out = lax.dynamic_slice_in_dim(centre, lax.axis_index("tile") * share, share, 0)
    return (resp_final, means_out, score)


def solution(mesh):
    in_specs = (P("slab", "tile", None, None), P("slab", "tile", None), P(), P(), P())
    out_specs = (P(None, "slab", "tile", None), P("tile", None), P())
    return jax.shard_map(shards, mesh=mesh, in_specs=in_specs, out_specs=out_specs, check_vma=False)
```

profile of v0, /device:TPU:1, one launch (start us, length us, event | category | flops | bytes accessed | tf_op | source)
XLA Modules:
  0.0 653.3 jit_solution(15050608254763178415)
XLA Ops:
  7.3 6.7 %copy.29 = f32[64,128,128]{0,2,1:T(8,128)} copy(bf16[64,128,128]{2,1,0:T(8,128)(2,1)} %param.13) | data formatting | bytes 6291456 | tf_op jit(solution)/shard_map/convert_element_type | solution.py:107
  14.0 3.3 fusion.68
  17.3 3.0 while.32
  18.1 0.3 fusion.84
  20.4 1.8 gather_fusion
  22.2 0.6 reduce_sum.139
  22.8 0.7 log_add_fusion.1
  23.9 1.3 collective-permute-start
  25.2 7.2 %collective-permute-start.1 = (f32[64,1,2,128]{3,2,1,0:T(2,128)S(1)}, f32[64,1,2,128]{3,2,1,0:T(2,128)S(1)}, u32[]{:S(2)}, u32[]{:S(2)}) collective-permute-start(f32[64,1,2,128]{3,2,1,0:T(2,128)S(1)} %divide_multiply_fusion.5), channel_id=1, source_target_pairs={{0,32},{32,64},{64,96},{96,128},{128,160},{160,192},{192,224},{224... | collective-permute-start | bytes 196616 | tf_op jit(solution)/shard_map/ppermute | solution.py:22
  32.5 1.3 collective-permute-done.1
  34.0 7.6 %collective-permute-start.2 = (f32[64,3,1,128]{3,2,1,0:T(1,128)S(1)}, f32[64,3,1,128]{3,2,1,0:T(1,128)S(1)}, u32[]{:S(2)}, u32[]{:S(2)}) collective-permute-start(f32[64,3,1,128]{3,2,1,0:T(1,128)S(1)} %get-tuple-element.170), channel_id=1, source_target_pairs={{1,0},{2,1},{3,2},{4,3},{5,4},{6,5},{7,6},{8,7},{9,8},{10,9},{11,1... | collective-permute-start | bytes 294920 | tf_op jit(solution)/shard_map/ppermute | solution.py:24
  41.6 1.9 collective-permute-start.3
  43.7 1.5 collective-permute-done.3
  45.5 1.3 collective-permute-start.4
  46.8 5.5 collective-permute-start.5
  52.5 1.2 collective-permute-done.4
  54.2 2.6 collective-permute-start.6
  56.8 4.2 collective-permute-start.7
  61.4 1.3 collective-permute-done.7
  63.0 0.6 fusion.55
  63.6 11.7 %while.33 = (s32[]{:T(128)}, f32[8,8,128,128]{2,3,1,0:T(8,128)}, f32[8,8,128]{2,1,0:T(8,128)S(1)}, f32[8,8,256]{2,1,0:T(8,128)S(1)}, bf16[1,2,128,128]{2,1,3,0:T...) while((s32[]{:T(128)}, f32[8,8,128,128]{2,3,1,0:T(8,128)}, f32[8,8,128]{2,1,0:T(8,128)S(1)}, ...), condition=%wide.region_16.17_spmd, body=%wide.region_14.16_spmd.sunk | while | flops 68713472 | bytes 1356373 | solution.py:118
  63.7 1.1 fusion.86
  65.1 1.1 fusion.86
  66.6 1.1 fusion.86
  68.1 1.1 fusion.86
  69.5 1.1 fusion.86
  71.0 1.1 fusion.86
  72.5 1.1 fusion.86
  73.9 1.1 fusion.86
  75.4 112.4 %all-reduce.9 = (f32[64,128]{1,0:T(8,128)S(1)}, f32[64]{0:T(128)S(1)}) all-reduce(f32[64,128]{1,0:T(8,128)S(1)} %bitcast.134, f32[64]{0:T(128)S(1)} %get-tuple-element.158), channel_id=1, replica_groups=mesh['slab'=16,'tile'=32] {'slab','tile'}, use_global_device_ids=true, to_apply=%region_19.20 | all-reduce | flops 8256 | bytes 66048 | tf_op jit(solution)/shard_map/psum | solution.py:124
  188.0 20.1 %reduce-scatter.2.cloned.1.call-done = f32[2,128,128]{1,2,0:T(8,128)} async-done(((f32[64,128,128]{1,2,0:T(8,128)}), f32[2,128,128]{1,2,0:T(8,128)}) %reduce-scatter.2.cloned.1.call-update) | async-done | bytes 131088 | tf_op jit(solution)/shard_map/reduce_scatter | solution.py:126
  208.4 161.7 %all-reduce.12.cloned.1.call-done = f32[2,128,128]{1,2,0:T(8,128)} async-done(((f32[2,128,128]{1,2,0:T(8,128)}), f32[2,128,128]{1,2,0:T(8,128)}) %all-reduce.12.cloned.1.call-update) | async-done | bytes 131088 | tf_op jit(solution)/shard_map/psum | solution.py:127
  370.1 1.0 copy.32
  371.1 1.0 fusion.22
  372.2 23.5 %custom-call.8 = f32[2,128,128]{2,1,0:T(8,128)S(1)} custom-call(f32[2,128,128]{2,1,0:T(8,128)S(1)} %fusion.18), custom_call_target="Cholesky" | custom-call | tf_op jit(solution)/shard_map/jit(cholesky)/cholesky | solution.py:78
  395.9 19.7 %custom-call.9 = f32[2,1,128,128]{2,3,1,0:T(8,128)S(1)} custom-call(f32[2,1,128,128]{3,2,1,0:T(8,128)S(1)} %get-tuple-element.156), custom_call_target="InvertDiagBlocksLowerTriangular" | custom-call | tf_op jit(solution)/shard_map/vmap(jit(_solve_triangular))/triangular_solve | solution.py:81
  415.6 1.0 fusion.16
  416.7 1.3 dynamic-slice
  418.6 0.6 reduce_sum.145
  419.3 4.6 copy.34
  423.9 1.8 gather_fusion.1
  425.9 63.8 %all-reduce.8 = f32[64]{0:T(128)S(1)} all-reduce(f32[64]{0:T(128)S(1)} %negate_dynamic-update-slice_fusion), channel_id=1, replica_groups=mesh['slab'=16,'tile'=32] {'tile'}, use_global_device_ids=true, to_apply=%add.8 | all-reduce | flops 64 | bytes 512
  489.7 0.7 log_add_fusion
  490.4 3.8 all-gather.2.cloned.1.call-done
  494.3 2.7 convert_element_type.42
  497.0 0.7 copy-done.1
  497.7 6.6 %fusion.69 = f32[64,1,128]{2,1,0:T(1,128)S(1)} fusion(f32[64,128,128]{2,1,0:T(8,128)S(1)} %copy-done.1, f32[64,128,1]{1,2,0:T(1,128)S(1)} %bitcast.131), kind=kOutput, calls=%fused_computation.142 | convolution fusion | flops 12582912 | bytes 4259840 | tf_op jit(solution)/shard_map/kde,ke->kd/dot_general | solution.py:89
  504.3 3.0 while.34
  506.6 0.3 fusion.89
  507.7 1.3 collective-permute-start.8
  509.0 5.1 collective-permute-start.9
  514.2 1.6 collective-permute-done.8
  516.1 2.6 collective-permute-start.10
  518.8 2.9 collective-permute-start.11
  521.7 0.6 fusion.50
  522.3 1.0 collective-permute-done.11
  523.7 1.3 collective-permute-start.12
  525.0 6.5 collective-permute-start.13
  531.5 0.6 constant_dynamic-slice_fusion
  532.0 104.5 %psum.31 = f32[]{:T(128)} all-reduce(f32[]{:T(128)} %fusion.50), channel_id=1, replica_groups=mesh['slab'=16,'tile'=32] {'slab','tile'}, use_global_device_ids=true, to_apply=%region_33.34 | all-reduce | flops 1 | bytes 8 | tf_op jit(solution)/shard_map/psum | solution.py:140
  637.5 2.6 collective-permute-start.14
  640.0 3.0 collective-permute-start.15
  643.4 1.3 collective-permute-done.15
  645.0 0.7 divide_multiply_fusion
  (168 shorter events, 12.9 us)
Async XLA Ops:
  7.2 6.8 %copy-start = (f32[64,128]{1,0:T(8,128)S(1)}, f32[64,128]{1,0:T(8,128)}, u32[]{:S(2)}) copy-start(f32[64,128]{1,0:T(8,128)} %param.14) | copy-start | bytes 98308
  7.2 200.9 %reduce-scatter.2.cloned.1.call-start = ((), (), s32[]{:S(2)}) async-start(), calls=%async_computation.1 | async-start | bytes 4325376 | tf_op jit(solution)/shard_map/reduce_scatter | solution.py:126
  7.2 6.7 %copy-start.2 = (bf16[64,128,128]{2,1,0:T(8,128)(2,1)S(1)}, bf16[64,128,128]{2,1,0:T(8,128)(2,1)}, u32[]{:S(2)}) copy-start(bf16[64,128,128]{2,1,0:T(8,128)(2,1)} %param.13) | copy-start | bytes 6291460
  7.2 10.1 %copy-start.3 = (bf16[1,2,128,128]{3,2,1,0:T(8,128)(2,1)S(1)}, bf16[1,2,128,128]{3,2,1,0:T(8,128)(2,1)}, u32[]{:S(2)}) copy-start(bf16[1,2,128,128]{3,2,1,0:T(8,128)(2,1)} %param.11) | copy-start | bytes 196612
  13.9 8.2 %copy-start.5 = (f32[64]{0:T(128)S(1)}, f32[64]{0:T(128)}, u32[]{:S(2)}) copy-start(f32[64]{0:T(128)} %param.15) | copy-start | bytes 772
  13.9 9.8 %copy-start.4 = (s32[1,2,128]{2,1,0:T(2,128)S(1)}, s32[1,2,128]{2,1,0:T(2,128)}, u32[]{:S(2)}) copy-start(s32[1,2,128]{2,1,0:T(2,128)} %param.12) | copy-start | bytes 3076
  23.9 8.5 %collective-permute-start = (f32[64,1,2,128]{3,2,1,0:T(2,128)S(1)}, f32[64,1,2,128]{3,2,1,0:T(2,128)S(1)}, u32[]{:S(2)}, u32[]{:S(2)}) collective-permute-start(f32[64,1,2,128]{3,2,1,0:T(2,128)S(1)} %divide_multiply_fusion.5), channel_id=1, source_target_pairs={{32,0},{64,32},{96,64},{128,96},{160,128},{192,160},{224,192},{256... | collective-permute-start | bytes 196616 | tf_op jit(solution)/shard_map/ppermute | solution.py:24
  25.2 8.5 %collective-permute-start.1 = (f32[64,1,2,128]{3,2,1,0:T(2,128)S(1)}, f32[64,1,2,128]{3,2,1,0:T(2,128)S(1)}, u32[]{:S(2)}, u32[]{:S(2)}) collective-permute-start(f32[64,1,2,128]{3,2,1,0:T(2,128)S(1)} %divide_multiply_fusion.5), channel_id=1, source_target_pairs={{0,32},{32,64},{64,96},{96,128},{128,160},{160,192},{192,224},{224... | collective-permute-start | bytes 196616 | tf_op jit(solution)/shard_map/ppermute | solution.py:22
  34.0 9.7 %collective-permute-start.2 = (f32[64,3,1,128]{3,2,1,0:T(1,128)S(1)}, f32[64,3,1,128]{3,2,1,0:T(1,128)S(1)}, u32[]{:S(2)}, u32[]{:S(2)}) collective-permute-start(f32[64,3,1,128]{3,2,1,0:T(1,128)S(1)} %get-tuple-element.170), channel_id=1, source_target_pairs={{1,0},{2,1},{3,2},{4,3},{5,4},{6,5},{7,6},{8,7},{9,8},{10,9},{11,1... | collective-permute-start | bytes 294920 | tf_op jit(solution)/shard_map/ppermute | solution.py:24
  41.6 3.5 collective-permute-start.3
  45.5 8.2 %collective-permute-start.4 = (f32[64,1,2,128]{3,2,1,0:T(2,128)S(1)}, f32[64,1,2,128]{3,2,1,0:T(2,128)S(1)}, u32[]{:S(2)}, u32[]{:S(2)}) collective-permute-start(f32[64,1,2,128]{3,2,1,0:T(2,128)S(1)} %divide_multiply_fusion.4), channel_id=1, source_target_pairs={{32,0},{64,32},{96,64},{128,96},{160,128},{192,160},{224,192},{256... | collective-permute-start | bytes 196616 | tf_op jit(solution)/shard_map/ppermute | solution.py:24
  46.8 7.2 %collective-permute-start.5 = (f32[64,1,2,128]{3,2,1,0:T(2,128)S(1)}, f32[64,1,2,128]{3,2,1,0:T(2,128)S(1)}, u32[]{:S(2)}, u32[]{:S(2)}) collective-permute-start(f32[64,1,2,128]{3,2,1,0:T(2,128)S(1)} %divide_multiply_fusion.4), channel_id=1, source_target_pairs={{0,32},{32,64},{64,96},{96,128},{128,160},{160,192},{192,224},{224... | collective-permute-start | bytes 196616 | tf_op jit(solution)/shard_map/ppermute | solution.py:22
  54.2 7.1 %collective-permute-start.6 = (f32[64,3,1,128]{3,2,1,0:T(1,128)S(1)}, f32[64,3,1,128]{3,2,1,0:T(1,128)S(1)}, u32[]{:S(2)}, u32[]{:S(2)}) collective-permute-start(f32[64,3,1,128]{3,2,1,0:T(1,128)S(1)} %get-tuple-element.168), channel_id=1, source_target_pairs={{1,0},{2,1},{3,2},{4,3},{5,4},{6,5},{7,6},{8,7},{9,8},{10,9},{11,1... | collective-permute-start | bytes 294920 | tf_op jit(solution)/shard_map/ppermute | solution.py:24
  56.8 5.8 collective-permute-start.7
  75.3 294.8 %all-reduce.12.cloned.1.call-start = ((), (), s32[]{:S(2)}) async-start(), calls=%async_computation.2 | async-start | bytes 262144 | tf_op jit(solution)/shard_map/psum | solution.py:127
  208.1 286.2 %all-gather.2.cloned.1.call-start = ((), (), s32[]{:S(2)}) async-start(), calls=%async_computation.3 | async-start | bytes 4325376 | tf_op jit(solution)/shard_map/all_gather | solution.py:132
  494.3 3.4 copy-start.1
  507.7 8.2 %collective-permute-start.8 = (f32[64,1,2,128]{3,2,1,0:T(2,128)S(1)}, f32[64,1,2,128]{3,2,1,0:T(2,128)S(1)}, u32[]{:S(2)}, u32[]{:S(2)}) collective-permute-start(f32[64,1,2,128]{3,2,1,0:T(2,128)S(1)} %divide_multiply_fusion.2), channel_id=1, source_target_pairs={{32,0},{64,32},{96,64},{128,96},{160,128},{192,160},{224,192},{256... | collective-permute-start | bytes 196616 | tf_op jit(solution)/shard_map/ppermute | solution.py:24
  509.0 6.9 %collective-permute-start.9 = (f32[64,1,2,128]{3,2,1,0:T(2,128)S(1)}, f32[64,1,2,128]{3,2,1,0:T(2,128)S(1)}, u32[]{:S(2)}, u32[]{:S(2)}) collective-permute-start(f32[64,1,2,128]{3,2,1,0:T(2,128)S(1)} %divide_multiply_fusion.2), channel_id=1, source_target_pairs={{0,32},{32,64},{64,96},{96,128},{128,160},{160,192},{192,224},{224... | collective-permute-start | bytes 196616 | tf_op jit(solution)/shard_map/ppermute | solution.py:22
  516.1 6.2 collective-permute-start.10
  518.8 4.5 collective-permute-start.11
  523.7 113.5 %collective-permute-start.12 = (f32[64,1,2,128]{3,2,1,0:T(2,128)S(1)}, f32[64,1,2,128]{3,2,1,0:T(2,128)S(1)}, u32[]{:S(2)}, u32[]{:S(2)}) collective-permute-start(f32[64,1,2,128]{3,2,1,0:T(2,128)S(1)} %divide_multiply_fusion.1), channel_id=1, source_target_pairs={{32,0},{64,32},{96,64},{128,96},{160,128},{192,160},{224,192},{256... | collective-permute-start | bytes 196616 | tf_op jit(solution)/shard_map/ppermute | solution.py:24
  525.0 112.2 %collective-permute-start.13 = (f32[64,1,2,128]{3,2,1,0:T(2,128)S(1)}, f32[64,1,2,128]{3,2,1,0:T(2,128)S(1)}, u32[]{:S(2)}, u32[]{:S(2)}) collective-permute-start(f32[64,1,2,128]{3,2,1,0:T(2,128)S(1)} %divide_multiply_fusion.1), channel_id=1, source_target_pairs={{0,32},{32,64},{64,96},{96,128},{128,160},{160,192},{192,224},{224... | collective-permute-start | bytes 196616 | tf_op jit(solution)/shard_map/ppermute | solution.py:22
  637.5 5.9 collective-permute-start.14
  640.0 4.6 collective-permute-start.15
Sparse Core Ops, SparseCore 0:
  75.4 132.5 reduce-scatter.1
  211.0 159.0 all-reduce.11
  416.8 77.4 all-gather.1
where the time goes:
time: 655 us; the launch traced here: 653 us
  blocking collectives  281 us (43%)
  waiting for transfers between devices  196 us (30%)
  starting transfers between devices  57.2 us (9%)
  other arithmetic  56.3 us (9%)
  matrix products  25.1 us (4%)
  local copies, waits for them, and re-layouts  20.7 us (3%)
  between operations  16.7 us (3%)
    psum x1, waiting for transfers between devices, shards(): owned = lax.psum(owned, 'slab')  162 us
    psum x1, blocking collectives, shards(): counts_all, first_all = lax.psum((counts, first_moment), ('slab', 'tile'))  112 us
    psum x1, blocking collectives, shards(): lax.psum(local_total, ('slab', 'tile'))  104 us
    unnamed x1, blocking collectives  63.8 us
    ppermute x8, starting transfers between devices, extended(): lax.ppermute(tail, axis, [(i, (i + 1) % count) for i in range(ends)])  36.3 us
    another operation x4, other arithmetic, factor(): lower = jnp.linalg.cholesky(cov)  23.6 us
    ppermute x8, starting transfers between devices, extended(): lax.ppermute(head, axis, [((i + 1) % count, i) for i in range(ends)])  20.5 us
    reduce_scatter x1, waiting for transfers between devices, shards(): owned = lax.psum_scatter(second, 'tile', scatter_dimension=0, tiled=True)  20.1 us
  transfers between devices with their start and end apart: 19, of which 13 were waited for; matrix products, arithmetic and copies ran while one was open for 2% of the time, Pallas kernels for 0%

commit v1 on v0

v1 whole, which is shorter than its diff:
```python
import jax
import jax.numpy as jnp
from jax import lax
from jax.experimental import pallas as pl
from jax.experimental.pallas import tpu as pltpu
from jax.sharding import Mesh
from jax.sharding import PartitionSpec as P

SWEEPS = 2
BETA_POTTS = 1.0
COV_RIDGE = 0.01

SLAB = ("x1", "x0", "z2", "z1")
TILE = ("z0", "y2", "y1", "y0", "core")
BRICK = ("z0", "y0", "core")
PAIRS = ("x0", "y1")
ROWS = ("x1", "z2", "z1", "y2")

WIDTH = 128
CELLS = 256
PACKET = 144
HIGH = lax.Precision.HIGHEST
VMEM = pl.BlockSpec(memory_space=pltpu.VMEM)
PARAMS = pltpu.CompilerParams(vmem_limit_bytes=40 * 1024 * 1024)


def call(kernel, shapes, *args, flops=1 << 20):
    out = [jax.ShapeDtypeStruct(shape, kind) for shape, kind in shapes]
    return pl.pallas_call(
        kernel,
        out_shape=out,
        in_specs=[VMEM] * len(args),
        out_specs=[VMEM] * len(out),
        compiler_params=PARAMS,
        cost_estimate=pl.CostEstimate(flops=flops, bytes_accessed=1 << 20, transcendentals=0),
    )(*args)


def iotas(shape):
    return (
        lax.broadcasted_iota(jnp.int32, shape, 0),
        lax.broadcasted_iota(jnp.int32, shape, 1),
    )


def matmul(lhs, rhs, dims=((1,), (0,)), precision=None):
    return lax.dot_general(
        lhs, rhs, (dims, ((), ())), precision=precision, preferred_element_type=jnp.float32
    )


def normalise(scores):
    top = jnp.max(scores, axis=0, keepdims=True)
    expon = jnp.exp(scores - top)
    return expon / jnp.sum(expon, axis=0, keepdims=True)


def put(resp, resp_ref, first_ref, last_ref):
    resp_ref[...] = resp
    first_ref[...] = resp[:, :WIDTH]
    last_ref[...] = resp[:, WIDTH:]


def domain_at(place):
    bit = lambda n: (place >> n) & 1
    return bit(5) * 32 + bit(2) * 16 + bit(1) * 8 + bit(4) * 4 + bit(3) * 2 + bit(0)


def start_kernel(flat, tissue, whiten, means, weights, scores, resp, first, last, diag, weigh):
    turned = flat[...].astype(jnp.float32).T.astype(jnp.bfloat16)
    row_at, col_at = iotas((WIDTH, WIDTH))
    count = whiten.shape[0]

    def domain(place, carry):
        own = domain_at(place)
        matrix = whiten[own]
        full = matrix.astype(jnp.float32)
        shift = jnp.sum(full * means[pl.ds(own, 1), :], axis=1, keepdims=True)
        proj = matmul(matrix, turned) - shift
        scores[pl.ds(place, 1), :] = jnp.sum(proj * proj, axis=0, keepdims=True)
        diag[pl.ds(place, 1), :] = jnp.sum(
            jnp.where(row_at == col_at, full, 0.0), axis=0, keepdims=True
        )
        weigh[pl.ds(place, 1), :] = weights[pl.ds(own, 1), :]
        return carry

    lax.fori_loop(0, count, domain, 0, unroll=4)
    total = jnp.sum(weigh[...], axis=0, keepdims=True)
    offset = jnp.log(weigh[...] / total) + jnp.sum(jnp.log(diag[...]), axis=1, keepdims=True)
    result = offset[:, :1] - 0.5 * scores[...]
    scores[...] = result
    put(normalise(result) * tissue[...], resp, first, last)


def start(flat, tissue, whiten, means, weights):
    count = whiten.shape[0]
    f32 = jnp.float32
    return pl.pallas_call(
        start_kernel,
        out_shape=[
            jax.ShapeDtypeStruct((count, CELLS), f32),
            jax.ShapeDtypeStruct((count, CELLS), f32),
            jax.ShapeDtypeStruct((count, WIDTH), f32),
            jax.ShapeDtypeStruct((count, WIDTH), f32),
        ],
        in_specs=[VMEM] * 5,
        out_specs=[VMEM] * 4,
        scratch_shapes=[pltpu.VMEM((count, WIDTH), f32), pltpu.VMEM((count, WIDTH), f32)],
        compiler_params=PARAMS,
        cost_estimate=pl.CostEstimate(flops=1 << 29, bytes_accessed=1 << 21, transcendentals=0),
    )(flat, tissue, whiten, means, weights)


def sweep_kernel(scores, resp, ahead, behind, below, above, tissue, out, first, last):
    lane = iotas((resp.shape[0], WIDTH))[1]
    rows = (resp[:, :WIDTH], resp[:, WIDTH:])
    fields = []
    for row, others in zip(rows, (below[...] + rows[1], rows[0] + above[...])):
        after = jnp.where(lane < WIDTH - 1, pltpu.roll(row, WIDTH - 1, 1), 0.0)
        before = jnp.where(lane > 0, pltpu.roll(row, 1, 1), 0.0)
        fields.append(others + after + before)
    field = jnp.concatenate(fields, axis=1) + ahead[...] + behind[...]
    put(normalise(scores[...] + BETA_POTTS * field) * tissue[...], out, first, last)


def sweep(scores, resp, first, last, tissue):
    def moved(part, axes, step):
        count = lax.axis_size(axes)
        pairs = [(i, i + step) for i in range(count) if 0 <= i + step < count]
        return lax.ppermute(part, axes, pairs)

    f32 = jnp.float32
    below = moved(last, TILE, 1)
    above = moved(first, TILE, -1)
    behind = moved(resp, SLAB, 1)
    ahead = moved(resp, SLAB, -1)
    count = resp.shape[0]
    return call(
        sweep_kernel,
        [((count, CELLS), f32), ((count, WIDTH), f32), ((count, WIDTH), f32)],
        scores, resp, ahead, behind, below, above, tissue,
    )


def moments_kernel(resp, shared, packet, turned, total):
    blocks, count = resp.shape[:2]
    row_at, col_at = iotas((WIDTH, WIDTH))
    ones = jnp.ones((CELLS, WIDTH), jnp.bfloat16)
    acc = [jnp.zeros((WIDTH, 2 * WIDTH), jnp.float32) for _ in range(count)]
    for block in range(blocks):
        cells = shared[block * CELLS : (block + 1) * CELLS, :]
        flipped = cells.T
        turned[block] = flipped.astype(jnp.bfloat16)
        wide = jnp.concatenate([cells.astype(jnp.bfloat16), ones], axis=1)
        for k in range(count):
            weighted = (flipped * resp[block, k : k + 1, :]).astype(jnp.bfloat16)
            acc[k] = acc[k] + matmul(weighted, wide)
    firsts = jnp.zeros((WIDTH, WIDTH), jnp.float32)
    for k in range(count):
        firsts = jnp.where(col_at == k, acc[k][:, WIDTH:], firsts)
    firsts = firsts.T
    counts = jnp.sum(jnp.sum(resp[...], axis=0), axis=1, keepdims=True)
    counts = jnp.broadcast_to(counts, (count, WIDTH))
    total[...] = jnp.sum(counts, axis=0, keepdims=True)
    for pair in range(count // 2):
        a, b = acc[2 * pair][:, :WIDTH], acc[2 * pair + 1][:, :WIDTH]
        crossed = jnp.where(row_at > col_at, b, a).T
        packet[pair, :WIDTH] = jnp.where(row_at >= col_at, a, b) + crossed
        diag = jnp.sum(jnp.where(row_at == col_at, b, 0.0), axis=0, keepdims=True)
        packet[pair, WIDTH:] = jnp.concatenate(
            [
                2.0 * diag,
                firsts[2 * pair : 2 * pair + 2],
                counts[2 * pair : 2 * pair + 2],
                jnp.zeros((PACKET - WIDTH - 5, WIDTH), jnp.float32),
            ],
            axis=0,
        )


STEP = 8


def whiten_chain(cov):
    row_at, col_at = iotas((WIDTH, WIDTH))
    wide = (STEP, 2 * WIDTH)
    rest = jnp.concatenate([cov, jnp.where(row_at == col_at, 1.0, 0.0)], axis=1)
    sub = lax.broadcasted_iota(jnp.int32, (STEP, WIDTH), 0)
    done, scales = [], []
    for begin in range(0, WIDTH, STEP):
        panel = rest[:STEP]
        cols = [
            jnp.broadcast_to(panel[:, begin + j : begin + j + 1], (STEP, WIDTH))
            for j in range(STEP)
        ]
        scale = jnp.broadcast_to(cols[0][:1], (STEP, WIDTH))
        for j in range(STEP - 1):
            pivot = jnp.broadcast_to(cols[j][j : j + 1], (STEP, WIDTH))
            mult = jnp.where(sub > j, cols[j] / pivot, 0.0)
            both = jnp.concatenate([mult, mult], axis=1)
            panel = panel - both * jnp.broadcast_to(panel[j : j + 1], wide)
            for l in range(j + 1, STEP):
                cols[l] = cols[l] - mult * jnp.broadcast_to(cols[l][j : j + 1], (STEP, WIDTH))
            scale = jnp.where(sub > j, jnp.broadcast_to(cols[j + 1][j + 1 : j + 2], (STEP, WIDTH)), scale)
        root = lax.rsqrt(scale)
        panel = panel * jnp.concatenate([root, root], axis=1)
        scales.append(scale)
        done.append(panel[:, WIDTH:])
        if begin + STEP < WIDTH:
            below = panel[:, :WIDTH]
            rest = rest[STEP:] - matmul(below, panel, ((0,), (0,)), HIGH)[begin + STEP :]
    logdet = -0.5 * jnp.sum(jnp.log(jnp.concatenate(scales, axis=0)), axis=0, keepdims=True)
    return jnp.concatenate(done, axis=0), logdet


def factor_kernel(packet, out):
    row_at, col_at = iotas((WIDTH, WIDTH))
    square = packet[:WIDTH]
    turned = square.T
    diag = packet[WIDTH : WIDTH + 1]
    syms = (
        jnp.where(row_at >= col_at, square, turned),
        jnp.where(row_at < col_at, square, jnp.where(row_at == col_at, diag, turned)),
    )
    extras = [jnp.zeros((1, WIDTH), jnp.float32)] * 8
    whitens = []
    for which, sym in enumerate(syms):
        counts = packet[WIDTH + 3 + which : WIDTH + 4 + which]
        centre = packet[WIDTH + 1 + which : WIDTH + 2 + which] / counts
        tall = jnp.broadcast_to(centre, (WIDTH, WIDTH))
        cov = 0.5 * sym / counts - tall.T * tall
        cov = jnp.where(row_at == col_at, cov + COV_RIDGE, cov)
        whiten, logdet = whiten_chain(cov)
        whitens.append(whiten)
        shift = jnp.sum(whiten * tall, axis=1, keepdims=True)
        extras[1 + which] = jnp.broadcast_to(shift, (WIDTH, WIDTH)).T[:1]
        extras[3 + which] = centre
        extras[5 + which] = jnp.log(counts) + logdet
    extras[0] = jnp.sum(jnp.where(row_at == col_at, whitens[1], 0.0), axis=0, keepdims=True)
    out[:WIDTH] = jnp.where(row_at >= col_at, whitens[0], whitens[1].T)
    out[WIDTH:] = jnp.concatenate(extras, axis=0)


def second_kernel(packets, turned, scores):
    row_at, col_at = iotas((WIDTH, WIDTH))
    blocks = turned.shape[0]
    for pair in range(packets.shape[0]):
        square = packets[pair, :WIDTH]
        extras = packets[pair, WIDTH:]
        upper = jnp.where(row_at < col_at, square, 0.0)
        upper = jnp.where(row_at == col_at, extras[:1], upper)
        whitens = (jnp.where(row_at >= col_at, square, 0.0), upper.T)
        for which, whiten in enumerate(whitens):
            half = whiten.astype(jnp.bfloat16)
            shift = jnp.broadcast_to(extras[1 + which : 2 + which], (WIDTH, WIDTH)).T
            shift = jnp.concatenate([shift, shift], axis=1)
            offset = extras[5 + which : 6 + which]
            offset = jnp.concatenate([offset, offset], axis=1)
            for block in range(blocks):
                proj = matmul(half, turned[block]) - shift
                quad = jnp.sum(proj * proj, axis=0, keepdims=True)
                k = 2 * pair + which
                scores[block, k : k + 1, :] = offset - 0.5 * quad


def likely_kernel(scores, tissue, total, resp, first, last, totals):
    values = scores[...]
    top = jnp.max(values, axis=0, keepdims=True)
    expon = jnp.exp(values - top)
    weight = jnp.sum(expon, axis=0, keepdims=True)
    put(expon / weight * tissue[...], resp, first, last)
    lse = jnp.sum((top + jnp.log(weight)) * tissue[...], axis=1, keepdims=True)
    cover = jnp.sum(tissue[...], axis=1, keepdims=True)
    lane = iotas((1, WIDTH))[1]
    totals[...] = jnp.where(lane == 0, lse, jnp.where(lane == 1, cover, total[...]))


def to_all(value, axes):
    count = lax.axis_size(axes)
    spread = jnp.broadcast_to(value[None], (count, *value.shape))
    return lax.all_to_all(spread, axes, 0, 0, tiled=True)


def shards(embed, tissue, whiten0, means0, weights0):
    count = whiten0.shape[0]
    f32 = jnp.float32
    flat = embed.reshape(CELLS, WIDTH)
    tissue_f = tissue.astype(f32).reshape(1, CELLS)

    shared = lax.all_gather(flat.astype(f32), BRICK, axis=0, tiled=True)
    shared = lax.optimization_barrier(shared)

    spread = jnp.broadcast_to(weights0[:, None], (count, WIDTH))
    scores, resp, first, last = start(flat, tissue_f, whiten0, means0, spread)
    for _ in range(SWEEPS):
        resp, first, last = sweep(scores, resp, first, last, tissue_f)

    part = lax.all_to_all(resp.reshape(8, 8, CELLS), BRICK, 0, 0, tiled=True)
    packet, turned, total = call(
        moments_kernel,
        [((4, PACKET, WIDTH), f32), ((8, WIDTH, CELLS), jnp.bfloat16), ((1, WIDTH), f32)],
        part, shared, flops=1 << 30,
    )
    packet = packet.reshape(64, 1, PACKET * WIDTH // 16)
    packet = lax.all_to_all(packet, PAIRS + ROWS, 0, 0, tiled=True)
    packet = to_all(jnp.sum(packet, axis=0), ROWS).reshape(PACKET, WIDTH)

    (own,) = call(factor_kernel, [((WIDTH + 8, WIDTH), f32)], packet, flops=1 << 27)
    packets = to_all(own, PAIRS)
    (part,) = call(second_kernel, [((8, 8, CELLS), f32)], packets, turned, flops=1 << 29)
    scores = lax.all_to_all(part, BRICK, 0, 0, tiled=True).reshape(count, CELLS)

    resp, first, last, totals = call(
        likely_kernel,
        [((count, CELLS), f32), ((count, WIDTH), f32), ((count, WIDTH), f32), ((1, WIDTH), f32)],
        scores, tissue_f, total,
    )
    totals = jnp.sum(to_all(totals, SLAB), axis=0)
    totals = jnp.sum(to_all(totals, TILE), axis=0)
    bins = CELLS * lax.axis_size(SLAB + TILE)
    score = (totals[0, 0] - totals[0, 1] * jnp.log(totals[0, 2])) / bins
    for _ in range(SWEEPS):
        resp, first, last = sweep(scores, resp, first, last, tissue_f)

    resp_final = resp.reshape(2, 2, 2, 2, 2, 2, 1, 2, WIDTH).transpose(0, 3, 4, 1, 2, 5, 6, 7, 8)
    means = packets[:, WIDTH + 3 : WIDTH + 5]
    place = lax.axis_index(("y2", "y1"))
    means_out = lax.dynamic_index_in_dim(means, place, 0, keepdims=False)
    return (resp_final.reshape(count, 1, 2, WIDTH), means_out, score)


def solution(mesh):
    bits = Mesh(mesh.devices.reshape((2,) * 9), SLAB + TILE)
    in_specs = (P(SLAB, TILE, None, None), P(SLAB, TILE, None), P(), P(), P())
    out_specs = (P(None, SLAB, TILE, None), P(TILE, None), P())
    return jax.shard_map(shards, mesh=bits, in_specs=in_specs, out_specs=out_specs, check_vma=False)
```

time: 655 us -> 216 us (0.33)
  blocking collectives: 281 us -> 72.9 us
  waiting for transfers between devices: 196 us -> 16.3 us
  other arithmetic: 56.3 us -> 2.42 us
  Pallas kernels: 0 us -> 25.9 us
  matrix products: 25.1 us -> 0 us
  local copies, waits for them, and re-layouts: 20.7 us -> 8.36 us
  starting transfers between devices: 57.2 us -> 69 us
    psum x2 -> x0, blocking collectives: 217 us -> none  [the longest x1 112 us: shards(): counts_all, first_all = lax.psum((counts, first_moment), ('slab', 'tile'))]
    psum x1 -> x0, waiting for transfers between devices: 162 us -> none  [shards(): owned = lax.psum(owned, 'slab')]
    all_to_all x0 -> x4, blocking collectives: none -> 72.9 us  [the longest x1 33.4 us: shards(): packet = lax.all_to_all(packet, PAIRS + ROWS, 0, 0, tiled=True)]
    unnamed x1 -> x0, blocking collectives: 63.8 us -> none
    another operation x6 -> x0, other arithmetic: 43.4 us -> none  [the longest x4 23.6 us: factor(): lower = jnp.linalg.cholesky(cov)]
    pallas_call x0 -> x9, Pallas kernels: none -> 25.9 us  [the longest x8 21.8 us: call(): pl.pallas_call(kernel, out_shape=out, in_specs=[VMEM] * len(args), out_sp...]
    dot_general x26 -> x0, matrix products: 24.1 us -> none  [the longest x2 9.91 us: offsets(): jnp.einsum('kde,ke->kd', whiten_full, centre, precision=lax.Precision.HIG...]
    reduce_scatter x1 -> x0, waiting for transfers between devices: 20.1 us -> none  [shards(): owned = lax.psum_scatter(second, 'tile', scatter_dimension=0, tiled=True)]
  transfers between devices with their start and end apart: 19 -> 20, of which waited for: 13 -> 5; matrix products, arithmetic and copies ran while one was open for 2% -> 2% of each run, Pallas kernels for 0% -> 2%
where the time goes in v1:
time: 216 us; the launch traced here: 212 us
  blocking collectives  72.9 us (34%)
  starting transfers between devices  69 us (32%)
  Pallas kernels  25.9 us (12%)
  between operations  17.5 us (8%)
  waiting for transfers between devices  16.3 us (8%)
  local copies, waits for them, and re-layouts  8.36 us (4%)
  other arithmetic  2.42 us (1%)
    ppermute x16, starting transfers between devices, moved(): return lax.ppermute(part, axes, pairs)  54.7 us
    all_to_all x1, blocking collectives, shards(): packet = lax.all_to_all(packet, PAIRS + ROWS, 0, 0, tiled=True)  33.4 us
    all_to_all x2, blocking collectives, to_all(): return lax.all_to_all(spread, axes, 0, 0, tiled=True)  29.4 us
    pallas_call x8, Pallas kernels, call(): pl.pallas_call(kernel, out_shape=out, in_specs=[VMEM] * len(args), out_sp...  21.8 us
    all_to_all x1, blocking collectives, shards(): scores = lax.all_to_all(part, BRICK, 0, 0, tiled=True).reshape(count, CELLS)  10.2 us
    all_to_all x2, starting transfers between devices, to_all(): return lax.all_to_all(spread, axes, 0, 0, tiled=True)  9.13 us
    all_to_all x2, waiting for transfers between devices, to_all(): return lax.all_to_all(spread, axes, 0, 0, tiled=True)  7.2 us
    all_to_all x1, starting transfers between devices, shards(): part = lax.all_to_all(resp.reshape(8, 8, CELLS), BRICK, 0, 0, tiled=True)  5.19 us
  transfers between devices with their start and end apart: 20, of which 5 were waited for; matrix products, arithmetic and copies ran while one was open for 2% of the time, Pallas kernels for 2%

profile of v1, /device:TPU:1, one launch (start us, length us, event | category | flops | bytes accessed | tf_op | source)
XLA Modules:
  0.0 212.4 jit_solution(4646174692898342309)
XLA Ops:
  7.2 0.0 all-gather.2.cloned.1.call-start
  7.2 1.5 bitcast_convert_fusion
  8.7 0.0 all-gather.2.cloned.1.call-update
  8.7 0.7 convert_element_type.6
  9.4 0.7 broadcast_in_dim.12.weights
  10.1 1.6 copy-done
  11.7 0.8 copy-done.1
  12.6 0.8 copy-done.2
  13.3 4.1 %shard_map.76 = (f32[64,256]{1,0:T(8,128)S(1)}, f32[64,256]{1,0:T(8,128)S(1)}, f32[64,128]{1,0:T(8,128)S(1)}, f32[64,128]{1,0:T(8,128)S(1)}) custom-call(bf16[256,128]{1,0:T(8,128)(2,1)S(1)} %bitcast.20, f32[1,256]{1,0:T(1,128)S(1)} %bitcast.22, bf16[64,128,128]{2,1,0:T(8,128)(2,1)S(1)} %copy-done, f32[64,128]{1,0:T(8,128)S(1)} %copy-done.2, ...), custom_call_target="tpu_custom_call" | custom-call | flops 536870912 | bytes 2097152 | tf_op jit(solution)/shard_map/pallas_call | solution.py:98
  17.5 1.3 collective-permute-start
  18.8 7.3 %collective-permute-start.1 = (f32[64,256]{1,0:T(8,128)S(1)}, f32[64,256]{1,0:T(8,128)S(1)}, u32[]{:S(2)}, u32[]{:S(2)}) collective-permute-start(f32[64,256]{1,0:T(8,128)S(1)} %get-tuple-element.23.resp), channel_id=1, source_target_pairs={{0,32},{32,64},{64,96},{96,128},{128,160},{160,192},{192,224},{224... | collective-permute-start | bytes 196616 | tf_op jit(solution)/shard_map/ppermute | solution.py:130
  26.0 4.0 %collective-permute-start.2 = (f32[64,128]{1,0:T(8,128)S(1)}, f32[64,128]{1,0:T(8,128)S(1)}, u32[]{:S(2)}, u32[]{:S(2)}) collective-permute-start(f32[64,128]{1,0:T(8,128)S(1)} %get-tuple-element.24), channel_id=1, source_target_pairs={{0,1},{1,2},{2,3},{3,4},{4,5},{5,6},{6,7},{7,8},{8,9},{9,10},{10,1... | collective-permute-start | bytes 98312 | tf_op jit(solution)/shard_map/ppermute | solution.py:130
  30.1 4.2 %collective-permute-start.3 = (f32[64,128]{1,0:T(8,128)S(1)}, f32[64,128]{1,0:T(8,128)S(1)}, u32[]{:S(2)}, u32[]{:S(2)}) collective-permute-start(f32[64,128]{1,0:T(8,128)S(1)} %get-tuple-element.25), channel_id=1, source_target_pairs={{1,0},{2,1},{3,2},{4,3},{5,4},{6,5},{7,6},{8,7},{9,8},{10,9},{11,1... | collective-permute-start | bytes 98312 | tf_op jit(solution)/shard_map/ppermute | solution.py:130
  34.3 0.0 collective-permute-done.2.below
  34.3 1.4 collective-permute-done.3.above
  35.8 0.0 collective-permute-done.ahead
  35.8 0.0 collective-permute-done.1.behind
  35.8 0.1 shard_map.77
  35.9 1.3 collective-permute-start.4
  37.2 8.1 %collective-permute-start.5 = (f32[64,256]{1,0:T(8,128)S(1)}, f32[64,256]{1,0:T(8,128)S(1)}, u32[]{:S(2)}, u32[]{:S(2)}) collective-permute-start(f32[64,256]{1,0:T(8,128)S(1)} %get-tuple-element.26.resp), channel_id=1, source_target_pairs={{0,32},{32,64},{64,96},{96,128},{128,160},{160,192},{192,224},{224... | collective-permute-start | bytes 196616 | tf_op jit(solution)/shard_map/ppermute | solution.py:130
  45.3 1.9 collective-permute-start.6
  47.2 2.4 %collective-permute-start.7 = (f32[64,128]{1,0:T(8,128)S(1)}, f32[64,128]{1,0:T(8,128)S(1)}, u32[]{:S(2)}, u32[]{:S(2)}) collective-permute-start(f32[64,128]{1,0:T(8,128)S(1)} %get-tuple-element.28), channel_id=1, source_target_pairs={{1,0},{2,1},{3,2},{4,3},{5,4},{6,5},{7,6},{8,7},{9,8},{10,9},{11,1... | collective-permute-start | bytes 98312 | tf_op jit(solution)/shard_map/ppermute | solution.py:130
  49.6 0.0 collective-permute-done.6.below
  49.7 2.8 %collective-permute-done.7.above = f32[64,128]{1,0:T(8,128)S(1)} collective-permute-done((f32[64,128]{1,0:T(8,128)S(1)}, f32[64,128]{1,0:T(8,128)S(1)}, u32[]{:S(2)}, u32[]{:S(2)}) %collective-permute-start.7) | collective-permute-done | bytes 32800 | tf_op jit(solution)/shard_map/ppermute | solution.py:130
  52.5 0.0 collective-permute-done.4.ahead
  52.5 0.0 collective-permute-done.5.behind
  52.5 0.8 shard_map.78
  53.3 5.2 %all-to-all-start = ((f32[8,8,256]{2,1,0:T(8,128)}), f32[8,8,256]{2,1,0:T(8,128)S(1)}, u32[]{:S(2)}, u32[]{:S(2)}) async-start(f32[8,8,256]{2,1,0:T(8,128)} %bitcast.2), calls=%async_computation | async-start | bytes 131072 | tf_op jit(solution)/shard_map/all_to_all | solution.py:298
  58.5 4.2 %all-to-all-done.resp = f32[8,8,256]{2,1,0:T(8,128)S(1)} async-done(((f32[8,8,256]{2,1,0:T(8,128)}), f32[8,8,256]{2,1,0:T(8,128)S(1)}, u32[]{:S(2)}, u32[]{:S(2)}) %all-to-all-start) | async-done | bytes 65568 | tf_op jit(solution)/shard_map/all_to_all | solution.py:298
  62.6 1.2 copy-done.3
  63.8 1.4 shard_map.79
  65.2 33.4 %all_to_all.35 = f32[64,1,1152]{2,1,0:T(1,128)S(1)} all-to-all(f32[64,1,1152]{2,1,0:T(1,128)S(1)} %bitcast.19), channel_id=1, replica_groups=mesh['x1'=2,'x0'=2,'z2'=2,'z1'=2,'z0'=2,'y2'=2,'y1'=2,'y0'=2,'core'=2] {..., dimensions={0} | all-to-all | bytes 589824 | tf_op jit(solution)/shard_map/all_to_all | solution.py:305
  98.6 0.2 reduce_sum.29
  98.8 19.0 %all_to_all.36 = f32[16,1,1152]{2,1,0:T(1,128)S(1)} all-to-all(f32[16,1,1152]{2,1,0:T(1,128)S(1)} %broadcast_in_dim.13), channel_id=1, replica_groups=mesh['x1'=2,'x0'=2,'z2'=2,'z1'=2,'z0'=2,'y2'=2,'y1'=2,'y0'=2,'core'=2] {..., dimensions={0} | all-to-all | bytes 147456 | tf_op jit(solution)/shard_map/all_to_all | solution.py:281
  117.9 17.1 %shard_map.80 = f32[136,128]{1,0:T(8,128)S(1)} custom-call(f32[144,128]{1,0:T(8,128)S(1)} %bitcast.21), custom_call_target="tpu_custom_call" | custom-call | flops 134217728 | bytes 1048576 | tf_op jit(solution)/shard_map/pallas_call | solution.py:29
  135.1 10.3 %all_to_all.37.packets = f32[4,136,128]{2,1,0:T(8,128)S(1)} all-to-all(f32[4,136,128]{2,1,0:T(8,128)S(1)} %broadcast_in_dim.14), channel_id=1, replica_groups=mesh['x1'=2,'x0'=2,'z2'=2,'z1'=2,'z0'=2,'y2'=2,'y1'=2,'y0'=2,'core'=2] {..., dimensions={0} | all-to-all | bytes 557056 | tf_op jit(solution)/shard_map/all_to_all | solution.py:281
  145.4 1.3 shard_map.81
  146.7 10.2 %all_to_all.38 = f32[8,8,256]{2,1,0:T(8,128)S(1)} all-to-all(f32[8,8,256]{2,1,0:T(8,128)S(1)} %shard_map.81), channel_id=1, replica_groups=mesh['x1'=2,'x0'=2,'z2'=2,'z1'=2,'z0'=2,'y2'=2,'y1'=2,'y0'=2,'core'=2] {..., dimensions={0} | all-to-all | bytes 131072 | tf_op jit(solution)/shard_map/all_to_all | solution.py:311
  156.9 0.1 shard_map.82
  157.0 0.6 broadcast_in_dim.16
  157.6 3.5 %all-to-all-start.5 = ((f32[16,1,128]{2,1,0:T(1,128)}), f32[16,1,128]{2,1,0:T(1,128)S(1)}, u32[]{:S(2)}, u32[]{:S(2)}) async-start(f32[16,1,128]{2,1,0:T(1,128)} %broadcast_in_dim.16), calls=%async_computation.5 | async-start | bytes 16384 | tf_op jit(solution)/shard_map/all_to_all | solution.py:281
  161.1 1.3 collective-permute-start.8
  162.4 4.9 %collective-permute-start.9 = (f32[64,256]{1,0:T(8,128)S(1)}, f32[64,256]{1,0:T(8,128)S(1)}, u32[]{:S(2)}, u32[]{:S(2)}) collective-permute-start(f32[64,256]{1,0:T(8,128)S(1)} %get-tuple-element.33.resp), channel_id=1, source_target_pairs={{0,32},{32,64},{64,96},{96,128},{128,160},{160,192},{192,224},{224... | collective-permute-start | bytes 196616 | tf_op jit(solution)/shard_map/ppermute | solution.py:130
  167.3 3.5 %collective-permute-start.10 = (f32[64,128]{1,0:T(8,128)S(1)}, f32[64,128]{1,0:T(8,128)S(1)}, u32[]{:S(2)}, u32[]{:S(2)}) collective-permute-start(f32[64,128]{1,0:T(8,128)S(1)} %get-tuple-element.34), channel_id=1, source_target_pairs={{0,1},{1,2},{2,3},{3,4},{4,5},{5,6},{6,7},{7,8},{8,9},{9,10},{10,1... | collective-permute-start | bytes 98312 | tf_op jit(solution)/shard_map/ppermute | solution.py:130
  170.8 1.9 collective-permute-start.11
  172.8 0.0 all-to-all-done.5
  172.8 0.6 broadcast_in_dim.17
  173.4 5.7 %all-to-all-start.6 = ((f32[32,1,128]{2,1,0:T(1,128)}), f32[32,1,128]{2,1,0:T(1,128)S(1)}, u32[]{:S(2)}, u32[]{:S(2)}) async-start(f32[32,1,128]{2,1,0:T(1,128)} %broadcast_in_dim.17), calls=%async_computation.6 | async-start | bytes 32768 | tf_op jit(solution)/shard_map/all_to_all | solution.py:281
  179.1 0.6 dynamic-slice_bitcast_fusion
  179.7 7.2 %all-to-all-done.6 = f32[32,1,128]{2,1,0:T(1,128)S(1)} async-done(((f32[32,1,128]{2,1,0:T(1,128)}), f32[32,1,128]{2,1,0:T(1,128)S(1)}, u32[]{:S(2)}, u32[]{:S(2)}) %all-to-all-start.6) | async-done | bytes 16416 | tf_op jit(solution)/shard_map/all_to_all | solution.py:281
  186.9 0.0 collective-permute-done.10.below
  186.9 0.0 collective-permute-done.11.above
  186.9 0.0 collective-permute-done.8.ahead
  186.9 0.0 collective-permute-done.9.behind
  186.9 0.1 shard_map.83
  187.1 1.3 collective-permute-start.12
  188.4 6.2 %collective-permute-start.13 = (f32[64,256]{1,0:T(8,128)S(1)}, f32[64,256]{1,0:T(8,128)S(1)}, u32[]{:S(2)}, u32[]{:S(2)}) collective-permute-start(f32[64,256]{1,0:T(8,128)S(1)} %get-tuple-element.36.resp), channel_id=1, source_target_pairs={{0,32},{32,64},{64,96},{96,128},{128,160},{160,192},{192,224},{224... | collective-permute-start | bytes 196616 | tf_op jit(solution)/shard_map/ppermute | solution.py:130
  194.5 3.2 %collective-permute-start.14 = (f32[64,128]{1,0:T(8,128)S(1)}, f32[64,128]{1,0:T(8,128)S(1)}, u32[]{:S(2)}, u32[]{:S(2)}) collective-permute-start(f32[64,128]{1,0:T(8,128)S(1)} %get-tuple-element.37), channel_id=1, source_target_pairs={{0,1},{1,2},{2,3},{3,4},{4,5},{5,6},{6,7},{7,8},{8,9},{9,10},{10,1... | collective-permute-start | bytes 98312 | tf_op jit(solution)/shard_map/ppermute | solution.py:130
  197.7 1.9 collective-permute-start.15
  199.7 0.7 fusion
  202.4 0.0 collective-permute-done.14.below
  202.4 0.6 collective-permute-done.15.above
  203.0 0.8 shard_map.84
  203.8 0.6 copy.14
  (13 shorter events, 0.2 us)
Async XLA Ops:
  7.2 51.3 %all-gather.2.cloned.1.call-start = ((), (), s32[]{:S(2)}) async-start(), calls=%async_computation.7 | async-start | bytes 1179648 | tf_op jit(solution)/shard_map/all_gather | solution.py:290
  10.1 1.6 copy-start
  11.7 0.8 copy-start.1
  12.6 0.8 copy-start.2
  17.5 18.3 %collective-permute-start = (f32[64,256]{1,0:T(8,128)S(1)}, f32[64,256]{1,0:T(8,128)S(1)}, u32[]{:S(2)}, u32[]{:S(2)}) collective-permute-start(f32[64,256]{1,0:T(8,128)S(1)} %get-tuple-element.23.resp), channel_id=1, source_target_pairs={{32,0},{64,32},{96,64},{128,96},{160,128},{192,160},{224,192},{256... | collective-permute-start | bytes 196616 | tf_op jit(solution)/shard_map/ppermute | solution.py:130
  18.8 17.0 %collective-permute-start.1 = (f32[64,256]{1,0:T(8,128)S(1)}, f32[64,256]{1,0:T(8,128)S(1)}, u32[]{:S(2)}, u32[]{:S(2)}) collective-permute-start(f32[64,256]{1,0:T(8,128)S(1)} %get-tuple-element.23.resp), channel_id=1, source_target_pairs={{0,32},{32,64},{64,96},{96,128},{128,160},{160,192},{192,224},{224... | collective-permute-start | bytes 196616 | tf_op jit(solution)/shard_map/ppermute | solution.py:130
  26.0 8.3 %collective-permute-start.2 = (f32[64,128]{1,0:T(8,128)S(1)}, f32[64,128]{1,0:T(8,128)S(1)}, u32[]{:S(2)}, u32[]{:S(2)}) collective-permute-start(f32[64,128]{1,0:T(8,128)S(1)} %get-tuple-element.24), channel_id=1, source_target_pairs={{0,1},{1,2},{2,3},{3,4},{4,5},{5,6},{6,7},{7,8},{8,9},{9,10},{10,1... | collective-permute-start | bytes 98312 | tf_op jit(solution)/shard_map/ppermute | solution.py:130
  30.1 5.7 %collective-permute-start.3 = (f32[64,128]{1,0:T(8,128)S(1)}, f32[64,128]{1,0:T(8,128)S(1)}, u32[]{:S(2)}, u32[]{:S(2)}) collective-permute-start(f32[64,128]{1,0:T(8,128)S(1)} %get-tuple-element.25), channel_id=1, source_target_pairs={{1,0},{2,1},{3,2},{4,3},{5,4},{6,5},{7,6},{8,7},{9,8},{10,9},{11,1... | collective-permute-start | bytes 98312 | tf_op jit(solution)/shard_map/ppermute | solution.py:130
  35.9 16.5 %collective-permute-start.4 = (f32[64,256]{1,0:T(8,128)S(1)}, f32[64,256]{1,0:T(8,128)S(1)}, u32[]{:S(2)}, u32[]{:S(2)}) collective-permute-start(f32[64,256]{1,0:T(8,128)S(1)} %get-tuple-element.26.resp), channel_id=1, source_target_pairs={{32,0},{64,32},{96,64},{128,96},{160,128},{192,160},{224,192},{256... | collective-permute-start | bytes 196616 | tf_op jit(solution)/shard_map/ppermute | solution.py:130
  37.2 15.2 %collective-permute-start.5 = (f32[64,256]{1,0:T(8,128)S(1)}, f32[64,256]{1,0:T(8,128)S(1)}, u32[]{:S(2)}, u32[]{:S(2)}) collective-permute-start(f32[64,256]{1,0:T(8,128)S(1)} %get-tuple-element.26.resp), channel_id=1, source_target_pairs={{0,32},{32,64},{64,96},{96,128},{128,160},{160,192},{192,224},{224... | collective-permute-start | bytes 196616 | tf_op jit(solution)/shard_map/ppermute | solution.py:130
  45.3 4.3 %collective-permute-start.6 = (f32[64,128]{1,0:T(8,128)S(1)}, f32[64,128]{1,0:T(8,128)S(1)}, u32[]{:S(2)}, u32[]{:S(2)}) collective-permute-start(f32[64,128]{1,0:T(8,128)S(1)} %get-tuple-element.27), channel_id=1, source_target_pairs={{0,1},{1,2},{2,3},{3,4},{4,5},{5,6},{6,7},{7,8},{8,9},{9,10},{10,1... | collective-permute-start | bytes 98312 | tf_op jit(solution)/shard_map/ppermute | solution.py:130
  47.2 5.2 %collective-permute-start.7 = (f32[64,128]{1,0:T(8,128)S(1)}, f32[64,128]{1,0:T(8,128)S(1)}, u32[]{:S(2)}, u32[]{:S(2)}) collective-permute-start(f32[64,128]{1,0:T(8,128)S(1)} %get-tuple-element.28), channel_id=1, source_target_pairs={{1,0},{2,1},{3,2},{4,3},{5,4},{6,5},{7,6},{8,7},{9,8},{10,9},{11,1... | collective-permute-start | bytes 98312 | tf_op jit(solution)/shard_map/ppermute | solution.py:130
  53.3 9.3 %all-to-all-start = ((f32[8,8,256]{2,1,0:T(8,128)}), f32[8,8,256]{2,1,0:T(8,128)S(1)}, u32[]{:S(2)}, u32[]{:S(2)}) async-start(f32[8,8,256]{2,1,0:T(8,128)} %bitcast.2), calls=%async_computation | async-start | bytes 131072 | tf_op jit(solution)/shard_map/all_to_all | solution.py:298
  62.6 1.2 copy-start.3
  157.6 15.1 %all-to-all-start.5 = ((f32[16,1,128]{2,1,0:T(1,128)}), f32[16,1,128]{2,1,0:T(1,128)S(1)}, u32[]{:S(2)}, u32[]{:S(2)}) async-start(f32[16,1,128]{2,1,0:T(1,128)} %broadcast_in_dim.16), calls=%async_computation.5 | async-start | bytes 16384 | tf_op jit(solution)/shard_map/all_to_all | solution.py:281
  161.1 25.8 %collective-permute-start.8 = (f32[64,256]{1,0:T(8,128)S(1)}, f32[64,256]{1,0:T(8,128)S(1)}, u32[]{:S(2)}, u32[]{:S(2)}) collective-permute-start(f32[64,256]{1,0:T(8,128)S(1)} %get-tuple-element.33.resp), channel_id=1, source_target_pairs={{32,0},{64,32},{96,64},{128,96},{160,128},{192,160},{224,192},{256... | collective-permute-start | bytes 196616 | tf_op jit(solution)/shard_map/ppermute | solution.py:130
  162.4 24.5 %collective-permute-start.9 = (f32[64,256]{1,0:T(8,128)S(1)}, f32[64,256]{1,0:T(8,128)S(1)}, u32[]{:S(2)}, u32[]{:S(2)}) collective-permute-start(f32[64,256]{1,0:T(8,128)S(1)} %get-tuple-element.33.resp), channel_id=1, source_target_pairs={{0,32},{32,64},{64,96},{96,128},{128,160},{160,192},{192,224},{224... | collective-permute-start | bytes 196616 | tf_op jit(solution)/shard_map/ppermute | solution.py:130
  167.3 19.5 %collective-permute-start.10 = (f32[64,128]{1,0:T(8,128)S(1)}, f32[64,128]{1,0:T(8,128)S(1)}, u32[]{:S(2)}, u32[]{:S(2)}) collective-permute-start(f32[64,128]{1,0:T(8,128)S(1)} %get-tuple-element.34), channel_id=1, source_target_pairs={{0,1},{1,2},{2,3},{3,4},{4,5},{5,6},{6,7},{7,8},{8,9},{9,10},{10,1... | collective-permute-start | bytes 98312 | tf_op jit(solution)/shard_map/ppermute | solution.py:130
  170.8 16.0 %collective-permute-start.11 = (f32[64,128]{1,0:T(8,128)S(1)}, f32[64,128]{1,0:T(8,128)S(1)}, u32[]{:S(2)}, u32[]{:S(2)}) collective-permute-start(f32[64,128]{1,0:T(8,128)S(1)} %get-tuple-element.35), channel_id=1, source_target_pairs={{1,0},{2,1},{3,2},{4,3},{5,4},{6,5},{7,6},{8,7},{9,8},{10,9},{11,1... | collective-permute-start | bytes 98312 | tf_op jit(solution)/shard_map/ppermute | solution.py:130
  173.4 13.4 %all-to-all-start.6 = ((f32[32,1,128]{2,1,0:T(1,128)}), f32[32,1,128]{2,1,0:T(1,128)S(1)}, u32[]{:S(2)}, u32[]{:S(2)}) async-start(f32[32,1,128]{2,1,0:T(1,128)} %broadcast_in_dim.17), calls=%async_computation.6 | async-start | bytes 32768 | tf_op jit(solution)/shard_map/all_to_all | solution.py:281
  187.1 15.9 %collective-permute-start.12 = (f32[64,256]{1,0:T(8,128)S(1)}, f32[64,256]{1,0:T(8,128)S(1)}, u32[]{:S(2)}, u32[]{:S(2)}) collective-permute-start(f32[64,256]{1,0:T(8,128)S(1)} %get-tuple-element.36.resp), channel_id=1, source_target_pairs={{32,0},{64,32},{96,64},{128,96},{160,128},{192,160},{224,192},{256... | collective-permute-start | bytes 196616 | tf_op jit(solution)/shard_map/ppermute | solution.py:130
  188.4 14.6 %collective-permute-start.13 = (f32[64,256]{1,0:T(8,128)S(1)}, f32[64,256]{1,0:T(8,128)S(1)}, u32[]{:S(2)}, u32[]{:S(2)}) collective-permute-start(f32[64,256]{1,0:T(8,128)S(1)} %get-tuple-element.36.resp), channel_id=1, source_target_pairs={{0,32},{32,64},{64,96},{96,128},{128,160},{160,192},{192,224},{224... | collective-permute-start | bytes 196616 | tf_op jit(solution)/shard_map/ppermute | solution.py:130
  194.5 7.8 %collective-permute-start.14 = (f32[64,128]{1,0:T(8,128)S(1)}, f32[64,128]{1,0:T(8,128)S(1)}, u32[]{:S(2)}, u32[]{:S(2)}) collective-permute-start(f32[64,128]{1,0:T(8,128)S(1)} %get-tuple-element.37), channel_id=1, source_target_pairs={{0,1},{1,2},{2,3},{3,4},{4,5},{5,6},{6,7},{7,8},{8,9},{9,10},{10,1... | collective-permute-start | bytes 98312 | tf_op jit(solution)/shard_map/ppermute | solution.py:130
  197.7 5.2 %collective-permute-start.15 = (f32[64,128]{1,0:T(8,128)S(1)}, f32[64,128]{1,0:T(8,128)S(1)}, u32[]{:S(2)}, u32[]{:S(2)}) collective-permute-start(f32[64,128]{1,0:T(8,128)S(1)} %get-tuple-element.38), channel_id=1, source_target_pairs={{1,0},{2,1},{3,2},{4,3},{5,4},{6,5},{7,6},{8,7},{9,8},{10,9},{11,1... | collective-permute-start | bytes 98312 | tf_op jit(solution)/shard_map/ppermute | solution.py:130
Sparse Core Ops, SparseCore 0:
  10.1 34.1 all-gather.1

commit v2 on v1

v2 whole, which is shorter than its diff:
```python
import jax
import jax.numpy as jnp
from jax import lax
from jax.experimental import pallas as pl
from jax.experimental.pallas import tpu as pltpu
from jax.sharding import Mesh
from jax.sharding import PartitionSpec as P

SWEEPS = 2
BETA_POTTS = 1.0
COV_RIDGE = 0.01

SLAB = ("x1", "x0", "z2", "z1")
TILE = ("z0", "y2", "y1", "y0", "core")
BRICK = ("x1", "x0", "core")
NEAR = ("y2", "y1", "y0")
FAR = ("z2", "z1", "z0")
ROUND = (("y2", "y1", "y0", "core"), ("x1", "x0", "z2", "z1", "z0"))

WIDTH = 128
CELLS = 256
HALF = 64
PACKET = HALF + 8
VMEM = pl.BlockSpec(memory_space=pltpu.VMEM)
SMEM = pl.BlockSpec(memory_space=pltpu.SMEM)
HBM = pl.BlockSpec(memory_space=pl.ANY)
PARAMS = pltpu.CompilerParams(vmem_limit_bytes=40 * 1024 * 1024)


def call(kernel, shapes, *args, scalars=0, flops=1 << 20):
    out = [jax.ShapeDtypeStruct(shape, kind) for shape, kind in shapes]
    return pl.pallas_call(
        kernel,
        out_shape=out,
        in_specs=[SMEM] * scalars + [VMEM] * (len(args) - scalars),
        out_specs=[VMEM] * len(out),
        compiler_params=PARAMS,
        cost_estimate=pl.CostEstimate(flops=flops, bytes_accessed=1 << 20, transcendentals=0),
    )(*args)


def iotas(shape):
    return (
        lax.broadcasted_iota(jnp.int32, shape, 0),
        lax.broadcasted_iota(jnp.int32, shape, 1),
    )


def matmul(lhs, rhs, dims=((1,), (0,))):
    return lax.dot_general(lhs, rhs, (dims, ((), ())), preferred_element_type=jnp.float32)


def normalise(scores):
    top = jnp.max(scores, axis=0, keepdims=True)
    expon = jnp.exp(scores - top)
    return expon / jnp.sum(expon, axis=0, keepdims=True)


def put(core, resp, resp_ref, near_ref, far_ref):
    first, last = resp[:, :WIDTH], resp[:, WIDTH:]
    resp_ref[...] = resp
    near_ref[...] = jnp.where(core == 0, last, first)
    far_ref[...] = jnp.where(core == 0, first, last)


CHUNK = 16


def start_kernel(
    core, weights, flat, tissue, means, whiten,
    scores, resp, near, far, spread, mask,
    weights_in, flat_in, tissue_in, means_in, whiten_in, diag, sems,
):
    count = whiten.shape[0]
    small = zip((flat, means, tissue, weights), (flat_in, means_in, tissue_in, weights_in))
    copies = [pltpu.make_async_copy(src, dst, sems.at[n]) for n, (src, dst) in enumerate(small)]
    blocks = [
        pltpu.make_async_copy(
            whiten.at[pl.ds(begin, CHUNK)],
            whiten_in.at[pl.ds(begin, CHUNK)],
            sems.at[4 + begin // CHUNK],
        )
        for begin in range(0, count, CHUNK)
    ]
    for copy in copies + blocks:
        copy.start()
    row_at, col_at = iotas((WIDTH, WIDTH))
    copies[0].wait()
    full = flat_in[...].astype(jnp.float32)
    cells = full.T.astype(jnp.bfloat16)
    for n in range(spread.shape[0]):
        spread[n] = full
    for copy in copies[1:]:
        copy.wait()
    for n, block in enumerate(blocks):
        block.wait()
        for own in range(n * CHUNK, (n + 1) * CHUNK):
            matrix = whiten_in[own]
            full = matrix.astype(jnp.float32)
            shift = jnp.sum(full * means_in[own : own + 1], axis=1, keepdims=True)
            proj = matmul(matrix, cells) - shift
            scores[own : own + 1] = jnp.sum(proj * proj, axis=0, keepdims=True)
            diag[own : own + 1] = jnp.sum(
                jnp.where(row_at == col_at, full, 0.0), axis=0, keepdims=True
            )
    prior = weights_in[...]
    prior = jnp.log(prior / jnp.sum(prior, axis=1, keepdims=True))
    row_at, col_at = iotas((count, count))
    prior = jnp.where(row_at == col_at, jnp.broadcast_to(prior, (count, count)), 0.0)
    offset = jnp.sum(prior, axis=1, keepdims=True) + jnp.sum(
        jnp.log(diag[...]), axis=1, keepdims=True
    )
    result = offset - 0.5 * scores[...]
    scores[...] = result
    tissue_f = tissue_in[...].astype(jnp.float32)
    tissue_f = jnp.concatenate([tissue_f[:1], tissue_f[1:]], axis=1)
    mask[...] = tissue_f
    put(core[0], normalise(result) * tissue_f, resp, near, far)


def start(core, weights, flat, tissue, means, whiten):
    count = whiten.shape[0]
    f32 = jnp.float32
    shapes = [(count, CELLS), (count, CELLS), (count, WIDTH), (count, WIDTH)]
    shapes += [(8, CELLS, WIDTH), (1, CELLS)]
    return pl.pallas_call(
        start_kernel,
        out_shape=[jax.ShapeDtypeStruct(shape, f32) for shape in shapes],
        in_specs=[SMEM] + [HBM] * 5,
        out_specs=[VMEM] * len(shapes),
        scratch_shapes=[
            pltpu.VMEM(weights.shape, f32),
            pltpu.VMEM(flat.shape, flat.dtype),
            pltpu.VMEM(tissue.shape, tissue.dtype),
            pltpu.VMEM(means.shape, f32),
            pltpu.VMEM(whiten.shape, whiten.dtype),
            pltpu.VMEM((count, WIDTH), f32),
            pltpu.SemaphoreType.DMA((4 + count // CHUNK,)),
        ],
        compiler_params=pltpu.CompilerParams(vmem_limit_bytes=58 * 1024 * 1024),
        cost_estimate=pl.CostEstimate(flops=1 << 29, bytes_accessed=1 << 21, transcendentals=0),
    )(core, weights, flat, tissue, means, whiten)


def sweep_kernel(
    core, scores, resp, slab_even, slab_odd, near_in, far_in, mask, out, near, far
):
    lane = iotas((resp.shape[0], WIDTH))[1]
    rows = (resp[:, :WIDTH], resp[:, WIDTH:])
    below = jnp.where(core[0] == 0, far_in[...], near_in[...])
    above = jnp.where(core[0] == 0, near_in[...], far_in[...])
    fields = []
    for row, others in zip(rows, (below + rows[1], rows[0] + above)):
        after = jnp.where(lane < WIDTH - 1, pltpu.roll(row, WIDTH - 1, 1), 0.0)
        before = jnp.where(lane > 0, pltpu.roll(row, 1, 1), 0.0)
        fields.append(others + after + before)
    field = jnp.concatenate(fields, axis=1) + slab_even[...] + slab_odd[...]
    put(core[0], normalise(scores[...] + BETA_POTTS * field) * mask[...], out, near, far)


def swapped(part, axes, begin):
    count = lax.axis_size(axes)
    pairs = [(i, i + 1) for i in range(begin, count - 1, 2)]
    return lax.ppermute(part, axes, pairs + [(j, i) for i, j in pairs])


def sweep(core, scores, resp, near, far, mask):
    f32 = jnp.float32
    count = resp.shape[0]
    return call(
        sweep_kernel,
        [((count, CELLS), f32), ((count, WIDTH), f32), ((count, WIDTH), f32)],
        core, scores, resp, swapped(resp, SLAB, 0), swapped(resp, SLAB, 1),
        swapped(near, TILE, 0), swapped(far, TILE, 1), mask, scalars=1,
    )


def moments_kernel(resp, shared, packet, turned, total):
    blocks, count = resp.shape[:2]
    row_at, col_at = iotas((WIDTH, WIDTH))
    ones = jnp.ones((CELLS, WIDTH), jnp.bfloat16)
    acc = [jnp.zeros((WIDTH, 2 * WIDTH), jnp.float32) for _ in range(count)]
    for block in range(blocks):
        cells = shared[block]
        flipped = cells.T
        turned[block] = flipped.astype(jnp.bfloat16)
        wide = jnp.concatenate([cells.astype(jnp.bfloat16), ones], axis=1)
        for k in range(count):
            weighted = (flipped * resp[block, k : k + 1, :]).astype(jnp.bfloat16)
            acc[k] = acc[k] + matmul(weighted, wide)
    firsts = jnp.zeros((WIDTH, WIDTH), jnp.float32)
    for k in range(count):
        firsts = jnp.where(col_at == k, acc[k][:, WIDTH:], firsts)
    firsts = firsts.T
    counts = jnp.sum(jnp.sum(resp[...], axis=0), axis=1, keepdims=True)
    counts = jnp.broadcast_to(counts, (count, WIDTH))
    total[...] = jnp.sum(counts, axis=0, keepdims=True)
    fold_row, fold_col = iotas((HALF, WIDTH))
    for k in range(count):
        sym = acc[k][:, :WIDTH]
        sym = sym + sym.T
        low = (fold_col < HALF) | (fold_row > fold_col - HALF)
        packet[k, :HALF] = jnp.where(low, sym[HALF:], pltpu.roll(sym[:HALF], HALF, 1))
        diag = jnp.sum(jnp.where(row_at == col_at, sym, 0.0), axis=0, keepdims=True)
        packet[k, HALF:] = jnp.concatenate(
            [diag, firsts[k : k + 1], counts[k : k + 1], jnp.zeros((5, WIDTH), jnp.float32)],
            axis=0,
        )


def gather_kernel(packets, out):
    total = jnp.sum(packets[...], axis=0)
    for k in range(out.shape[0]):
        out[k] = total


def split(value):
    high = value.astype(jnp.bfloat16).astype(jnp.float32)
    rest = value - high
    middle = rest.astype(jnp.bfloat16).astype(jnp.float32)
    return high, middle, rest - middle


STEP = 16


def whiten_chain(cov):
    row_at, col_at = iotas((WIDTH, WIDTH))
    wide = (STEP, 2 * WIDTH)
    rest = jnp.concatenate([cov, jnp.where(row_at == col_at, 1.0, 0.0)], axis=1)
    sub = lax.broadcasted_iota(jnp.int32, (STEP, WIDTH), 0)
    done, scales = [], []
    for begin in range(0, WIDTH, STEP):
        panel = rest[:STEP]
        cols = [
            jnp.broadcast_to(panel[:, begin + j : begin + j + 1], (STEP, WIDTH))
            for j in range(STEP)
        ]
        scale = jnp.broadcast_to(cols[0][:1], (STEP, WIDTH))
        for j in range(STEP - 1):
            inverse = 1.0 / cols[j][j : j + 1]
            mult = jnp.where(sub > j, cols[j] * inverse, 0.0)
            for l in range(j + 1, STEP):
                cols[l] = cols[l] - mult * jnp.broadcast_to(cols[l][j : j + 1], (STEP, WIDTH))
            both = jnp.concatenate([mult, mult], axis=1)
            panel = panel - both * jnp.broadcast_to(panel[j : j + 1], wide)
            pivot = jnp.broadcast_to(cols[j + 1][j + 1 : j + 2], (STEP, WIDTH))
            scale = jnp.where(sub > j, pivot, scale)
        root = lax.rsqrt(scale)
        panel = panel * jnp.concatenate([root, root], axis=1)
        scales.append(scale)
        done.append(panel[:, WIDTH:])
        if begin + STEP < WIDTH:
            high, middle, low = split(panel)
            right = jnp.concatenate([high, middle, low, high, middle, high], axis=0)
            high, middle, low = (part[:, :WIDTH] for part in (high, middle, low))
            left = jnp.concatenate([high, high, high, middle, middle, low], axis=0)
            update = matmul(left.astype(jnp.bfloat16), right.astype(jnp.bfloat16), ((0,), (0,)))
            rest = rest[STEP:] - update[begin + STEP :]
    logdet = -0.5 * jnp.sum(jnp.log(jnp.concatenate(scales, axis=0)), axis=0, keepdims=True)
    return jnp.concatenate(done, axis=0), logdet


def unfolded(fold):
    both = jnp.concatenate([pltpu.roll(fold, HALF, 1), fold], axis=0)
    return both, both.T


def factor_kernel(packets, out):
    row_at, col_at = iotas((WIDTH, WIDTH))
    packet = jnp.sum(packets[...], axis=0)
    both, turned = unfolded(packet[:HALF])
    diag, first, counts = (packet[HALF + n : HALF + n + 1] for n in range(3))
    left = col_at < HALF
    kept = (left & (row_at <= col_at)) | ((row_at >= HALF) & (left | (row_at > col_at)))
    sym = jnp.where(row_at == col_at, diag, jnp.where(kept, both, turned))
    centre = first / counts
    tall = jnp.broadcast_to(centre, (WIDTH, WIDTH))
    cov = 0.5 * sym / counts - tall.T * tall
    cov = jnp.where(row_at == col_at, cov + COV_RIDGE, cov)
    whiten, logdet = whiten_chain(cov)
    shift = jnp.sum(whiten * tall, axis=1, keepdims=True)
    shift = jnp.broadcast_to(shift, (WIDTH, WIDTH)).T[:1]
    offset = jnp.log(counts) + logdet
    diag = jnp.sum(jnp.where(row_at == col_at, whiten, 0.0), axis=0, keepdims=True)
    fold_row, fold_col = iotas((HALF, WIDTH))
    low = (fold_col < HALF) | (fold_row >= fold_col - HALF)
    fold = jnp.where(low, whiten[HALF:], pltpu.roll(whiten.T[:HALF], HALF, 1))
    zeros = jnp.zeros((4, WIDTH), jnp.float32)
    result = jnp.concatenate([fold, diag, shift, centre, offset, zeros], axis=0)
    for k in range(out.shape[0]):
        out[k] = result


def second_kernel(packets, turned, scores):
    row_at, col_at = iotas((WIDTH, WIDTH))
    top, left = row_at < HALF, col_at < HALF
    below = (row_at >= HALF) & (left | (row_at >= col_at))
    above = top & (row_at > col_at)
    for k in range(packets.shape[0]):
        both, flipped = unfolded(packets[k, :HALF])
        diag, shift, centre, offset = (packets[k, HALF + n : HALF + n + 1] for n in range(4))
        whiten = jnp.where(below, both, jnp.where(above, flipped, 0.0))
        half = jnp.where(top & (row_at == col_at), diag, whiten).astype(jnp.bfloat16)
        shift = jnp.broadcast_to(shift, (WIDTH, WIDTH)).T
        shift = jnp.concatenate([shift, shift], axis=1)
        offset = jnp.concatenate([offset, offset], axis=1)
        for block in range(turned.shape[0]):
            proj = matmul(half, turned[block]) - shift
            quad = jnp.sum(proj * proj, axis=0, keepdims=True)
            scores[block, k : k + 1, :CELLS] = offset - 0.5 * quad
            scores[block, k : k + 1, CELLS:] = centre


def likely_kernel(place, part, mask, total, scores, resp, near, far, means, totals):
    values = part[:, :CELLS]
    scores[...] = values
    row = iotas((part.shape[0], WIDTH))[0]
    for n in range(2):
        own = jnp.where(row == 2 * place[1] + n, part[:, CELLS:], 0.0)
        means[n : n + 1] = jnp.sum(own, axis=0, keepdims=True)
    tissue_f = mask[...]
    top = jnp.max(values, axis=0, keepdims=True)
    expon = jnp.exp(values - top)
    weight = jnp.sum(expon, axis=0, keepdims=True)
    put(place[0], expon / weight * tissue_f, resp, near, far)
    lse = jnp.sum((top + jnp.log(weight)) * tissue_f, axis=1, keepdims=True)
    cells = jnp.sum(tissue_f, axis=1, keepdims=True)
    lane = iotas((1, WIDTH))[1]
    result = jnp.where(lane == 0, lse, jnp.where(lane == 1, cells, total[...]))
    for n in range(totals.shape[0]):
        totals[n] = result


def swap_all(value, axes):
    return lax.all_to_all(value, axes, 0, 0, tiled=True)


def shards(embed, tissue, whiten0, means0, weights0):
    count = whiten0.shape[0]
    f32 = jnp.float32
    flat = embed.reshape(CELLS, WIDTH)
    place = jnp.stack([lax.axis_index("core"), lax.axis_index(TILE)])
    resp_shapes = [((count, CELLS), f32), ((count, WIDTH), f32), ((count, WIDTH), f32)]

    scores, resp, near, far, spread, mask = start(
        place, weights0.reshape(1, count), flat, tissue.reshape(2, WIDTH), means0, whiten0
    )
    shared = swap_all(spread, BRICK)
    for _ in range(SWEEPS):
        resp, near, far = sweep(place, scores, resp, near, far, mask)

    part = swap_all(resp.reshape(8, 8, CELLS), BRICK)
    packets, turned, total = call(
        moments_kernel,
        [((8, PACKET, WIDTH), f32), ((8, WIDTH, CELLS), jnp.bfloat16), ((1, WIDTH), f32)],
        part, shared, flops=1 << 30,
    )
    (packets,) = call(gather_kernel, [((8, PACKET, WIDTH), f32)], swap_all(packets, NEAR))
    packets = swap_all(packets, FAR)
    (packets,) = call(factor_kernel, [((8, PACKET, WIDTH), f32)], packets, flops=1 << 27)
    packets = swap_all(packets, NEAR)
    (part,) = call(
        second_kernel, [((8, 8, CELLS + WIDTH), f32)], packets, turned, flops=1 << 29
    )
    part = swap_all(part, BRICK).reshape(count, CELLS + WIDTH)

    sizes = [lax.axis_size(axes) for axes in ROUND]
    scores, resp, near, far, means_out, totals = call(
        likely_kernel,
        [((count, CELLS), f32)] + resp_shapes + [((2, WIDTH), f32), ((sizes[0], 1, WIDTH), f32)],
        place, part, mask, total, scalars=1,
    )
    totals = jnp.sum(swap_all(totals, ROUND[0]), axis=0)
    totals = swap_all(jnp.broadcast_to(totals[None], (sizes[1], 1, WIDTH)), ROUND[1])
    for _ in range(SWEEPS):
        resp, near, far = sweep(place, scores, resp, near, far, mask)
    totals, resp = lax.optimization_barrier((totals, resp))
    totals = jnp.sum(totals, axis=0)
    bins = CELLS * sizes[0] * sizes[1]
    score = (totals[0, 0] - totals[0, 1] * jnp.log(totals[0, 2])) / bins
    return (resp.reshape(count, 1, 2, WIDTH), means_out, score)


def solution(mesh):
    bits = Mesh(mesh.devices.reshape((2,) * 9), SLAB + TILE)
    in_specs = (P(SLAB, TILE, None, None), P(SLAB, TILE, None), P(), P(), P())
    out_specs = (P(None, SLAB, TILE, None), P(TILE, None), P())
    return jax.shard_map(shards, mesh=bits, in_specs=in_specs, out_specs=out_specs, check_vma=False)
```

time: 216 us -> 199 us (0.921)
  blocking collectives: 72.9 us -> 89.8 us
  between operations: 17.5 us -> 4.06 us
  Pallas kernels: 25.9 us -> 17.3 us
  starting transfers between devices: 69 us -> 63.6 us
  local copies, waits for them, and re-layouts: 8.36 us -> 4.98 us
    all_to_all x4 -> x6, blocking collectives: 72.9 us -> 89.8 us  [swap_all(): return lax.all_to_all(value, axes, 0, 0, tiled=True)]
    pallas_call x9 -> x10, Pallas kernels: 25.9 us -> 17.3 us  [the longest x9 12.3 us: call(): pl.pallas_call(kernel, out_shape=out, in_specs=[SMEM] * scalars + [VMEM]...]
    ppermute x16, starting transfers between devices: 54.7 us -> 50 us  [swapped(): return lax.ppermute(part, axes, pairs + [(j, i) for i, j in pairs])]
    ppermute x16, waiting for transfers between devices: 4.89 us -> 8.34 us  [swapped(): return lax.ppermute(part, axes, pairs + [(j, i) for i, j in pairs])]
    all_to_all x3 -> x2, waiting for transfers between devices: 11.4 us -> 8.62 us  [swap_all(): return lax.all_to_all(value, axes, 0, 0, tiled=True)]
    convert_element_type x2 -> x0, other arithmetic: 2.18 us -> none  [the longest x1 1.49 us: shards(): shared = lax.all_gather(flat.astype(f32), BRICK, axis=0, tiled=True)]
    unnamed x8 -> x12, local copies, waits for them, and re-layouts: 4.42 us -> 3.04 us
    all_to_all x3 -> x2, starting transfers between devices: 14.3 us -> 13.6 us  [swap_all(): return lax.all_to_all(value, axes, 0, 0, tiled=True)]
  transfers between devices with their start and end apart: 20 -> 18, of which waited for: 5 -> 5; matrix products, arithmetic and copies ran while one was open for 2% -> 0% of each run, Pallas kernels for 2% -> 1%
where the time goes in v2:
time: 199 us; the launch traced here: 197 us
  blocking collectives  89.8 us (45%)
  starting transfers between devices  63.6 us (32%)
  Pallas kernels  17.3 us (9%)
  waiting for transfers between devices  17 us (9%)
  local copies, waits for them, and re-layouts  4.98 us (3%)
  between operations  4.06 us (2%)
    all_to_all x6, blocking collectives, swap_all(): return lax.all_to_all(value, axes, 0, 0, tiled=True)  89.8 us
    ppermute x16, starting transfers between devices, swapped(): return lax.ppermute(part, axes, pairs + [(j, i) for i, j in pairs])  50 us
    all_to_all x2, starting transfers between devices, swap_all(): return lax.all_to_all(value, axes, 0, 0, tiled=True)  13.6 us
    pallas_call x9, Pallas kernels, call(): pl.pallas_call(kernel, out_shape=out, in_specs=[SMEM] * scalars + [VMEM]...  12.3 us
    all_to_all x2, waiting for transfers between devices, swap_all(): return lax.all_to_all(value, axes, 0, 0, tiled=True)  8.62 us
    ppermute x16, waiting for transfers between devices, swapped(): return lax.ppermute(part, axes, pairs + [(j, i) for i, j in pairs])  8.34 us
    pallas_call x1, Pallas kernels, start(): pl.pallas_call(start_kernel, out_shape=[jax.ShapeDtypeStruct(shape, f32)...  5.01 us
  transfers between devices with their start and end apart: 18, of which 5 were waited for; matrix products, arithmetic and copies ran while one was open for 0% of the time, Pallas kernels for 1%

profile of v2, /device:TPU:1, one launch (start us, length us, event | category | flops | bytes accessed | tf_op | source)
XLA Modules:
  0.0 197.5 jit_solution(507272754569229378)
XLA Ops:
  0.6 0.7 pad_add_fusion.core.place
  1.3 5.0 %shard_map.76 = (f32[64,256]{1,0:T(8,128)}, f32[64,256]{1,0:T(8,128)}, f32[64,128]{1,0:T(8,128)}, f32[64,128]{1,0:T(8,128)}, f32[8,256,128]{2,1,0:T(8,128)}, /*index=5*/f32[1,256]{1,0:T(1,128)}) custom-call(s32[2]{0:T(128)} %pad_add_fusion.core.place, f32[1,64]{1,0:T(1,128)} %bitcast.16, bf16[256,128]{1,0:T(8,128)(2,1)} %bitcast.12, s32[2,128]{1,0:T(2,128)} %bitcast.15, ...), custom_call_target="tpu_custom_call" | custom-call | flops 536870912 | bytes 2097152 | tf_op jit(solution)/shard_map/pallas_call | solution.py:126
  6.3 6.6 %collective-permute-start = (f32[64,256]{1,0:T(8,128)}, f32[64,256]{1,0:T(8,128)S(1)}, u32[]{:S(2)}, u32[]{:S(2)}) collective-permute-start(f32[64,256]{1,0:T(8,128)} %get-tuple-element.29.resp), channel_id=1, source_target_pairs={{0,32},{64,96},{128,160},{192,224},{256,288},{320,352},{384,416},{... | collective-permute-start | bytes 196616 | tf_op jit(solution)/shard_map/ppermute | solution.py:164
  13.0 0.7 collective-permute-start.1
  13.7 4.1 %collective-permute-start.2 = (f32[64,128]{1,0:T(8,128)}, f32[64,128]{1,0:T(8,128)S(1)}, u32[]{:S(2)}, u32[]{:S(2)}) collective-permute-start(f32[64,128]{1,0:T(8,128)} %get-tuple-element.30), channel_id=1, source_target_pairs={{0,1},{2,3},{4,5},{6,7},{8,9},{10,11},{12,13},{14,15},{16,17},{18,... | collective-permute-start | bytes 98312 | tf_op jit(solution)/shard_map/ppermute | solution.py:164
  17.7 1.9 collective-permute-start.3
  19.7 0.0 collective-permute-done.2.near_in
  19.7 3.5 %collective-permute-done.3.far_in = f32[64,128]{1,0:T(8,128)S(1)} collective-permute-done((f32[64,128]{1,0:T(8,128)}, f32[64,128]{1,0:T(8,128)S(1)}, u32[]{:S(2)}, u32[]{:S(2)}) %collective-permute-start.3) | collective-permute-done | bytes 32800 | tf_op jit(solution)/shard_map/ppermute | solution.py:164
  23.2 0.0 collective-permute-done.slab_even
  23.2 0.0 collective-permute-done.1.slab_odd
  23.2 0.0 copy-done.5
  23.2 0.0 copy-start
  23.2 0.8 copy-done
  24.0 0.8 copy-done.1
  24.9 0.7 copy-done.2
  25.5 0.7 shard_map.77
  26.2 9.4 %collective-permute-start.4 = (f32[64,256]{1,0:T(8,128)S(1)}, f32[64,256]{1,0:T(8,128)S(1)}, u32[]{:S(2)}, u32[]{:S(2)}) collective-permute-start(f32[64,256]{1,0:T(8,128)S(1)} %get-tuple-element.33.resp), channel_id=1, source_target_pairs={{0,32},{64,96},{128,160},{192,224},{256,288},{320,352},{384,416},{... | collective-permute-start | bytes 196616 | tf_op jit(solution)/shard_map/ppermute | solution.py:164
  35.7 0.7 collective-permute-start.5
  36.4 1.9 collective-permute-start.6
  38.3 3.6 %collective-permute-start.7 = (f32[64,128]{1,0:T(8,128)S(1)}, f32[64,128]{1,0:T(8,128)S(1)}, u32[]{:S(2)}, u32[]{:S(2)}) collective-permute-start(f32[64,128]{1,0:T(8,128)S(1)} %get-tuple-element.35), channel_id=1, source_target_pairs={{1,2},{3,4},{5,6},{7,8},{9,10},{11,12},{13,14},{15,16},{17,18},{19... | collective-permute-start | bytes 98312 | tf_op jit(solution)/shard_map/ppermute | solution.py:164
  41.9 0.0 collective-permute-done.6.near_in
  41.9 1.6 collective-permute-done.7.far_in
  43.5 0.0 collective-permute-done.4.slab_even
  43.5 0.0 collective-permute-done.5.slab_odd
  43.5 0.7 copy-done.3
  44.2 1.3 shard_map.78
  45.5 10.3 %all_to_all.40.resp = f32[8,8,256]{2,1,0:T(8,128)S(1)} all-to-all(f32[8,8,256]{2,1,0:T(8,128)S(1)} %bitcast.11), channel_id=1, replica_groups=mesh['x1'=2,'x0'=2,'z2'=2,'z1'=2,'z0'=2,'y2'=2,'y1'=2,'y0'=2,'core'=2] {..., dimensions={0} | all-to-all | bytes 131072 | tf_op jit(solution)/shard_map/all_to_all | solution.py:336
  55.8 19.3 %all_to_all.41.shared = f32[8,256,128]{2,1,0:T(8,128)S(1)} all-to-all(f32[8,256,128]{2,1,0:T(8,128)} %get-tuple-element.37), channel_id=1, replica_groups=mesh['x1'=2,'x0'=2,'z2'=2,'z1'=2,'z0'=2,'y2'=2,'y1'=2,'y0'=2,'core'=2] {..., dimensions={0} | all-to-all | bytes 2097152 | tf_op jit(solution)/shard_map/all_to_all | solution.py:336
  75.1 1.6 shard_map.79
  76.7 19.8 %all_to_all.42.packets = f32[8,72,128]{2,1,0:T(8,128)S(1)} all-to-all(f32[8,72,128]{2,1,0:T(8,128)S(1)} %get-tuple-element.38), channel_id=1, replica_groups=mesh['x1'=2,'x0'=2,'z2'=2,'z1'=2,'z0'=2,'y2'=2,'y1'=2,'y0'=2,'core'=2] {..., dimensions={0} | all-to-all | bytes 589824 | tf_op jit(solution)/shard_map/all_to_all | solution.py:336
  96.5 0.0 copy-start.4
  96.5 15.3 %all_to_all.43.packets = f32[8,72,128]{2,1,0:T(8,128)S(1)} all-to-all(f32[8,72,128]{2,1,0:T(8,128)S(1)} %shard_map.80), channel_id=1, replica_groups=mesh['x1'=2,'x0'=2,'z2'=2,'z1'=2,'z0'=2,'y2'=2,'y1'=2,'y0'=2,'core'=2] {..., dimensions={0} | all-to-all | bytes 589824 | tf_op jit(solution)/shard_map/all_to_all | solution.py:336
  111.7 3.8 %shard_map.81 = f32[8,72,128]{2,1,0:T(8,128)S(1)} custom-call(f32[8,72,128]{2,1,0:T(8,128)S(1)} %all_to_all.43.packets), custom_call_target="tpu_custom_call" | custom-call | flops 134217728 | bytes 1048576 | tf_op jit(solution)/shard_map/pallas_call | solution.py:32
  115.6 13.2 %all_to_all.44.packets = f32[8,72,128]{2,1,0:T(8,128)S(1)} all-to-all(f32[8,72,128]{2,1,0:T(8,128)S(1)} %shard_map.81), channel_id=1, replica_groups=mesh['x1'=2,'x0'=2,'z2'=2,'z1'=2,'z0'=2,'y2'=2,'y1'=2,'y0'=2,'core'=2] {..., dimensions={0} | all-to-all | bytes 589824 | tf_op jit(solution)/shard_map/all_to_all | solution.py:336
  128.7 1.6 shard_map.82
  130.4 12.0 %all_to_all.45 = f32[8,8,384]{2,1,0:T(8,128)S(1)} all-to-all(f32[8,8,384]{2,1,0:T(8,128)S(1)} %shard_map.82), channel_id=1, replica_groups=mesh['x1'=2,'x0'=2,'z2'=2,'z1'=2,'z0'=2,'y2'=2,'y1'=2,'y0'=2,'core'=2] {..., dimensions={0} | all-to-all | bytes 196608 | tf_op jit(solution)/shard_map/all_to_all | solution.py:336
  142.4 0.0 copy-done.4
  142.4 1.3 shard_map.83
  143.7 2.1 %collective-permute-start.8 = (f32[64,256]{1,0:T(8,128)S(1)}, f32[64,256]{1,0:T(8,128)S(1)}, u32[]{:S(2)}, u32[]{:S(2)}) collective-permute-start(f32[64,256]{1,0:T(8,128)S(1)} %get-tuple-element.43.resp), channel_id=1, source_target_pairs={{0,32},{64,96},{128,160},{192,224},{256,288},{320,352},{384,416},{... | collective-permute-start | bytes 196616 | tf_op jit(solution)/shard_map/ppermute | solution.py:164
  145.8 0.7 collective-permute-start.9
  146.5 3.0 %collective-permute-start.10 = (f32[64,128]{1,0:T(8,128)S(1)}, f32[64,128]{1,0:T(8,128)S(1)}, u32[]{:S(2)}, u32[]{:S(2)}) collective-permute-start(f32[64,128]{1,0:T(8,128)S(1)} %get-tuple-element.44), channel_id=1, source_target_pairs={{0,1},{2,3},{4,5},{6,7},{8,9},{10,11},{12,13},{14,15},{16,17},{18,... | collective-permute-start | bytes 98312 | tf_op jit(solution)/shard_map/ppermute | solution.py:164
  149.5 2.0 %collective-permute-start.11 = (f32[64,128]{1,0:T(8,128)S(1)}, f32[64,128]{1,0:T(8,128)S(1)}, u32[]{:S(2)}, u32[]{:S(2)}) collective-permute-start(f32[64,128]{1,0:T(8,128)S(1)} %get-tuple-element.45), channel_id=1, source_target_pairs={{1,2},{3,4},{5,6},{7,8},{9,10},{11,12},{13,14},{15,16},{17,18},{19... | collective-permute-start | bytes 98312 | tf_op jit(solution)/shard_map/ppermute | solution.py:164
  151.5 0.0 collective-permute-done.10.near_in
  151.6 3.2 %collective-permute-done.11.far_in = f32[64,128]{1,0:T(8,128)S(1)} collective-permute-done((f32[64,128]{1,0:T(8,128)S(1)}, f32[64,128]{1,0:T(8,128)S(1)}, u32[]{:S(2)}, u32[]{:S(2)}) %collective-permute-start.11) | collective-permute-done | bytes 32800 | tf_op jit(solution)/shard_map/ppermute | solution.py:164
  154.7 0.0 collective-permute-done.8.slab_even
  154.7 0.0 collective-permute-done.9.slab_odd
  154.7 0.7 shard_map.84
  155.4 7.0 %collective-permute-start.12 = (f32[64,256]{1,0:T(8,128)S(1)}, f32[64,256]{1,0:T(8,128)S(1)}, u32[]{:S(2)}, u32[]{:S(2)}) collective-permute-start(f32[64,256]{1,0:T(8,128)S(1)} %get-tuple-element.46.resp), channel_id=1, source_target_pairs={{0,32},{64,96},{128,160},{192,224},{256,288},{320,352},{384,416},{... | collective-permute-start | bytes 196616 | tf_op jit(solution)/shard_map/ppermute | solution.py:164
  162.4 0.7 collective-permute-start.13
  163.1 3.9 %all-to-all-start.6 = ((f32[16,1,128]{2,1,0:T(1,128)}), f32[16,1,128]{2,1,0:T(1,128)S(1)}, u32[]{:S(2)}, u32[]{:S(2)}) async-start(f32[16,1,128]{2,1,0:T(1,128)} %get-tuple-element.41), calls=%async_computation.6 | async-start | bytes 16384 | tf_op jit(solution)/shard_map/all_to_all | solution.py:336
  166.9 2.0 %collective-permute-start.14 = (f32[64,128]{1,0:T(8,128)S(1)}, f32[64,128]{1,0:T(8,128)S(1)}, u32[]{:S(2)}, u32[]{:S(2)}) collective-permute-start(f32[64,128]{1,0:T(8,128)S(1)} %get-tuple-element.47), channel_id=1, source_target_pairs={{0,1},{2,3},{4,5},{6,7},{8,9},{10,11},{12,13},{14,15},{16,17},{18,... | collective-permute-start | bytes 98312 | tf_op jit(solution)/shard_map/ppermute | solution.py:164
  169.0 3.6 %collective-permute-start.15 = (f32[64,128]{1,0:T(8,128)S(1)}, f32[64,128]{1,0:T(8,128)S(1)}, u32[]{:S(2)}, u32[]{:S(2)}) collective-permute-start(f32[64,128]{1,0:T(8,128)S(1)} %get-tuple-element.48), channel_id=1, source_target_pairs={{1,2},{3,4},{5,6},{7,8},{9,10},{11,12},{13,14},{15,16},{17,18},{19... | collective-permute-start | bytes 98312 | tf_op jit(solution)/shard_map/ppermute | solution.py:164
  172.6 1.3 all-to-all-done.6
  173.9 0.6 broadcast_in_dim.2
  174.5 9.8 %all-to-all-start.7 = ((f32[32,1,128]{2,1,0:T(1,128)}), f32[32,1,128]{2,1,0:T(1,128)S(1)}, u32[]{:S(2)}, u32[]{:S(2)}) async-start(f32[32,1,128]{2,1,0:T(1,128)} %broadcast_in_dim.2), calls=%async_computation.7 | async-start | bytes 32768 | tf_op jit(solution)/shard_map/all_to_all | solution.py:336
  184.3 0.0 collective-permute-done.14.near_in
  184.3 0.0 collective-permute-done.15.far_in
  184.3 0.0 collective-permute-done.12.slab_even
  184.3 0.0 collective-permute-done.13.slab_odd
  184.4 1.3 shard_map.85
  185.7 7.3 %all-to-all-done.7 = f32[32,1,128]{2,1,0:T(1,128)S(1)} async-done(((f32[32,1,128]{2,1,0:T(1,128)}), f32[32,1,128]{2,1,0:T(1,128)S(1)}, u32[]{:S(2)}, u32[]{:S(2)}) %all-to-all-start.7) | async-done | bytes 16416 | tf_op jit(solution)/shard_map/all_to_all | solution.py:336
  192.9 0.1 reduce_sum.21
  193.0 0.7 fusion
  194.4 0.7 reshape.40
  (6 shorter events, 0.1 us)
Async XLA Ops:
  1.3 21.9 %copy-start.5 = (s32[2]{0:T(128)S(1)}, s32[2]{0:T(128)}, u32[]{:S(2)}) copy-start(s32[2]{0:T(128)} %pad_add_fusion.core.place) | copy-start | bytes 28
  6.3 16.8 %collective-permute-start = (f32[64,256]{1,0:T(8,128)}, f32[64,256]{1,0:T(8,128)S(1)}, u32[]{:S(2)}, u32[]{:S(2)}) collective-permute-start(f32[64,256]{1,0:T(8,128)} %get-tuple-element.29.resp), channel_id=1, source_target_pairs={{0,32},{64,96},{128,160},{192,224},{256,288},{320,352},{384,416},{... | collective-permute-start | bytes 196616 | tf_op jit(solution)/shard_map/ppermute | solution.py:164
  13.0 10.2 %collective-permute-start.1 = (f32[64,256]{1,0:T(8,128)}, f32[64,256]{1,0:T(8,128)S(1)}, u32[]{:S(2)}, u32[]{:S(2)}) collective-permute-start(f32[64,256]{1,0:T(8,128)} %get-tuple-element.29.resp), channel_id=1, source_target_pairs={{32,64},{96,128},{160,192},{224,256},{288,320},{352,384},{416,448}... | collective-permute-start | bytes 196616 | tf_op jit(solution)/shard_map/ppermute | solution.py:164
  13.7 6.0 %collective-permute-start.2 = (f32[64,128]{1,0:T(8,128)}, f32[64,128]{1,0:T(8,128)S(1)}, u32[]{:S(2)}, u32[]{:S(2)}) collective-permute-start(f32[64,128]{1,0:T(8,128)} %get-tuple-element.30), channel_id=1, source_target_pairs={{0,1},{2,3},{4,5},{6,7},{8,9},{10,11},{12,13},{14,15},{16,17},{18,... | collective-permute-start | bytes 98312 | tf_op jit(solution)/shard_map/ppermute | solution.py:164
  17.7 5.4 %collective-permute-start.3 = (f32[64,128]{1,0:T(8,128)}, f32[64,128]{1,0:T(8,128)S(1)}, u32[]{:S(2)}, u32[]{:S(2)}) collective-permute-start(f32[64,128]{1,0:T(8,128)} %get-tuple-element.31), channel_id=1, source_target_pairs={{1,2},{3,4},{5,6},{7,8},{9,10},{11,12},{13,14},{15,16},{17,18},{19... | collective-permute-start | bytes 98312 | tf_op jit(solution)/shard_map/ppermute | solution.py:164
  23.2 0.8 copy-start
  24.0 0.8 copy-start.1
  24.9 0.7 copy-start.2
  26.2 17.3 %collective-permute-start.4 = (f32[64,256]{1,0:T(8,128)S(1)}, f32[64,256]{1,0:T(8,128)S(1)}, u32[]{:S(2)}, u32[]{:S(2)}) collective-permute-start(f32[64,256]{1,0:T(8,128)S(1)} %get-tuple-element.33.resp), channel_id=1, source_target_pairs={{0,32},{64,96},{128,160},{192,224},{256,288},{320,352},{384,416},{... | collective-permute-start | bytes 196616 | tf_op jit(solution)/shard_map/ppermute | solution.py:164
  35.7 7.8 %collective-permute-start.5 = (f32[64,256]{1,0:T(8,128)S(1)}, f32[64,256]{1,0:T(8,128)S(1)}, u32[]{:S(2)}, u32[]{:S(2)}) collective-permute-start(f32[64,256]{1,0:T(8,128)S(1)} %get-tuple-element.33.resp), channel_id=1, source_target_pairs={{32,64},{96,128},{160,192},{224,256},{288,320},{352,384},{416,448}... | collective-permute-start | bytes 196616 | tf_op jit(solution)/shard_map/ppermute | solution.py:164
  36.4 5.5 %collective-permute-start.6 = (f32[64,128]{1,0:T(8,128)S(1)}, f32[64,128]{1,0:T(8,128)S(1)}, u32[]{:S(2)}, u32[]{:S(2)}) collective-permute-start(f32[64,128]{1,0:T(8,128)S(1)} %get-tuple-element.34), channel_id=1, source_target_pairs={{0,1},{2,3},{4,5},{6,7},{8,9},{10,11},{12,13},{14,15},{16,17},{18,... | collective-permute-start | bytes 98312 | tf_op jit(solution)/shard_map/ppermute | solution.py:164
  38.3 5.2 %collective-permute-start.7 = (f32[64,128]{1,0:T(8,128)S(1)}, f32[64,128]{1,0:T(8,128)S(1)}, u32[]{:S(2)}, u32[]{:S(2)}) collective-permute-start(f32[64,128]{1,0:T(8,128)S(1)} %get-tuple-element.35), channel_id=1, source_target_pairs={{1,2},{3,4},{5,6},{7,8},{9,10},{11,12},{13,14},{15,16},{17,18},{19... | collective-permute-start | bytes 98312 | tf_op jit(solution)/shard_map/ppermute | solution.py:164
  43.5 0.7 copy-start.3
  96.5 46.0 %copy-start.4 = (f32[1,256]{1,0:T(1,128)S(1)}, f32[1,256]{1,0:T(1,128)}, u32[]{:S(2)}) copy-start(f32[1,256]{1,0:T(1,128)} %get-tuple-element.32.mask) | copy-start | bytes 3076
  143.7 11.1 %collective-permute-start.8 = (f32[64,256]{1,0:T(8,128)S(1)}, f32[64,256]{1,0:T(8,128)S(1)}, u32[]{:S(2)}, u32[]{:S(2)}) collective-permute-start(f32[64,256]{1,0:T(8,128)S(1)} %get-tuple-element.43.resp), channel_id=1, source_target_pairs={{0,32},{64,96},{128,160},{192,224},{256,288},{320,352},{384,416},{... | collective-permute-start | bytes 196616 | tf_op jit(solution)/shard_map/ppermute | solution.py:164
  145.8 8.9 %collective-permute-start.9 = (f32[64,256]{1,0:T(8,128)S(1)}, f32[64,256]{1,0:T(8,128)S(1)}, u32[]{:S(2)}, u32[]{:S(2)}) collective-permute-start(f32[64,256]{1,0:T(8,128)S(1)} %get-tuple-element.43.resp), channel_id=1, source_target_pairs={{32,64},{96,128},{160,192},{224,256},{288,320},{352,384},{416,448}... | collective-permute-start | bytes 196616 | tf_op jit(solution)/shard_map/ppermute | solution.py:164
  146.5 5.1 %collective-permute-start.10 = (f32[64,128]{1,0:T(8,128)S(1)}, f32[64,128]{1,0:T(8,128)S(1)}, u32[]{:S(2)}, u32[]{:S(2)}) collective-permute-start(f32[64,128]{1,0:T(8,128)S(1)} %get-tuple-element.44), channel_id=1, source_target_pairs={{0,1},{2,3},{4,5},{6,7},{8,9},{10,11},{12,13},{14,15},{16,17},{18,... | collective-permute-start | bytes 98312 | tf_op jit(solution)/shard_map/ppermute | solution.py:164
  149.5 5.2 %collective-permute-start.11 = (f32[64,128]{1,0:T(8,128)S(1)}, f32[64,128]{1,0:T(8,128)S(1)}, u32[]{:S(2)}, u32[]{:S(2)}) collective-permute-start(f32[64,128]{1,0:T(8,128)S(1)} %get-tuple-element.45), channel_id=1, source_target_pairs={{1,2},{3,4},{5,6},{7,8},{9,10},{11,12},{13,14},{15,16},{17,18},{19... | collective-permute-start | bytes 98312 | tf_op jit(solution)/shard_map/ppermute | solution.py:164
  155.4 28.9 %collective-permute-start.12 = (f32[64,256]{1,0:T(8,128)S(1)}, f32[64,256]{1,0:T(8,128)S(1)}, u32[]{:S(2)}, u32[]{:S(2)}) collective-permute-start(f32[64,256]{1,0:T(8,128)S(1)} %get-tuple-element.46.resp), channel_id=1, source_target_pairs={{0,32},{64,96},{128,160},{192,224},{256,288},{320,352},{384,416},{... | collective-permute-start | bytes 196616 | tf_op jit(solution)/shard_map/ppermute | solution.py:164
  162.4 21.9 %collective-permute-start.13 = (f32[64,256]{1,0:T(8,128)S(1)}, f32[64,256]{1,0:T(8,128)S(1)}, u32[]{:S(2)}, u32[]{:S(2)}) collective-permute-start(f32[64,256]{1,0:T(8,128)S(1)} %get-tuple-element.46.resp), channel_id=1, source_target_pairs={{32,64},{96,128},{160,192},{224,256},{288,320},{352,384},{416,448}... | collective-permute-start | bytes 196616 | tf_op jit(solution)/shard_map/ppermute | solution.py:164
  163.1 10.8 %all-to-all-start.6 = ((f32[16,1,128]{2,1,0:T(1,128)}), f32[16,1,128]{2,1,0:T(1,128)S(1)}, u32[]{:S(2)}, u32[]{:S(2)}) async-start(f32[16,1,128]{2,1,0:T(1,128)} %get-tuple-element.41), calls=%async_computation.6 | async-start | bytes 16384 | tf_op jit(solution)/shard_map/all_to_all | solution.py:336
  166.9 17.4 %collective-permute-start.14 = (f32[64,128]{1,0:T(8,128)S(1)}, f32[64,128]{1,0:T(8,128)S(1)}, u32[]{:S(2)}, u32[]{:S(2)}) collective-permute-start(f32[64,128]{1,0:T(8,128)S(1)} %get-tuple-element.47), channel_id=1, source_target_pairs={{0,1},{2,3},{4,5},{6,7},{8,9},{10,11},{12,13},{14,15},{16,17},{18,... | collective-permute-start | bytes 98312 | tf_op jit(solution)/shard_map/ppermute | solution.py:164
  169.0 15.4 %collective-permute-start.15 = (f32[64,128]{1,0:T(8,128)S(1)}, f32[64,128]{1,0:T(8,128)S(1)}, u32[]{:S(2)}, u32[]{:S(2)}) collective-permute-start(f32[64,128]{1,0:T(8,128)S(1)} %get-tuple-element.48), channel_id=1, source_target_pairs={{1,2},{3,4},{5,6},{7,8},{9,10},{11,12},{13,14},{15,16},{17,18},{19... | collective-permute-start | bytes 98312 | tf_op jit(solution)/shard_map/ppermute | solution.py:164
  174.5 18.4 %all-to-all-start.7 = ((f32[32,1,128]{2,1,0:T(1,128)}), f32[32,1,128]{2,1,0:T(1,128)S(1)}, u32[]{:S(2)}, u32[]{:S(2)}) async-start(f32[32,1,128]{2,1,0:T(1,128)} %broadcast_in_dim.2), calls=%async_computation.7 | async-start | bytes 32768 | tf_op jit(solution)/shard_map/all_to_all | solution.py:336

commit v3 on v2

--- a/solution.py
+++ b/solution.py
@@ -19,6 +19,7 @@
 
 WIDTH = 128
 CELLS = 256
+DEVICES = 512
 HALF = 64
 PACKET = HALF + 8
 VMEM = pl.BlockSpec(memory_space=pltpu.VMEM)
@@ -56,6 +57,13 @@
     return expon / jnp.sum(expon, axis=0, keepdims=True)
 
 
+def keep(scores, resp, mask, state):
+    count = scores.shape[0]
+    state[:count] = scores
+    state[count : 2 * count] = resp
+    state[2 * count :] = jnp.broadcast_to(mask, (state.shape[0] - 2 * count, CELLS))
+
+
 def put(core, resp, resp_ref, near_ref, far_ref):
     first, last = resp[:, :WIDTH], resp[:, WIDTH:]
     resp_ref[...] = resp
@@ -68,7 +76,7 @@
 
 def start_kernel(
     core, weights, flat, tissue, means, whiten,
-    scores, resp, near, far, spread, mask,
+    state, resp, near, far, spread,
     weights_in, flat_in, tissue_in, means_in, whiten_in, diag, sems,
 ):
     count = whiten.shape[0]
@@ -99,7 +107,7 @@
             full = matrix.astype(jnp.float32)
             shift = jnp.sum(full * means_in[own : own + 1], axis=1, keepdims=True)
             proj = matmul(matrix, cells) - shift
-            scores[own : own + 1] = jnp.sum(proj * proj, axis=0, keepdims=True)
+            state[own : own + 1] = jnp.sum(proj * proj, axis=0, keepdims=True)
             diag[own : own + 1] = jnp.sum(
                 jnp.where(row_at == col_at, full, 0.0), axis=0, keepdims=True
             )
@@ -110,19 +118,19 @@
     offset = jnp.sum(prior, axis=1, keepdims=True) + jnp.sum(
         jnp.log(diag[...]), axis=1, keepdims=True
     )
-    result = offset - 0.5 * scores[...]
-    scores[...] = result
+    result = offset - 0.5 * state[:count]
     tissue_f = tissue_in[...].astype(jnp.float32)
     tissue_f = jnp.concatenate([tissue_f[:1], tissue_f[1:]], axis=1)
-    mask[...] = tissue_f
-    put(core[0], normalise(result) * tissue_f, resp, near, far)
+    first = normalise(result) * tissue_f
+    keep(result, first, tissue_f, state)
+    put(core[0], first, resp, near, far)
 
 
 def start(core, weights, flat, tissue, means, whiten):
     count = whiten.shape[0]
     f32 = jnp.float32
-    shapes = [(count, CELLS), (count, CELLS), (count, WIDTH), (count, WIDTH)]
-    shapes += [(8, CELLS, WIDTH), (1, CELLS)]
+    shapes = [(2 * count + 8, CELLS), (count, CELLS), (count, WIDTH), (count, WIDTH)]
+    shapes += [(4, CELLS, WIDTH)]
     return pl.pallas_call(
         start_kernel,
         out_shape=[jax.ShapeDtypeStruct(shape, f32) for shape in shapes],
@@ -142,10 +150,9 @@
     )(core, weights, flat, tissue, means, whiten)
 
 
-def sweep_kernel(
-    core, scores, resp, slab_even, slab_odd, near_in, far_in, mask, out, near, far
-):
-    lane = iotas((resp.shape[0], WIDTH))[1]
+def swept(core, state, resp, slab_even, slab_odd, near_in, far_in):
+    count = resp.shape[0]
+    lane = iotas((count, WIDTH))[1]
     rows = (resp[:, :WIDTH], resp[:, WIDTH:])
     below = jnp.where(core[0] == 0, far_in[...], near_in[...])
     above = jnp.where(core[0] == 0, near_in[...], far_in[...])
@@ -155,7 +162,32 @@
         before = jnp.where(lane > 0, pltpu.roll(row, 1, 1), 0.0)
         fields.append(others + after + before)
     field = jnp.concatenate(fields, axis=1) + slab_even[...] + slab_odd[...]
-    put(core[0], normalise(scores[...] + BETA_POTTS * field) * mask[...], out, near, far)
+    scores, mask = state[:count], state[2 * count : 2 * count + 1]
+    return normalise(scores + BETA_POTTS * field) * mask
+
+
+def first_kernel(core, state, slab_even, slab_odd, near_in, far_in, out, near, far):
+    count = out.shape[0]
+    resp = state[count : 2 * count]
+    put(core[0], swept(core, state, resp, slab_even, slab_odd, near_in, far_in), out, near, far)
+
+
+def later_kernel(core, state, resp, slab_even, slab_odd, near_in, far_in, out):
+    out[...] = swept(core, state, resp[...], slab_even, slab_odd, near_in, far_in)
+
+
+def last_kernel(core, state, resp, slab_even, slab_odd, near_in, far_in, totals, out, score):
+    result = swept(core, state, resp[...], slab_even, slab_odd, near_in, far_in)
+    out[:, 0, :] = result[:, :WIDTH]
+    out[:, 1, :] = result[:, WIDTH:]
+    total = totals[0]
+    for n in range(1, totals.shape[0]):
+        total = total + totals[n]
+    lane = iotas((1, WIDTH))[1]
+    lse = jnp.sum(jnp.where(lane == 0, total, 0.0))
+    level = jnp.sum(jnp.where(lane == 2, jnp.log(total), 0.0))
+    cells = jnp.sum(jnp.where(lane == 1, total, 0.0))
+    score[0, 0] = (lse - cells * level) / (CELLS * DEVICES)
 
 
 def swapped(part, axes, begin):
@@ -164,29 +196,26 @@
     return lax.ppermute(part, axes, pairs + [(j, i) for i, j in pairs])
 
 
-def sweep(core, scores, resp, near, far, mask):
-    f32 = jnp.float32
-    count = resp.shape[0]
-    return call(
-        sweep_kernel,
-        [((count, CELLS), f32), ((count, WIDTH), f32), ((count, WIDTH), f32)],
-        core, scores, resp, swapped(resp, SLAB, 0), swapped(resp, SLAB, 1),
-        swapped(near, TILE, 0), swapped(far, TILE, 1), mask, scalars=1,
-    )
-
-
-def moments_kernel(resp, shared, packet, turned, total):
+def halos(resp, near, far):
+    return (
+        swapped(resp, SLAB, 0), swapped(resp, SLAB, 1), swapped(near, TILE, 0), swapped(far, TILE, 1)
+    )
+
+
+def moments_kernel(core, resp, mine, theirs, packet, turned, total):
     blocks, count = resp.shape[:2]
     row_at, col_at = iotas((WIDTH, WIDTH))
     ones = jnp.ones((CELLS, WIDTH), jnp.bfloat16)
     acc = [jnp.zeros((WIDTH, 2 * WIDTH), jnp.float32) for _ in range(count)]
-    for block in range(blocks):
-        cells = shared[block]
+    for n in range(blocks):
+        cells = mine[n // 2] if n % 2 == 0 else theirs[n // 2]
+        block = n + core[0] if n % 2 == 0 else n - core[0]
+        weight = resp[block]
         flipped = cells.T
         turned[block] = flipped.astype(jnp.bfloat16)
         wide = jnp.concatenate([cells.astype(jnp.bfloat16), ones], axis=1)
         for k in range(count):
-            weighted = (flipped * resp[block, k : k + 1, :]).astype(jnp.bfloat16)
+            weighted = (flipped * weight[k : k + 1]).astype(jnp.bfloat16)
             acc[k] = acc[k] + matmul(weighted, wide)
     firsts = jnp.zeros((WIDTH, WIDTH), jnp.float32)
     for k in range(count):
@@ -312,18 +341,19 @@
             scores[block, k : k + 1, CELLS:] = centre
 
 
-def likely_kernel(place, part, mask, total, scores, resp, near, far, means, totals):
+def likely_kernel(core, tile, part, mask, total, state, resp, near, far, means, totals):
     values = part[:, :CELLS]
-    scores[...] = values
     row = iotas((part.shape[0], WIDTH))[0]
     for n in range(2):
-        own = jnp.where(row == 2 * place[1] + n, part[:, CELLS:], 0.0)
+        own = jnp.where(row == 2 * tile[0] + n, part[:, CELLS:], 0.0)
         means[n : n + 1] = jnp.sum(own, axis=0, keepdims=True)
-    tissue_f = mask[...]
+    tissue_f = mask[2 * part.shape[0] : 2 * part.shape[0] + 1]
     top = jnp.max(values, axis=0, keepdims=True)
     expon = jnp.exp(values - top)
     weight = jnp.sum(expon, axis=0, keepdims=True)
-    put(place[0], expon / weight * tissue_f, resp, near, far)
+    first = expon / weight * tissue_f
+    keep(values, first, tissue_f, state)
+    put(core[0], first, resp, near, far)
     lse = jnp.sum((top + jnp.log(weight)) * tissue_f, axis=1, keepdims=True)
     cells = jnp.sum(tissue_f, axis=1, keepdims=True)
     lane = iotas((1, WIDTH))[1]
@@ -340,21 +370,30 @@
     count = whiten0.shape[0]
     f32 = jnp.float32
     flat = embed.reshape(CELLS, WIDTH)
-    place = jnp.stack([lax.axis_index("core"), lax.axis_index(TILE)])
+    core = lax.axis_index("core").reshape(1)
+    tile = lax.axis_index(TILE).reshape(1)
     resp_shapes = [((count, CELLS), f32), ((count, WIDTH), f32), ((count, WIDTH), f32)]
-
-    scores, resp, near, far, spread, mask = start(
-        place, weights0.reshape(1, count), flat, tissue.reshape(2, WIDTH), means0, whiten0
-    )
-    shared = swap_all(spread, BRICK)
-    for _ in range(SWEEPS):
-        resp, near, far = sweep(place, scores, resp, near, far, mask)
+    state_shape = ((2 * count + 8, CELLS), f32)
+
+    before, resp, near, far, spread = start(
+        core, weights0.reshape(1, count), flat, tissue.reshape(2, WIDTH), means0, whiten0
+    )
+    mine = swap_all(spread, BRICK[:2])
+    resp, near, far = call(
+        first_kernel, resp_shapes, core, before, *halos(resp, near, far), scalars=1
+    )
+    resp, near, far, mine = lax.optimization_barrier((resp, near, far, mine))
+    theirs = lax.ppermute(mine, "core", [(0, 1), (1, 0)])
+    (resp,) = call(
+        later_kernel, resp_shapes[:1], core, before, resp, *halos(resp, near, far), scalars=1
+    )
+    resp, theirs = lax.optimization_barrier((resp, theirs))
 
     part = swap_all(resp.reshape(8, 8, CELLS), BRICK)
     packets, turned, total = call(
         moments_kernel,
         [((8, PACKET, WIDTH), f32), ((8, WIDTH, CELLS), jnp.bfloat16), ((1, WIDTH), f32)],
-        part, shared, flops=1 << 30,
+        core, part, mine, theirs, scalars=1, flops=1 << 30,
     )
     (packets,) = call(gather_kernel, [((8, PACKET, WIDTH), f32)], swap_all(packets, NEAR))
     packets = swap_all(packets, FAR)
@@ -366,20 +405,29 @@
     part = swap_all(part, BRICK).reshape(count, CELLS + WIDTH)
 
     sizes = [lax.axis_size(axes) for axes in ROUND]
-    scores, resp, near, far, means_out, totals = call(
+    state, resp, near, far, means_out, totals = call(
         likely_kernel,
-        [((count, CELLS), f32)] + resp_shapes + [((2, WIDTH), f32), ((sizes[0], 1, WIDTH), f32)],
-        place, part, mask, total, scalars=1,
-    )
-    totals = jnp.sum(swap_all(totals, ROUND[0]), axis=0)
-    totals = swap_all(jnp.broadcast_to(totals[None], (sizes[1], 1, WIDTH)), ROUND[1])
-    for _ in range(SWEEPS):
-        resp, near, far = sweep(place, scores, resp, near, far, mask)
-    totals, resp = lax.optimization_barrier((totals, resp))
-    totals = jnp.sum(totals, axis=0)
-    bins = CELLS * sizes[0] * sizes[1]
-    score = (totals[0, 0] - totals[0, 1] * jnp.log(totals[0, 2])) / bins
-    return (resp.reshape(count, 1, 2, WIDTH), means_out, score)
+        [state_shape] + resp_shapes + [((2, WIDTH), f32), ((sizes[0], 1, WIDTH), f32)],
+        core, tile, part, before, total, scalars=2,
+    )
+    totals = swap_all(totals, ROUND[0])
+    resp, near, far = call(
+        first_kernel, resp_shapes, core, state, *halos(resp, near, far), scalars=1
+    )
+    totals, resp, near, far = lax.optimization_barrier((totals, resp, near, far))
+    totals = jnp.broadcast_to(jnp.sum(totals, axis=0)[None], (sizes[1], 1, WIDTH))
+    totals = swap_all(totals, ROUND[1])
+    sides = halos(resp, near, far)
+    resp_final, score = pl.pallas_call(
+        last_kernel,
+        out_shape=[
+            jax.ShapeDtypeStruct((count, 2, WIDTH), f32), jax.ShapeDtypeStruct((1, 1), f32)
+        ],
+        in_specs=[SMEM] + [VMEM] * 7,
+        out_specs=[VMEM, SMEM],
+        compiler_params=PARAMS,
+    )(core, state, resp, *sides, totals)
+    return (resp_final.reshape(count, 1, 2, WIDTH), means_out, score.reshape(()))
 
 
 def solution(mesh):

time: 199 us -> 179 us (0.90)
  blocking collectives: 89.8 us -> 69.5 us
  starting transfers between devices: 63.6 us -> 74.1 us
  Pallas kernels: 17.3 us -> 13.8 us
  local copies, waits for them, and re-layouts: 4.98 us -> 1.83 us
  between operations: 4.06 us -> 0.91 us
    all_to_all x6 -> x5, blocking collectives: 89.8 us -> 69.5 us  [swap_all(): return lax.all_to_all(value, axes, 0, 0, tiled=True)]
    ppermute x16, starting transfers between devices: 50 us -> 55.1 us  [swapped(): return lax.ppermute(part, axes, pairs + [(j, i) for i, j in pairs])]
    all_to_all x2 -> x3, starting transfers between devices: 13.6 us -> 17.1 us  [swap_all(): return lax.all_to_all(value, axes, 0, 0, tiled=True)]
    pallas_call x9 -> x8, Pallas kernels: 12.3 us -> 8.84 us  [call(): pl.pallas_call(kernel, out_shape=out, in_specs=[SMEM] * scalars + [VMEM]...]
    all_to_all x2 -> x3, waiting for transfers between devices: 8.62 us -> 11.7 us  [swap_all(): return lax.all_to_all(value, axes, 0, 0, tiled=True)]
    ppermute x16, waiting for transfers between devices: 8.34 us -> 5.55 us  [swapped(): return lax.ppermute(part, axes, pairs + [(j, i) for i, j in pairs])]
  transfers between devices with their start and end apart: 18 -> 20, of which waited for: 5 -> 4; matrix products, arithmetic and copies ran while one was open for 0% -> 0% of each run, Pallas kernels for 1% -> 0%
where the time goes in v3:
time: 179 us; the launch traced here: 178 us
  starting transfers between devices  74.1 us (41%)
  blocking collectives  69.5 us (39%)
  waiting for transfers between devices  17.3 us (10%)
  Pallas kernels  13.8 us (8%)
  local copies, waits for them, and re-layouts  1.83 us (1%)
    all_to_all x5, blocking collectives, swap_all(): return lax.all_to_all(value, axes, 0, 0, tiled=True)  69.5 us
    ppermute x16, starting transfers between devices, swapped(): return lax.ppermute(part, axes, pairs + [(j, i) for i, j in pairs])  55.1 us
    all_to_all x3, starting transfers between devices, swap_all(): return lax.all_to_all(value, axes, 0, 0, tiled=True)  17.1 us
    all_to_all x3, waiting for transfers between devices, swap_all(): return lax.all_to_all(value, axes, 0, 0, tiled=True)  11.7 us
    pallas_call x8, Pallas kernels, call(): pl.pallas_call(kernel, out_shape=out, in_specs=[SMEM] * scalars + [VMEM]...  8.84 us
    ppermute x16, waiting for transfers between devices, swapped(): return lax.ppermute(part, axes, pairs + [(j, i) for i, j in pairs])  5.55 us
    pallas_call x1, Pallas kernels, start(): pl.pallas_call(start_kernel, out_shape=[jax.ShapeDtypeStruct(shape, f32)...  4.12 us
  transfers between devices with their start and end apart: 20, of which 4 were waited for; matrix products, arithmetic and copies ran while one was open for 0% of the time, Pallas kernels for 0%

profile of v3, /device:TPU:1, one launch (start us, length us, event | category | flops | bytes accessed | tf_op | source)
XLA Modules:
  0.0 177.5 jit_solution(8676345168372378529)
XLA Ops:
  0.6 4.1 %shard_map.76 = (f32[136,256]{1,0:T(8,128)}, f32[64,256]{1,0:T(8,128)}, f32[64,128]{1,0:T(8,128)}, f32[64,128]{1,0:T(8,128)}, f32[4,256,128]{2,1,0:T(8,128)}) custom-call(s32[1]{0:T(128)} %bitcast.core, f32[1,64]{1,0:T(1,128)} %bitcast.15, bf16[256,128]{1,0:T(8,128)(2,1)} %bitcast.13, s32[2,128]{1,0:T(2,128)} %bitcast.14, f32[64,128]{1,0:T(8,128)} %means.1, ...), custom_call_target="tpu_custom_call" | custom-call | flops 536870912 | bytes 2097152 | tf_op jit(solution)/shard_map/pallas_call | solution.py:134
  4.8 4.9 %all-to-all-start = ((f32[4,256,128]{2,1,0:T(8,128)}), f32[4,256,128]{2,1,0:T(8,128)S(1)}, u32[]{:S(2)}, u32[]{:S(2)}) async-start(f32[4,256,128]{2,1,0:T(8,128)} %get-tuple-element.42), calls=%async_computation | async-start | bytes 1048576 | tf_op jit(solution)/shard_map/all_to_all | solution.py:366
  9.6 0.7 collective-permute-start.1
  10.3 12.2 %collective-permute-start = (f32[64,256]{1,0:T(8,128)}, f32[64,256]{1,0:T(8,128)S(1)}, u32[]{:S(2)}, u32[]{:S(2)}) collective-permute-start(f32[64,256]{1,0:T(8,128)} %get-tuple-element.36), channel_id=1, source_target_pairs={{0,32},{64,96},{128,160},{192,224},{256,288},{320,352},{384,416},{... | collective-permute-start | bytes 196616 | tf_op jit(solution)/shard_map/ppermute | solution.py:196
  22.5 3.4 %collective-permute-start.2 = (f32[64,128]{1,0:T(8,128)}, f32[64,128]{1,0:T(8,128)S(1)}, u32[]{:S(2)}, u32[]{:S(2)}) collective-permute-start(f32[64,128]{1,0:T(8,128)} %get-tuple-element.37), channel_id=1, source_target_pairs={{0,1},{2,3},{4,5},{6,7},{8,9},{10,11},{12,13},{14,15},{16,17},{18,... | collective-permute-start | bytes 98312 | tf_op jit(solution)/shard_map/ppermute | solution.py:196
  25.9 3.1 %collective-permute-start.3 = (f32[64,128]{1,0:T(8,128)}, f32[64,128]{1,0:T(8,128)S(1)}, u32[]{:S(2)}, u32[]{:S(2)}) collective-permute-start(f32[64,128]{1,0:T(8,128)} %get-tuple-element.38), channel_id=1, source_target_pairs={{1,2},{3,4},{5,6},{7,8},{9,10},{11,12},{13,14},{15,16},{17,18},{19... | collective-permute-start | bytes 98312 | tf_op jit(solution)/shard_map/ppermute | solution.py:196
  29.0 0.0 collective-permute-done.2.near_in
  29.0 2.3 %collective-permute-done.3.far_in = f32[64,128]{1,0:T(8,128)S(1)} collective-permute-done((f32[64,128]{1,0:T(8,128)}, f32[64,128]{1,0:T(8,128)S(1)}, u32[]{:S(2)}, u32[]{:S(2)}) %collective-permute-start.3) | collective-permute-done | bytes 32800 | tf_op jit(solution)/shard_map/ppermute | solution.py:196
  31.3 0.0 collective-permute-done.1.slab_odd
  31.3 0.0 collective-permute-done.slab_even
  31.3 0.0 copy-start
  31.3 0.9 copy-done
  32.2 0.1 shard_map.77
  32.4 0.0 all-to-all-done.mine
  32.4 1.9 %collective-permute-start.8 = (f32[4,256,128]{2,1,0:T(8,128)S(1)}, f32[4,256,128]{2,1,0:T(8,128)S(1)}, u32[]{:S(2)}, u32[]{:S(2)}) collective-permute-start(f32[4,256,128]{2,1,0:T(8,128)S(1)} %all-to-all-done.mine), channel_id=1, source_target_pairs={{0,1},{1,0},{2,3},{3,2},{4,5},{5,4},{6,7},{7,6},{8,9},{9,8},{10,11... | collective-permute-start | bytes 1572872 | tf_op jit(solution)/shard_map/ppermute | solution.py:386
  34.3 0.7 collective-permute-start.5
  35.0 6.1 %collective-permute-start.4 = (f32[64,256]{1,0:T(8,128)S(1)}, f32[64,256]{1,0:T(8,128)S(1)}, u32[]{:S(2)}, u32[]{:S(2)}) collective-permute-start(f32[64,256]{1,0:T(8,128)S(1)} %get-tuple-element.43.resp), channel_id=1, source_target_pairs={{0,32},{64,96},{128,160},{192,224},{256,288},{320,352},{384,416},{... | collective-permute-start | bytes 196616 | tf_op jit(solution)/shard_map/ppermute | solution.py:196
  41.1 3.0 %collective-permute-start.6 = (f32[64,128]{1,0:T(8,128)S(1)}, f32[64,128]{1,0:T(8,128)S(1)}, u32[]{:S(2)}, u32[]{:S(2)}) collective-permute-start(f32[64,128]{1,0:T(8,128)S(1)} %get-tuple-element.44), channel_id=1, source_target_pairs={{0,1},{2,3},{4,5},{6,7},{8,9},{10,11},{12,13},{14,15},{16,17},{18,... | collective-permute-start | bytes 98312 | tf_op jit(solution)/shard_map/ppermute | solution.py:196
  44.0 2.0 %collective-permute-start.7 = (f32[64,128]{1,0:T(8,128)S(1)}, f32[64,128]{1,0:T(8,128)S(1)}, u32[]{:S(2)}, u32[]{:S(2)}) collective-permute-start(f32[64,128]{1,0:T(8,128)S(1)} %get-tuple-element.45), channel_id=1, source_target_pairs={{1,2},{3,4},{5,6},{7,8},{9,10},{11,12},{13,14},{15,16},{17,18},{19... | collective-permute-start | bytes 98312 | tf_op jit(solution)/shard_map/ppermute | solution.py:196
  46.1 0.0 collective-permute-done.6.near_in
  46.1 3.2 %collective-permute-done.7.far_in = f32[64,128]{1,0:T(8,128)S(1)} collective-permute-done((f32[64,128]{1,0:T(8,128)S(1)}, f32[64,128]{1,0:T(8,128)S(1)}, u32[]{:S(2)}, u32[]{:S(2)}) %collective-permute-start.7) | collective-permute-done | bytes 32800 | tf_op jit(solution)/shard_map/ppermute | solution.py:196
  49.3 0.0 collective-permute-done.5.slab_odd
  49.3 0.0 collective-permute-done.4.slab_even
  49.3 0.0 copy-start.1
  49.3 0.9 copy-done.1
  50.2 0.1 shard_map.78
  50.3 0.0 collective-permute-done.8.theirs
  50.4 8.7 %all_to_all.40.resp = f32[8,8,256]{2,1,0:T(8,128)S(1)} all-to-all(f32[8,8,256]{2,1,0:T(8,128)S(1)} %bitcast.12), channel_id=1, replica_groups=mesh['x1'=2,'x0'=2,'z2'=2,'z1'=2,'z0'=2,'y2'=2,'y1'=2,'y0'=2,'core'=2] {..., dimensions={0} | all-to-all | bytes 131072 | tf_op jit(solution)/shard_map/all_to_all | solution.py:366
  59.1 1.6 shard_map.79
  60.6 19.1 %all_to_all.41.packets = f32[8,72,128]{2,1,0:T(8,128)S(1)} all-to-all(f32[8,72,128]{2,1,0:T(8,128)S(1)} %get-tuple-element.49), channel_id=1, replica_groups=mesh['x1'=2,'x0'=2,'z2'=2,'z1'=2,'z0'=2,'y2'=2,'y1'=2,'y0'=2,'core'=2] {..., dimensions={0} | all-to-all | bytes 589824 | tf_op jit(solution)/shard_map/all_to_all | solution.py:366
  79.8 0.0 copy-start.2
  79.8 15.2 %all_to_all.42.packets = f32[8,72,128]{2,1,0:T(8,128)S(1)} all-to-all(f32[8,72,128]{2,1,0:T(8,128)S(1)} %shard_map.80), channel_id=1, replica_groups=mesh['x1'=2,'x0'=2,'z2'=2,'z1'=2,'z0'=2,'y2'=2,'y1'=2,'y0'=2,'core'=2] {..., dimensions={0} | all-to-all | bytes 589824 | tf_op jit(solution)/shard_map/all_to_all | solution.py:366
  94.9 3.8 %shard_map.81 = f32[8,72,128]{2,1,0:T(8,128)S(1)} custom-call(f32[8,72,128]{2,1,0:T(8,128)S(1)} %all_to_all.42.packets), custom_call_target="tpu_custom_call" | custom-call | flops 134217728 | bytes 1048576 | tf_op jit(solution)/shard_map/pallas_call | solution.py:33
  98.8 13.6 %all_to_all.43.packets = f32[8,72,128]{2,1,0:T(8,128)S(1)} all-to-all(f32[8,72,128]{2,1,0:T(8,128)S(1)} %shard_map.81), channel_id=1, replica_groups=mesh['x1'=2,'x0'=2,'z2'=2,'z1'=2,'z0'=2,'y2'=2,'y1'=2,'y0'=2,'core'=2] {..., dimensions={0} | all-to-all | bytes 589824 | tf_op jit(solution)/shard_map/all_to_all | solution.py:366
  112.4 2.3 %shard_map.82 = f32[8,8,384]{2,1,0:T(8,128)} custom-call(f32[8,72,128]{2,1,0:T(8,128)S(1)} %all_to_all.43.packets, bf16[8,128,256]{2,1,0:T(8,128)(2,1)S(1)} %get-tuple-element.50.turned), custom_call_target="tpu_custom_call" | custom-call | flops 536870912 | bytes 1048576 | tf_op jit(solution)/shard_map/pallas_call | solution.py:33
  114.6 7.7 %all-to-all-start.5 = ((f32[8,8,384]{2,1,0:T(8,128)}), f32[8,8,384]{2,1,0:T(8,128)S(1)}, u32[]{:S(2)}, u32[]{:S(2)}) async-start(f32[8,8,384]{2,1,0:T(8,128)} %shard_map.82), calls=%async_computation.5 | async-start | bytes 196608 | tf_op jit(solution)/shard_map/all_to_all | solution.py:366
  122.3 5.0 %all-to-all-done.5 = f32[8,8,384]{2,1,0:T(8,128)S(1)} async-done(((f32[8,8,384]{2,1,0:T(8,128)}), f32[8,8,384]{2,1,0:T(8,128)S(1)}, u32[]{:S(2)}, u32[]{:S(2)}) %all-to-all-start.5) | async-done | bytes 98336 | tf_op jit(solution)/shard_map/all_to_all | solution.py:366
  127.3 0.0 copy-done.2
  127.3 0.7 shard_map.83
  128.1 0.7 collective-permute-start.10
  128.7 4.7 %collective-permute-start.9 = (f32[64,256]{1,0:T(8,128)S(1)}, f32[64,256]{1,0:T(8,128)S(1)}, u32[]{:S(2)}, u32[]{:S(2)}) collective-permute-start(f32[64,256]{1,0:T(8,128)S(1)} %get-tuple-element.54), channel_id=1, source_target_pairs={{0,32},{64,96},{128,160},{192,224},{256,288},{320,352},{384,416},{... | collective-permute-start | bytes 196616 | tf_op jit(solution)/shard_map/ppermute | solution.py:196
  133.4 3.3 %collective-permute-start.11 = (f32[64,128]{1,0:T(8,128)S(1)}, f32[64,128]{1,0:T(8,128)S(1)}, u32[]{:S(2)}, u32[]{:S(2)}) collective-permute-start(f32[64,128]{1,0:T(8,128)S(1)} %get-tuple-element.55), channel_id=1, source_target_pairs={{0,1},{2,3},{4,5},{6,7},{8,9},{10,11},{12,13},{14,15},{16,17},{18,... | collective-permute-start | bytes 98312 | tf_op jit(solution)/shard_map/ppermute | solution.py:196
  136.7 2.1 %collective-permute-start.12 = (f32[64,128]{1,0:T(8,128)S(1)}, f32[64,128]{1,0:T(8,128)S(1)}, u32[]{:S(2)}, u32[]{:S(2)}) collective-permute-start(f32[64,128]{1,0:T(8,128)S(1)} %get-tuple-element.56), channel_id=1, source_target_pairs={{1,2},{3,4},{5,6},{7,8},{9,10},{11,12},{13,14},{15,16},{17,18},{19... | collective-permute-start | bytes 98312 | tf_op jit(solution)/shard_map/ppermute | solution.py:196
  138.8 4.6 %all-to-all-start.6 = ((f32[16,1,128]{2,1,0:T(1,128)}), f32[16,1,128]{2,1,0:T(1,128)S(1)}, u32[]{:S(2)}, u32[]{:S(2)}) async-start(f32[16,1,128]{2,1,0:T(1,128)} %get-tuple-element.53), calls=%async_computation.6 | async-start | bytes 16384 | tf_op jit(solution)/shard_map/all_to_all | solution.py:366
  143.4 0.0 collective-permute-done.11.near_in
  143.4 0.0 collective-permute-done.12.far_in
  143.4 0.0 collective-permute-done.10.slab_odd
  143.4 0.0 collective-permute-done.9.slab_even
  143.4 0.2 shard_map.84
  143.6 6.7 %all-to-all-done.6 = f32[16,1,128]{2,1,0:T(1,128)S(1)} async-done(((f32[16,1,128]{2,1,0:T(1,128)}), f32[16,1,128]{2,1,0:T(1,128)S(1)}, u32[]{:S(2)}, u32[]{:S(2)}) %all-to-all-start.6) | async-done | bytes 8224 | tf_op jit(solution)/shard_map/all_to_all | solution.py:366
  150.3 0.7 collective-permute-start.14
  151.0 7.5 %collective-permute-start.13 = (f32[64,256]{1,0:T(8,128)S(1)}, f32[64,256]{1,0:T(8,128)S(1)}, u32[]{:S(2)}, u32[]{:S(2)}) collective-permute-start(f32[64,256]{1,0:T(8,128)S(1)} %get-tuple-element.60.resp), channel_id=1, source_target_pairs={{0,32},{64,96},{128,160},{192,224},{256,288},{320,352},{384,416},{... | collective-permute-start | bytes 196616 | tf_op jit(solution)/shard_map/ppermute | solution.py:196
  158.5 3.1 %collective-permute-start.15 = (f32[64,128]{1,0:T(8,128)S(1)}, f32[64,128]{1,0:T(8,128)S(1)}, u32[]{:S(2)}, u32[]{:S(2)}) collective-permute-start(f32[64,128]{1,0:T(8,128)S(1)} %get-tuple-element.61), channel_id=1, source_target_pairs={{0,1},{2,3},{4,5},{6,7},{8,9},{10,11},{12,13},{14,15},{16,17},{18,... | collective-permute-start | bytes 98312 | tf_op jit(solution)/shard_map/ppermute | solution.py:196
  161.6 2.1 %collective-permute-start.16 = (f32[64,128]{1,0:T(8,128)S(1)}, f32[64,128]{1,0:T(8,128)S(1)}, u32[]{:S(2)}, u32[]{:S(2)}) collective-permute-start(f32[64,128]{1,0:T(8,128)S(1)} %get-tuple-element.62), channel_id=1, source_target_pairs={{1,2},{3,4},{5,6},{7,8},{9,10},{11,12},{13,14},{15,16},{17,18},{19... | collective-permute-start | bytes 98312 | tf_op jit(solution)/shard_map/ppermute | solution.py:196
  163.7 12.9 %all_to_all.44.totals = f32[32,1,128]{2,1,0:T(1,128)S(1)} all-to-all(f32[32,1,128]{2,1,0:T(1,128)S(1)} %broadcast_in_dim.2), channel_id=1, replica_groups=mesh['x1'=2,'x0'=2,'z2'=2,'z1'=2,'z0'=2,'y2'=2,'y1'=2,'y0'=2,'core'=2] {..., dimensions={0} | all-to-all | bytes 32768 | tf_op jit(solution)/shard_map/all_to_all | solution.py:366
  176.7 0.0 collective-permute-done.15.near_in
  176.7 0.0 collective-permute-done.16.far_in
  176.7 0.0 collective-permute-done.14.slab_odd
  176.7 0.0 collective-permute-done.13.slab_even
  176.7 0.8 shard_map.85
  (3 shorter events, 0.1 us)
Async XLA Ops:
  4.8 27.6 %all-to-all-start = ((f32[4,256,128]{2,1,0:T(8,128)}), f32[4,256,128]{2,1,0:T(8,128)S(1)}, u32[]{:S(2)}, u32[]{:S(2)}) async-start(f32[4,256,128]{2,1,0:T(8,128)} %get-tuple-element.42), calls=%async_computation | async-start | bytes 1048576 | tf_op jit(solution)/shard_map/all_to_all | solution.py:366
  9.6 21.7 %collective-permute-start.1 = (f32[64,256]{1,0:T(8,128)}, f32[64,256]{1,0:T(8,128)S(1)}, u32[]{:S(2)}, u32[]{:S(2)}) collective-permute-start(f32[64,256]{1,0:T(8,128)} %get-tuple-element.36), channel_id=1, source_target_pairs={{32,64},{96,128},{160,192},{224,256},{288,320},{352,384},{416,448}... | collective-permute-start | bytes 196616 | tf_op jit(solution)/shard_map/ppermute | solution.py:196
  10.3 21.1 %collective-permute-start = (f32[64,256]{1,0:T(8,128)}, f32[64,256]{1,0:T(8,128)S(1)}, u32[]{:S(2)}, u32[]{:S(2)}) collective-permute-start(f32[64,256]{1,0:T(8,128)} %get-tuple-element.36), channel_id=1, source_target_pairs={{0,32},{64,96},{128,160},{192,224},{256,288},{320,352},{384,416},{... | collective-permute-start | bytes 196616 | tf_op jit(solution)/shard_map/ppermute | solution.py:196
  22.5 6.5 %collective-permute-start.2 = (f32[64,128]{1,0:T(8,128)}, f32[64,128]{1,0:T(8,128)S(1)}, u32[]{:S(2)}, u32[]{:S(2)}) collective-permute-start(f32[64,128]{1,0:T(8,128)} %get-tuple-element.37), channel_id=1, source_target_pairs={{0,1},{2,3},{4,5},{6,7},{8,9},{10,11},{12,13},{14,15},{16,17},{18,... | collective-permute-start | bytes 98312 | tf_op jit(solution)/shard_map/ppermute | solution.py:196
  25.9 5.4 %collective-permute-start.3 = (f32[64,128]{1,0:T(8,128)}, f32[64,128]{1,0:T(8,128)S(1)}, u32[]{:S(2)}, u32[]{:S(2)}) collective-permute-start(f32[64,128]{1,0:T(8,128)} %get-tuple-element.38), channel_id=1, source_target_pairs={{1,2},{3,4},{5,6},{7,8},{9,10},{11,12},{13,14},{15,16},{17,18},{19... | collective-permute-start | bytes 98312 | tf_op jit(solution)/shard_map/ppermute | solution.py:196
  31.3 0.9 copy-start
  32.4 17.9 %collective-permute-start.8 = (f32[4,256,128]{2,1,0:T(8,128)S(1)}, f32[4,256,128]{2,1,0:T(8,128)S(1)}, u32[]{:S(2)}, u32[]{:S(2)}) collective-permute-start(f32[4,256,128]{2,1,0:T(8,128)S(1)} %all-to-all-done.mine), channel_id=1, source_target_pairs={{0,1},{1,0},{2,3},{3,2},{4,5},{5,4},{6,7},{7,6},{8,9},{9,8},{10,11... | collective-permute-start | bytes 1572872 | tf_op jit(solution)/shard_map/ppermute | solution.py:386
  34.3 14.9 %collective-permute-start.5 = (f32[64,256]{1,0:T(8,128)S(1)}, f32[64,256]{1,0:T(8,128)S(1)}, u32[]{:S(2)}, u32[]{:S(2)}) collective-permute-start(f32[64,256]{1,0:T(8,128)S(1)} %get-tuple-element.43.resp), channel_id=1, source_target_pairs={{32,64},{96,128},{160,192},{224,256},{288,320},{352,384},{416,448}... | collective-permute-start | bytes 196616 | tf_op jit(solution)/shard_map/ppermute | solution.py:196
  35.0 14.3 %collective-permute-start.4 = (f32[64,256]{1,0:T(8,128)S(1)}, f32[64,256]{1,0:T(8,128)S(1)}, u32[]{:S(2)}, u32[]{:S(2)}) collective-permute-start(f32[64,256]{1,0:T(8,128)S(1)} %get-tuple-element.43.resp), channel_id=1, source_target_pairs={{0,32},{64,96},{128,160},{192,224},{256,288},{320,352},{384,416},{... | collective-permute-start | bytes 196616 | tf_op jit(solution)/shard_map/ppermute | solution.py:196
  41.1 5.0 %collective-permute-start.6 = (f32[64,128]{1,0:T(8,128)S(1)}, f32[64,128]{1,0:T(8,128)S(1)}, u32[]{:S(2)}, u32[]{:S(2)}) collective-permute-start(f32[64,128]{1,0:T(8,128)S(1)} %get-tuple-element.44), channel_id=1, source_target_pairs={{0,1},{2,3},{4,5},{6,7},{8,9},{10,11},{12,13},{14,15},{16,17},{18,... | collective-permute-start | bytes 98312 | tf_op jit(solution)/shard_map/ppermute | solution.py:196
  44.0 5.2 %collective-permute-start.7 = (f32[64,128]{1,0:T(8,128)S(1)}, f32[64,128]{1,0:T(8,128)S(1)}, u32[]{:S(2)}, u32[]{:S(2)}) collective-permute-start(f32[64,128]{1,0:T(8,128)S(1)} %get-tuple-element.45), channel_id=1, source_target_pairs={{1,2},{3,4},{5,6},{7,8},{9,10},{11,12},{13,14},{15,16},{17,18},{19... | collective-permute-start | bytes 98312 | tf_op jit(solution)/shard_map/ppermute | solution.py:196
  49.3 0.9 copy-start.1
  79.8 47.5 %copy-start.2 = (f32[136,256]{1,0:T(8,128)S(1)}, f32[136,256]{1,0:T(8,128)}, u32[]{:S(2)}) copy-start(f32[136,256]{1,0:T(8,128)} %get-tuple-element.35.state.mask) | copy-start | bytes 417796
  114.6 12.7 %all-to-all-start.5 = ((f32[8,8,384]{2,1,0:T(8,128)}), f32[8,8,384]{2,1,0:T(8,128)S(1)}, u32[]{:S(2)}, u32[]{:S(2)}) async-start(f32[8,8,384]{2,1,0:T(8,128)} %shard_map.82), calls=%async_computation.5 | async-start | bytes 196608 | tf_op jit(solution)/shard_map/all_to_all | solution.py:366
  128.1 15.4 %collective-permute-start.10 = (f32[64,256]{1,0:T(8,128)S(1)}, f32[64,256]{1,0:T(8,128)S(1)}, u32[]{:S(2)}, u32[]{:S(2)}) collective-permute-start(f32[64,256]{1,0:T(8,128)S(1)} %get-tuple-element.54), channel_id=1, source_target_pairs={{32,64},{96,128},{160,192},{224,256},{288,320},{352,384},{416,448}... | collective-permute-start | bytes 196616 | tf_op jit(solution)/shard_map/ppermute | solution.py:196
  128.7 14.7 %collective-permute-start.9 = (f32[64,256]{1,0:T(8,128)S(1)}, f32[64,256]{1,0:T(8,128)S(1)}, u32[]{:S(2)}, u32[]{:S(2)}) collective-permute-start(f32[64,256]{1,0:T(8,128)S(1)} %get-tuple-element.54), channel_id=1, source_target_pairs={{0,32},{64,96},{128,160},{192,224},{256,288},{320,352},{384,416},{... | collective-permute-start | bytes 196616 | tf_op jit(solution)/shard_map/ppermute | solution.py:196
  133.4 10.0 %collective-permute-start.11 = (f32[64,128]{1,0:T(8,128)S(1)}, f32[64,128]{1,0:T(8,128)S(1)}, u32[]{:S(2)}, u32[]{:S(2)}) collective-permute-start(f32[64,128]{1,0:T(8,128)S(1)} %get-tuple-element.55), channel_id=1, source_target_pairs={{0,1},{2,3},{4,5},{6,7},{8,9},{10,11},{12,13},{14,15},{16,17},{18,... | collective-permute-start | bytes 98312 | tf_op jit(solution)/shard_map/ppermute | solution.py:196
  136.7 6.7 %collective-permute-start.12 = (f32[64,128]{1,0:T(8,128)S(1)}, f32[64,128]{1,0:T(8,128)S(1)}, u32[]{:S(2)}, u32[]{:S(2)}) collective-permute-start(f32[64,128]{1,0:T(8,128)S(1)} %get-tuple-element.56), channel_id=1, source_target_pairs={{1,2},{3,4},{5,6},{7,8},{9,10},{11,12},{13,14},{15,16},{17,18},{19... | collective-permute-start | bytes 98312 | tf_op jit(solution)/shard_map/ppermute | solution.py:196
  138.8 11.5 %all-to-all-start.6 = ((f32[16,1,128]{2,1,0:T(1,128)}), f32[16,1,128]{2,1,0:T(1,128)S(1)}, u32[]{:S(2)}, u32[]{:S(2)}) async-start(f32[16,1,128]{2,1,0:T(1,128)} %get-tuple-element.53), calls=%async_computation.6 | async-start | bytes 16384 | tf_op jit(solution)/shard_map/all_to_all | solution.py:366
  150.3 26.3 %collective-permute-start.14 = (f32[64,256]{1,0:T(8,128)S(1)}, f32[64,256]{1,0:T(8,128)S(1)}, u32[]{:S(2)}, u32[]{:S(2)}) collective-permute-start(f32[64,256]{1,0:T(8,128)S(1)} %get-tuple-element.60.resp), channel_id=1, source_target_pairs={{32,64},{96,128},{160,192},{224,256},{288,320},{352,384},{416,448}... | collective-permute-start | bytes 196616 | tf_op jit(solution)/shard_map/ppermute | solution.py:196
  151.0 25.7 %collective-permute-start.13 = (f32[64,256]{1,0:T(8,128)S(1)}, f32[64,256]{1,0:T(8,128)S(1)}, u32[]{:S(2)}, u32[]{:S(2)}) collective-permute-start(f32[64,256]{1,0:T(8,128)S(1)} %get-tuple-element.60.resp), channel_id=1, source_target_pairs={{0,32},{64,96},{128,160},{192,224},{256,288},{320,352},{384,416},{... | collective-permute-start | bytes 196616 | tf_op jit(solution)/shard_map/ppermute | solution.py:196
  158.5 18.2 %collective-permute-start.15 = (f32[64,128]{1,0:T(8,128)S(1)}, f32[64,128]{1,0:T(8,128)S(1)}, u32[]{:S(2)}, u32[]{:S(2)}) collective-permute-start(f32[64,128]{1,0:T(8,128)S(1)} %get-tuple-element.61), channel_id=1, source_target_pairs={{0,1},{2,3},{4,5},{6,7},{8,9},{10,11},{12,13},{14,15},{16,17},{18,... | collective-permute-start | bytes 98312 | tf_op jit(solution)/shard_map/ppermute | solution.py:196
  161.6 15.1 %collective-permute-start.16 = (f32[64,128]{1,0:T(8,128)S(1)}, f32[64,128]{1,0:T(8,128)S(1)}, u32[]{:S(2)}, u32[]{:S(2)}) collective-permute-start(f32[64,128]{1,0:T(8,128)S(1)} %get-tuple-element.62), channel_id=1, source_target_pairs={{1,2},{3,4},{5,6},{7,8},{9,10},{11,12},{13,14},{15,16},{17,18},{19... | collective-permute-start | bytes 98312 | tf_op jit(solution)/shard_map/ppermute | solution.py:196

commit v4 on v3

--- a/solution.py
+++ b/solution.py
@@ -162,7 +162,7 @@
         before = jnp.where(lane > 0, pltpu.roll(row, 1, 1), 0.0)
         fields.append(others + after + before)
     field = jnp.concatenate(fields, axis=1) + slab_even[...] + slab_odd[...]
-    scores, mask = state[:count], state[2 * count : 2 * count + 1]
+    scores, mask = state[:count], state[state.shape[0] - 1 :]
     return normalise(scores + BETA_POTTS * field) * mask
 
 
@@ -170,6 +170,13 @@
     count = out.shape[0]
     resp = state[count : 2 * count]
     put(core[0], swept(core, state, resp, slab_even, slab_odd, near_in, far_in), out, near, far)
+
+
+def early_kernel(core, state, slab_even, slab_odd, near_in, far_in, out, near, far, kept):
+    count = out.shape[0]
+    kept[:count] = state[:count]
+    kept[count:] = state[2 * count :]
+    first_kernel(core, state, slab_even, slab_odd, near_in, far_in, out, near, far)
 
 
 def later_kernel(core, state, resp, slab_even, slab_odd, near_in, far_in, out):
@@ -183,6 +190,7 @@
     total = totals[0]
     for n in range(1, totals.shape[0]):
         total = total + totals[n]
+    total = total[:1]
     lane = iotas((1, WIDTH))[1]
     lse = jnp.sum(jnp.where(lane == 0, total, 0.0))
     level = jnp.sum(jnp.where(lane == 2, jnp.log(total), 0.0))
@@ -326,19 +334,30 @@
     top, left = row_at < HALF, col_at < HALF
     below = (row_at >= HALF) & (left | (row_at >= col_at))
     above = top & (row_at > col_at)
-    for k in range(packets.shape[0]):
+    count = packets.shape[0]
+    halves, shifts, offsets, centres = [], [], [], []
+    for k in range(count):
         both, flipped = unfolded(packets[k, :HALF])
         diag, shift, centre, offset = (packets[k, HALF + n : HALF + n + 1] for n in range(4))
         whiten = jnp.where(below, both, jnp.where(above, flipped, 0.0))
-        half = jnp.where(top & (row_at == col_at), diag, whiten).astype(jnp.bfloat16)
-        shift = jnp.broadcast_to(shift, (WIDTH, WIDTH)).T
-        shift = jnp.concatenate([shift, shift], axis=1)
-        offset = jnp.concatenate([offset, offset], axis=1)
-        for block in range(turned.shape[0]):
-            proj = matmul(half, turned[block]) - shift
-            quad = jnp.sum(proj * proj, axis=0, keepdims=True)
-            scores[block, k : k + 1, :CELLS] = offset - 0.5 * quad
-            scores[block, k : k + 1, CELLS:] = centre
+        whiten = jnp.where(top & (row_at == col_at), diag, whiten)
+        halves.append(whiten.astype(jnp.bfloat16))
+        shifts.append(jnp.broadcast_to(shift, (WIDTH, WIDTH)).T)
+        offsets.append(offset)
+        centres.append(centre)
+    halves = jnp.concatenate(halves, axis=0)
+    offsets = jnp.concatenate(offsets, axis=0)
+    offsets = jnp.concatenate([offsets, offsets], axis=1)
+    centres = jnp.concatenate(centres, axis=0)
+    for block in range(turned.shape[0]):
+        proj = matmul(halves, turned[block])
+        quads = []
+        for k in range(count):
+            shift = jnp.concatenate([shifts[k], shifts[k]], axis=1)
+            off = proj[k * WIDTH : (k + 1) * WIDTH] - shift
+            quads.append(jnp.sum(off * off, axis=0, keepdims=True))
+        scores[block, :, :CELLS] = offsets - 0.5 * jnp.concatenate(quads, axis=0)
+        scores[block, :, CELLS:] = centres
 
 
 def likely_kernel(core, tile, part, mask, total, state, resp, near, far, means, totals):
@@ -347,7 +366,7 @@
     for n in range(2):
         own = jnp.where(row == 2 * tile[0] + n, part[:, CELLS:], 0.0)
         means[n : n + 1] = jnp.sum(own, axis=0, keepdims=True)
-    tissue_f = mask[2 * part.shape[0] : 2 * part.shape[0] + 1]
+    tissue_f = mask[mask.shape[0] - 1 :]
     top = jnp.max(values, axis=0, keepdims=True)
     expon = jnp.exp(values - top)
     weight = jnp.sum(expon, axis=0, keepdims=True)
@@ -359,7 +378,7 @@
     lane = iotas((1, WIDTH))[1]
     result = jnp.where(lane == 0, lse, jnp.where(lane == 1, cells, total[...]))
     for n in range(totals.shape[0]):
-        totals[n] = result
+        totals[n] = jnp.broadcast_to(result, totals.shape[1:])
 
 
 def swap_all(value, axes):
@@ -379,13 +398,14 @@
         core, weights0.reshape(1, count), flat, tissue.reshape(2, WIDTH), means0, whiten0
     )
     mine = swap_all(spread, BRICK[:2])
-    resp, near, far = call(
-        first_kernel, resp_shapes, core, before, *halos(resp, near, far), scalars=1
+    kept_shape = ((count + 8, CELLS), f32)
+    resp, near, far, kept = call(
+        early_kernel, resp_shapes + [kept_shape], core, before, *halos(resp, near, far), scalars=1
     )
     resp, near, far, mine = lax.optimization_barrier((resp, near, far, mine))
     theirs = lax.ppermute(mine, "core", [(0, 1), (1, 0)])
     (resp,) = call(
-        later_kernel, resp_shapes[:1], core, before, resp, *halos(resp, near, far), scalars=1
+        later_kernel, resp_shapes[:1], core, kept, resp, *halos(resp, near, far), scalars=1
     )
     resp, theirs = lax.optimization_barrier((resp, theirs))
 
@@ -407,15 +427,15 @@
     sizes = [lax.axis_size(axes) for axes in ROUND]
     state, resp, near, far, means_out, totals = call(
         likely_kernel,
-        [state_shape] + resp_shapes + [((2, WIDTH), f32), ((sizes[0], 1, WIDTH), f32)],
-        core, tile, part, before, total, scalars=2,
+        [state_shape] + resp_shapes + [((2, WIDTH), f32), ((sizes[0], 16, WIDTH), f32)],
+        core, tile, part, kept, total, scalars=2,
     )
     totals = swap_all(totals, ROUND[0])
     resp, near, far = call(
         first_kernel, resp_shapes, core, state, *halos(resp, near, far), scalars=1
     )
     totals, resp, near, far = lax.optimization_barrier((totals, resp, near, far))
-    totals = jnp.broadcast_to(jnp.sum(totals, axis=0)[None], (sizes[1], 1, WIDTH))
+    totals = jnp.broadcast_to(jnp.sum(totals, axis=0)[None, :8], (sizes[1], 8, WIDTH))
     totals = swap_all(totals, ROUND[1])
     sides = halos(resp, near, far)
     resp_final, score = pl.pallas_call(

time: 179 us -> 174 us (0.972)
  blocking collectives: 69.5 us -> 56.5 us
  starting transfers between devices: 74.1 us -> 84 us
    all_to_all x5 -> x4, blocking collectives: 69.5 us -> 56.5 us  [swap_all(): return lax.all_to_all(value, axes, 0, 0, tiled=True)]
    all_to_all x3 -> x4, starting transfers between devices: 17.1 us -> 24 us  [swap_all(): return lax.all_to_all(value, axes, 0, 0, tiled=True)]
    all_to_all x3 -> x4, waiting for transfers between devices: 11.7 us -> 5.01 us  [swap_all(): return lax.all_to_all(value, axes, 0, 0, tiled=True)]
    ppermute x16, waiting for transfers between devices: 5.55 us -> 10.7 us  [swapped(): return lax.ppermute(part, axes, pairs + [(j, i) for i, j in pairs])]
    ppermute x16, starting transfers between devices: 55.1 us -> 58.1 us  [swapped(): return lax.ppermute(part, axes, pairs + [(j, i) for i, j in pairs])]
  transfers between devices with their start and end apart: 20 -> 21, of which waited for: 4 -> 5; matrix products, arithmetic and copies ran while one was open for 0% -> 0% of each run, Pallas kernels for 0% -> 0%
where the time goes in v4:
time: 174 us; the launch traced here: 172 us
  starting transfers between devices  84 us (48%)
  blocking collectives  56.5 us (32%)
  waiting for transfers between devices  15.7 us (9%)
  Pallas kernels  13.6 us (8%)
    ppermute x16, starting transfers between devices, swapped(): return lax.ppermute(part, axes, pairs + [(j, i) for i, j in pairs])  58.1 us
    all_to_all x4, blocking collectives, swap_all(): return lax.all_to_all(value, axes, 0, 0, tiled=True)  56.5 us
    all_to_all x4, starting transfers between devices, swap_all(): return lax.all_to_all(value, axes, 0, 0, tiled=True)  24 us
    ppermute x16, waiting for transfers between devices, swapped(): return lax.ppermute(part, axes, pairs + [(j, i) for i, j in pairs])  10.7 us
    pallas_call x8, Pallas kernels, call(): pl.pallas_call(kernel, out_shape=out, in_specs=[SMEM] * scalars + [VMEM]...  8.68 us
    all_to_all x4, waiting for transfers between devices, swap_all(): return lax.all_to_all(value, axes, 0, 0, tiled=True)  5.01 us
    pallas_call x1, Pallas kernels, start(): pl.pallas_call(start_kernel, out_shape=[jax.ShapeDtypeStruct(shape, f32)...  4.12 us
  transfers between devices with their start and end apart: 21, of which 5 were waited for; matrix products, arithmetic and copies ran while one was open for 0% of the time, Pallas kernels for 0%

profile of v4, /device:TPU:1, one launch (start us, length us, event | category | flops | bytes accessed | tf_op | source)
XLA Modules:
  0.0 172.3 jit_solution(7278334230657162520)
XLA Ops:
  0.6 4.1 %shard_map.76 = (f32[136,256]{1,0:T(8,128)}, f32[64,256]{1,0:T(8,128)}, f32[64,128]{1,0:T(8,128)}, f32[64,128]{1,0:T(8,128)}, f32[4,256,128]{2,1,0:T(8,128)}) custom-call(s32[1]{0:T(128)} %bitcast.core, f32[1,64]{1,0:T(1,128)} %bitcast.15, bf16[256,128]{1,0:T(8,128)(2,1)} %bitcast.13, s32[2,128]{1,0:T(2,128)} %bitcast.14, f32[64,128]{1,0:T(8,128)} %means.1, ...), custom_call_target="tpu_custom_call" | custom-call | flops 536870912 | bytes 2097152 | tf_op jit(solution)/shard_map/pallas_call | solution.py:134
  4.8 4.9 %all-to-all-start = ((f32[4,256,128]{2,1,0:T(8,128)}), f32[4,256,128]{2,1,0:T(8,128)S(1)}, u32[]{:S(2)}, u32[]{:S(2)}) async-start(f32[4,256,128]{2,1,0:T(8,128)} %get-tuple-element.44), calls=%async_computation | async-start | bytes 1048576 | tf_op jit(solution)/shard_map/all_to_all | solution.py:385
  9.6 0.7 collective-permute-start.1
  10.3 12.2 %collective-permute-start = (f32[64,256]{1,0:T(8,128)}, f32[64,256]{1,0:T(8,128)S(1)}, u32[]{:S(2)}, u32[]{:S(2)}) collective-permute-start(f32[64,256]{1,0:T(8,128)} %get-tuple-element.37), channel_id=1, source_target_pairs={{0,32},{64,96},{128,160},{192,224},{256,288},{320,352},{384,416},{... | collective-permute-start | bytes 196616 | tf_op jit(solution)/shard_map/ppermute | solution.py:204
  22.5 3.4 %collective-permute-start.2 = (f32[64,128]{1,0:T(8,128)}, f32[64,128]{1,0:T(8,128)S(1)}, u32[]{:S(2)}, u32[]{:S(2)}) collective-permute-start(f32[64,128]{1,0:T(8,128)} %get-tuple-element.38), channel_id=1, source_target_pairs={{0,1},{2,3},{4,5},{6,7},{8,9},{10,11},{12,13},{14,15},{16,17},{18,... | collective-permute-start | bytes 98312 | tf_op jit(solution)/shard_map/ppermute | solution.py:204
  25.9 3.1 %collective-permute-start.3 = (f32[64,128]{1,0:T(8,128)}, f32[64,128]{1,0:T(8,128)S(1)}, u32[]{:S(2)}, u32[]{:S(2)}) collective-permute-start(f32[64,128]{1,0:T(8,128)} %get-tuple-element.39), channel_id=1, source_target_pairs={{1,2},{3,4},{5,6},{7,8},{9,10},{11,12},{13,14},{15,16},{17,18},{19... | collective-permute-start | bytes 98312 | tf_op jit(solution)/shard_map/ppermute | solution.py:204
  29.0 0.0 collective-permute-done.2.near_in
  29.0 2.3 %collective-permute-done.3.far_in = f32[64,128]{1,0:T(8,128)S(1)} collective-permute-done((f32[64,128]{1,0:T(8,128)}, f32[64,128]{1,0:T(8,128)S(1)}, u32[]{:S(2)}, u32[]{:S(2)}) %collective-permute-start.3) | collective-permute-done | bytes 32800 | tf_op jit(solution)/shard_map/ppermute | solution.py:204
  31.3 0.0 collective-permute-done.1.slab_odd
  31.3 0.0 collective-permute-done.slab_even
  31.3 0.0 copy-start
  31.3 0.9 copy-done
  32.2 0.1 shard_map.77
  32.4 0.0 all-to-all-done.mine
  32.4 1.9 %collective-permute-start.8 = (f32[4,256,128]{2,1,0:T(8,128)S(1)}, f32[4,256,128]{2,1,0:T(8,128)S(1)}, u32[]{:S(2)}, u32[]{:S(2)}) collective-permute-start(f32[4,256,128]{2,1,0:T(8,128)S(1)} %all-to-all-done.mine), channel_id=1, source_target_pairs={{0,1},{1,0},{2,3},{3,2},{4,5},{5,4},{6,7},{7,6},{8,9},{9,8},{10,11... | collective-permute-start | bytes 1572872 | tf_op jit(solution)/shard_map/ppermute | solution.py:406
  34.3 0.7 collective-permute-start.5
  35.0 6.1 %collective-permute-start.4 = (f32[64,256]{1,0:T(8,128)S(1)}, f32[64,256]{1,0:T(8,128)S(1)}, u32[]{:S(2)}, u32[]{:S(2)}) collective-permute-start(f32[64,256]{1,0:T(8,128)S(1)} %get-tuple-element.45.resp), channel_id=1, source_target_pairs={{0,32},{64,96},{128,160},{192,224},{256,288},{320,352},{384,416},{... | collective-permute-start | bytes 196616 | tf_op jit(solution)/shard_map/ppermute | solution.py:204
  41.1 3.0 %collective-permute-start.6 = (f32[64,128]{1,0:T(8,128)S(1)}, f32[64,128]{1,0:T(8,128)S(1)}, u32[]{:S(2)}, u32[]{:S(2)}) collective-permute-start(f32[64,128]{1,0:T(8,128)S(1)} %get-tuple-element.46), channel_id=1, source_target_pairs={{0,1},{2,3},{4,5},{6,7},{8,9},{10,11},{12,13},{14,15},{16,17},{18,... | collective-permute-start | bytes 98312 | tf_op jit(solution)/shard_map/ppermute | solution.py:204
  44.0 2.0 %collective-permute-start.7 = (f32[64,128]{1,0:T(8,128)S(1)}, f32[64,128]{1,0:T(8,128)S(1)}, u32[]{:S(2)}, u32[]{:S(2)}) collective-permute-start(f32[64,128]{1,0:T(8,128)S(1)} %get-tuple-element.47), channel_id=1, source_target_pairs={{1,2},{3,4},{5,6},{7,8},{9,10},{11,12},{13,14},{15,16},{17,18},{19... | collective-permute-start | bytes 98312 | tf_op jit(solution)/shard_map/ppermute | solution.py:204
  46.1 0.0 collective-permute-done.6.near_in
  46.1 3.2 %collective-permute-done.7.far_in = f32[64,128]{1,0:T(8,128)S(1)} collective-permute-done((f32[64,128]{1,0:T(8,128)S(1)}, f32[64,128]{1,0:T(8,128)S(1)}, u32[]{:S(2)}, u32[]{:S(2)}) %collective-permute-start.7) | collective-permute-done | bytes 32800 | tf_op jit(solution)/shard_map/ppermute | solution.py:204
  49.3 0.0 collective-permute-done.5.slab_odd
  49.3 0.0 collective-permute-done.4.slab_even
  49.3 0.1 shard_map.78
  49.4 0.0 collective-permute-done.8.theirs
  49.4 8.7 %all_to_all.40.resp = f32[8,8,256]{2,1,0:T(8,128)S(1)} all-to-all(f32[8,8,256]{2,1,0:T(8,128)S(1)} %bitcast.12), channel_id=1, replica_groups=mesh['x1'=2,'x0'=2,'z2'=2,'z1'=2,'z0'=2,'y2'=2,'y1'=2,'y0'=2,'core'=2] {..., dimensions={0} | all-to-all | bytes 131072 | tf_op jit(solution)/shard_map/all_to_all | solution.py:385
  58.2 1.6 shard_map.79
  59.7 19.1 %all_to_all.41.packets = f32[8,72,128]{2,1,0:T(8,128)S(1)} all-to-all(f32[8,72,128]{2,1,0:T(8,128)S(1)} %get-tuple-element.51), channel_id=1, replica_groups=mesh['x1'=2,'x0'=2,'z2'=2,'z1'=2,'z0'=2,'y2'=2,'y1'=2,'y0'=2,'core'=2] {..., dimensions={0} | all-to-all | bytes 589824 | tf_op jit(solution)/shard_map/all_to_all | solution.py:385
  78.9 15.0 %all_to_all.42.packets = f32[8,72,128]{2,1,0:T(8,128)S(1)} all-to-all(f32[8,72,128]{2,1,0:T(8,128)S(1)} %shard_map.80), channel_id=1, replica_groups=mesh['x1'=2,'x0'=2,'z2'=2,'z1'=2,'z0'=2,'y2'=2,'y1'=2,'y0'=2,'core'=2] {..., dimensions={0} | all-to-all | bytes 589824 | tf_op jit(solution)/shard_map/all_to_all | solution.py:385
  93.9 3.8 %shard_map.81 = f32[8,72,128]{2,1,0:T(8,128)S(1)} custom-call(f32[8,72,128]{2,1,0:T(8,128)S(1)} %all_to_all.42.packets), custom_call_target="tpu_custom_call" | custom-call | flops 134217728 | bytes 1048576 | tf_op jit(solution)/shard_map/pallas_call | solution.py:33
  97.7 13.6 %all_to_all.43.packets = f32[8,72,128]{2,1,0:T(8,128)S(1)} all-to-all(f32[8,72,128]{2,1,0:T(8,128)S(1)} %shard_map.81), channel_id=1, replica_groups=mesh['x1'=2,'x0'=2,'z2'=2,'z1'=2,'z0'=2,'y2'=2,'y1'=2,'y0'=2,'core'=2] {..., dimensions={0} | all-to-all | bytes 589824 | tf_op jit(solution)/shard_map/all_to_all | solution.py:385
  111.3 2.0 %shard_map.82 = f32[8,8,384]{2,1,0:T(8,128)} custom-call(f32[8,72,128]{2,1,0:T(8,128)S(1)} %all_to_all.43.packets, bf16[8,128,256]{2,1,0:T(8,128)(2,1)S(1)} %get-tuple-element.52.turned), custom_call_target="tpu_custom_call" | custom-call | flops 536870912 | bytes 1048576 | tf_op jit(solution)/shard_map/pallas_call | solution.py:33
  113.4 7.7 %all-to-all-start.5 = ((f32[8,8,384]{2,1,0:T(8,128)}), f32[8,8,384]{2,1,0:T(8,128)S(1)}, u32[]{:S(2)}, u32[]{:S(2)}) async-start(f32[8,8,384]{2,1,0:T(8,128)} %shard_map.82), calls=%async_computation.5 | async-start | bytes 196608 | tf_op jit(solution)/shard_map/all_to_all | solution.py:385
  121.1 5.0 %all-to-all-done.5 = f32[8,8,384]{2,1,0:T(8,128)S(1)} async-done(((f32[8,8,384]{2,1,0:T(8,128)}), f32[8,8,384]{2,1,0:T(8,128)S(1)}, u32[]{:S(2)}, u32[]{:S(2)}) %all-to-all-start.5) | async-done | bytes 98336 | tf_op jit(solution)/shard_map/all_to_all | solution.py:385
  126.1 0.8 shard_map.83
  126.8 4.1 %all-to-all-start.6 = ((f32[16,16,128]{2,1,0:T(8,128)}), f32[16,16,128]{2,1,0:T(8,128)S(1)}, u32[]{:S(2)}, u32[]{:S(2)}) async-start(f32[16,16,128]{2,1,0:T(8,128)} %get-tuple-element.55), calls=%async_computation.6 | async-start | bytes 262144 | tf_op jit(solution)/shard_map/all_to_all | solution.py:385
  131.0 0.7 collective-permute-start.10
  131.6 4.7 %collective-permute-start.9 = (f32[64,256]{1,0:T(8,128)S(1)}, f32[64,256]{1,0:T(8,128)S(1)}, u32[]{:S(2)}, u32[]{:S(2)}) collective-permute-start(f32[64,256]{1,0:T(8,128)S(1)} %get-tuple-element.56), channel_id=1, source_target_pairs={{0,32},{64,96},{128,160},{192,224},{256,288},{320,352},{384,416},{... | collective-permute-start | bytes 196616 | tf_op jit(solution)/shard_map/ppermute | solution.py:204
  136.3 2.7 %collective-permute-start.11 = (f32[64,128]{1,0:T(8,128)S(1)}, f32[64,128]{1,0:T(8,128)S(1)}, u32[]{:S(2)}, u32[]{:S(2)}) collective-permute-start(f32[64,128]{1,0:T(8,128)S(1)} %get-tuple-element.57), channel_id=1, source_target_pairs={{0,1},{2,3},{4,5},{6,7},{8,9},{10,11},{12,13},{14,15},{16,17},{18,... | collective-permute-start | bytes 98312 | tf_op jit(solution)/shard_map/ppermute | solution.py:204
  139.0 3.3 %collective-permute-start.12 = (f32[64,128]{1,0:T(8,128)S(1)}, f32[64,128]{1,0:T(8,128)S(1)}, u32[]{:S(2)}, u32[]{:S(2)}) collective-permute-start(f32[64,128]{1,0:T(8,128)S(1)} %get-tuple-element.58), channel_id=1, source_target_pairs={{1,2},{3,4},{5,6},{7,8},{9,10},{11,12},{13,14},{15,16},{17,18},{19... | collective-permute-start | bytes 98312 | tf_op jit(solution)/shard_map/ppermute | solution.py:204
  142.3 0.0 collective-permute-done.11.near_in
  142.4 1.9 %collective-permute-done.12.far_in = f32[64,128]{1,0:T(8,128)S(1)} collective-permute-done((f32[64,128]{1,0:T(8,128)S(1)}, f32[64,128]{1,0:T(8,128)S(1)}, u32[]{:S(2)}, u32[]{:S(2)}) %collective-permute-start.12) | collective-permute-done | bytes 32800 | tf_op jit(solution)/shard_map/ppermute | solution.py:204
  144.2 0.0 collective-permute-done.10.slab_odd
  144.2 0.0 collective-permute-done.9.slab_even
  144.2 0.1 shard_map.84
  144.4 0.0 all-to-all-done.6
  144.5 0.7 broadcast_in_dim.2
  145.1 7.3 %all-to-all-start.7 = ((f32[32,8,128]{2,1,0:T(8,128)}), f32[32,8,128]{2,1,0:T(8,128)S(1)}, u32[]{:S(2)}, u32[]{:S(2)}) async-start(f32[32,8,128]{2,1,0:T(8,128)} %broadcast_in_dim.2), calls=%async_computation.7 | async-start | bytes 262144 | tf_op jit(solution)/shard_map/all_to_all | solution.py:385
  152.4 0.7 collective-permute-start.14
  153.1 8.6 %collective-permute-start.13 = (f32[64,256]{1,0:T(8,128)S(1)}, f32[64,256]{1,0:T(8,128)S(1)}, u32[]{:S(2)}, u32[]{:S(2)}) collective-permute-start(f32[64,256]{1,0:T(8,128)S(1)} %get-tuple-element.62.resp), channel_id=1, source_target_pairs={{0,32},{64,96},{128,160},{192,224},{256,288},{320,352},{384,416},{... | collective-permute-start | bytes 196616 | tf_op jit(solution)/shard_map/ppermute | solution.py:204
  161.7 4.5 %collective-permute-start.15 = (f32[64,128]{1,0:T(8,128)S(1)}, f32[64,128]{1,0:T(8,128)S(1)}, u32[]{:S(2)}, u32[]{:S(2)}) collective-permute-start(f32[64,128]{1,0:T(8,128)S(1)} %get-tuple-element.63), channel_id=1, source_target_pairs={{0,1},{2,3},{4,5},{6,7},{8,9},{10,11},{12,13},{14,15},{16,17},{18,... | collective-permute-start | bytes 98312 | tf_op jit(solution)/shard_map/ppermute | solution.py:204
  166.2 1.9 %collective-permute-start.16 = (f32[64,128]{1,0:T(8,128)S(1)}, f32[64,128]{1,0:T(8,128)S(1)}, u32[]{:S(2)}, u32[]{:S(2)}) collective-permute-start(f32[64,128]{1,0:T(8,128)S(1)} %get-tuple-element.64), channel_id=1, source_target_pairs={{1,2},{3,4},{5,6},{7,8},{9,10},{11,12},{13,14},{15,16},{17,18},{19... | collective-permute-start | bytes 98312 | tf_op jit(solution)/shard_map/ppermute | solution.py:204
  168.1 0.0 collective-permute-done.15.near_in
  168.1 3.3 %collective-permute-done.16.far_in = f32[64,128]{1,0:T(8,128)S(1)} collective-permute-done((f32[64,128]{1,0:T(8,128)S(1)}, f32[64,128]{1,0:T(8,128)S(1)}, u32[]{:S(2)}, u32[]{:S(2)}) %collective-permute-start.16) | collective-permute-done | bytes 32800 | tf_op jit(solution)/shard_map/ppermute | solution.py:204
  171.4 0.0 collective-permute-done.14.slab_odd
  171.4 0.0 collective-permute-done.13.slab_even
  171.4 0.0 all-to-all-done.7.totals
  171.4 0.8 shard_map.85
  (3 shorter events, 0.1 us)
Async XLA Ops:
  4.8 27.6 %all-to-all-start = ((f32[4,256,128]{2,1,0:T(8,128)}), f32[4,256,128]{2,1,0:T(8,128)S(1)}, u32[]{:S(2)}, u32[]{:S(2)}) async-start(f32[4,256,128]{2,1,0:T(8,128)} %get-tuple-element.44), calls=%async_computation | async-start | bytes 1048576 | tf_op jit(solution)/shard_map/all_to_all | solution.py:385
  9.6 21.7 %collective-permute-start.1 = (f32[64,256]{1,0:T(8,128)}, f32[64,256]{1,0:T(8,128)S(1)}, u32[]{:S(2)}, u32[]{:S(2)}) collective-permute-start(f32[64,256]{1,0:T(8,128)} %get-tuple-element.37), channel_id=1, source_target_pairs={{32,64},{96,128},{160,192},{224,256},{288,320},{352,384},{416,448}... | collective-permute-start | bytes 196616 | tf_op jit(solution)/shard_map/ppermute | solution.py:204
  10.3 21.1 %collective-permute-start = (f32[64,256]{1,0:T(8,128)}, f32[64,256]{1,0:T(8,128)S(1)}, u32[]{:S(2)}, u32[]{:S(2)}) collective-permute-start(f32[64,256]{1,0:T(8,128)} %get-tuple-element.37), channel_id=1, source_target_pairs={{0,32},{64,96},{128,160},{192,224},{256,288},{320,352},{384,416},{... | collective-permute-start | bytes 196616 | tf_op jit(solution)/shard_map/ppermute | solution.py:204
  22.5 6.5 %collective-permute-start.2 = (f32[64,128]{1,0:T(8,128)}, f32[64,128]{1,0:T(8,128)S(1)}, u32[]{:S(2)}, u32[]{:S(2)}) collective-permute-start(f32[64,128]{1,0:T(8,128)} %get-tuple-element.38), channel_id=1, source_target_pairs={{0,1},{2,3},{4,5},{6,7},{8,9},{10,11},{12,13},{14,15},{16,17},{18,... | collective-permute-start | bytes 98312 | tf_op jit(solution)/shard_map/ppermute | solution.py:204
  25.9 5.4 %collective-permute-start.3 = (f32[64,128]{1,0:T(8,128)}, f32[64,128]{1,0:T(8,128)S(1)}, u32[]{:S(2)}, u32[]{:S(2)}) collective-permute-start(f32[64,128]{1,0:T(8,128)} %get-tuple-element.39), channel_id=1, source_target_pairs={{1,2},{3,4},{5,6},{7,8},{9,10},{11,12},{13,14},{15,16},{17,18},{19... | collective-permute-start | bytes 98312 | tf_op jit(solution)/shard_map/ppermute | solution.py:204
  31.3 0.9 copy-start
  32.4 17.0 %collective-permute-start.8 = (f32[4,256,128]{2,1,0:T(8,128)S(1)}, f32[4,256,128]{2,1,0:T(8,128)S(1)}, u32[]{:S(2)}, u32[]{:S(2)}) collective-permute-start(f32[4,256,128]{2,1,0:T(8,128)S(1)} %all-to-all-done.mine), channel_id=1, source_target_pairs={{0,1},{1,0},{2,3},{3,2},{4,5},{5,4},{6,7},{7,6},{8,9},{9,8},{10,11... | collective-permute-start | bytes 1572872 | tf_op jit(solution)/shard_map/ppermute | solution.py:406
  34.3 14.9 %collective-permute-start.5 = (f32[64,256]{1,0:T(8,128)S(1)}, f32[64,256]{1,0:T(8,128)S(1)}, u32[]{:S(2)}, u32[]{:S(2)}) collective-permute-start(f32[64,256]{1,0:T(8,128)S(1)} %get-tuple-element.45.resp), channel_id=1, source_target_pairs={{32,64},{96,128},{160,192},{224,256},{288,320},{352,384},{416,448}... | collective-permute-start | bytes 196616 | tf_op jit(solution)/shard_map/ppermute | solution.py:204
  35.0 14.3 %collective-permute-start.4 = (f32[64,256]{1,0:T(8,128)S(1)}, f32[64,256]{1,0:T(8,128)S(1)}, u32[]{:S(2)}, u32[]{:S(2)}) collective-permute-start(f32[64,256]{1,0:T(8,128)S(1)} %get-tuple-element.45.resp), channel_id=1, source_target_pairs={{0,32},{64,96},{128,160},{192,224},{256,288},{320,352},{384,416},{... | collective-permute-start | bytes 196616 | tf_op jit(solution)/shard_map/ppermute | solution.py:204
  41.1 5.0 %collective-permute-start.6 = (f32[64,128]{1,0:T(8,128)S(1)}, f32[64,128]{1,0:T(8,128)S(1)}, u32[]{:S(2)}, u32[]{:S(2)}) collective-permute-start(f32[64,128]{1,0:T(8,128)S(1)} %get-tuple-element.46), channel_id=1, source_target_pairs={{0,1},{2,3},{4,5},{6,7},{8,9},{10,11},{12,13},{14,15},{16,17},{18,... | collective-permute-start | bytes 98312 | tf_op jit(solution)/shard_map/ppermute | solution.py:204
  44.0 5.2 %collective-permute-start.7 = (f32[64,128]{1,0:T(8,128)S(1)}, f32[64,128]{1,0:T(8,128)S(1)}, u32[]{:S(2)}, u32[]{:S(2)}) collective-permute-start(f32[64,128]{1,0:T(8,128)S(1)} %get-tuple-element.47), channel_id=1, source_target_pairs={{1,2},{3,4},{5,6},{7,8},{9,10},{11,12},{13,14},{15,16},{17,18},{19... | collective-permute-start | bytes 98312 | tf_op jit(solution)/shard_map/ppermute | solution.py:204
  113.4 12.7 %all-to-all-start.5 = ((f32[8,8,384]{2,1,0:T(8,128)}), f32[8,8,384]{2,1,0:T(8,128)S(1)}, u32[]{:S(2)}, u32[]{:S(2)}) async-start(f32[8,8,384]{2,1,0:T(8,128)} %shard_map.82), calls=%async_computation.5 | async-start | bytes 196608 | tf_op jit(solution)/shard_map/all_to_all | solution.py:385
  126.8 17.6 %all-to-all-start.6 = ((f32[16,16,128]{2,1,0:T(8,128)}), f32[16,16,128]{2,1,0:T(8,128)S(1)}, u32[]{:S(2)}, u32[]{:S(2)}) async-start(f32[16,16,128]{2,1,0:T(8,128)} %get-tuple-element.55), calls=%async_computation.6 | async-start | bytes 262144 | tf_op jit(solution)/shard_map/all_to_all | solution.py:385
  131.0 13.3 %collective-permute-start.10 = (f32[64,256]{1,0:T(8,128)S(1)}, f32[64,256]{1,0:T(8,128)S(1)}, u32[]{:S(2)}, u32[]{:S(2)}) collective-permute-start(f32[64,256]{1,0:T(8,128)S(1)} %get-tuple-element.56), channel_id=1, source_target_pairs={{32,64},{96,128},{160,192},{224,256},{288,320},{352,384},{416,448}... | collective-permute-start | bytes 196616 | tf_op jit(solution)/shard_map/ppermute | solution.py:204
  131.6 12.6 %collective-permute-start.9 = (f32[64,256]{1,0:T(8,128)S(1)}, f32[64,256]{1,0:T(8,128)S(1)}, u32[]{:S(2)}, u32[]{:S(2)}) collective-permute-start(f32[64,256]{1,0:T(8,128)S(1)} %get-tuple-element.56), channel_id=1, source_target_pairs={{0,32},{64,96},{128,160},{192,224},{256,288},{320,352},{384,416},{... | collective-permute-start | bytes 196616 | tf_op jit(solution)/shard_map/ppermute | solution.py:204
  136.3 6.0 %collective-permute-start.11 = (f32[64,128]{1,0:T(8,128)S(1)}, f32[64,128]{1,0:T(8,128)S(1)}, u32[]{:S(2)}, u32[]{:S(2)}) collective-permute-start(f32[64,128]{1,0:T(8,128)S(1)} %get-tuple-element.57), channel_id=1, source_target_pairs={{0,1},{2,3},{4,5},{6,7},{8,9},{10,11},{12,13},{14,15},{16,17},{18,... | collective-permute-start | bytes 98312 | tf_op jit(solution)/shard_map/ppermute | solution.py:204
  139.0 5.2 %collective-permute-start.12 = (f32[64,128]{1,0:T(8,128)S(1)}, f32[64,128]{1,0:T(8,128)S(1)}, u32[]{:S(2)}, u32[]{:S(2)}) collective-permute-start(f32[64,128]{1,0:T(8,128)S(1)} %get-tuple-element.58), channel_id=1, source_target_pairs={{1,2},{3,4},{5,6},{7,8},{9,10},{11,12},{13,14},{15,16},{17,18},{19... | collective-permute-start | bytes 98312 | tf_op jit(solution)/shard_map/ppermute | solution.py:204
  145.1 26.3 %all-to-all-start.7 = ((f32[32,8,128]{2,1,0:T(8,128)}), f32[32,8,128]{2,1,0:T(8,128)S(1)}, u32[]{:S(2)}, u32[]{:S(2)}) async-start(f32[32,8,128]{2,1,0:T(8,128)} %broadcast_in_dim.2), calls=%async_computation.7 | async-start | bytes 262144 | tf_op jit(solution)/shard_map/all_to_all | solution.py:385
  152.4 19.0 %collective-permute-start.14 = (f32[64,256]{1,0:T(8,128)S(1)}, f32[64,256]{1,0:T(8,128)S(1)}, u32[]{:S(2)}, u32[]{:S(2)}) collective-permute-start(f32[64,256]{1,0:T(8,128)S(1)} %get-tuple-element.62.resp), channel_id=1, source_target_pairs={{32,64},{96,128},{160,192},{224,256},{288,320},{352,384},{416,448}... | collective-permute-start | bytes 196616 | tf_op jit(solution)/shard_map/ppermute | solution.py:204
  153.1 18.3 %collective-permute-start.13 = (f32[64,256]{1,0:T(8,128)S(1)}, f32[64,256]{1,0:T(8,128)S(1)}, u32[]{:S(2)}, u32[]{:S(2)}) collective-permute-start(f32[64,256]{1,0:T(8,128)S(1)} %get-tuple-element.62.resp), channel_id=1, source_target_pairs={{0,32},{64,96},{128,160},{192,224},{256,288},{320,352},{384,416},{... | collective-permute-start | bytes 196616 | tf_op jit(solution)/shard_map/ppermute | solution.py:204
  161.7 6.4 %collective-permute-start.15 = (f32[64,128]{1,0:T(8,128)S(1)}, f32[64,128]{1,0:T(8,128)S(1)}, u32[]{:S(2)}, u32[]{:S(2)}) collective-permute-start(f32[64,128]{1,0:T(8,128)S(1)} %get-tuple-element.63), channel_id=1, source_target_pairs={{0,1},{2,3},{4,5},{6,7},{8,9},{10,11},{12,13},{14,15},{16,17},{18,... | collective-permute-start | bytes 98312 | tf_op jit(solution)/shard_map/ppermute | solution.py:204
  166.2 5.2 %collective-permute-start.16 = (f32[64,128]{1,0:T(8,128)S(1)}, f32[64,128]{1,0:T(8,128)S(1)}, u32[]{:S(2)}, u32[]{:S(2)}) collective-permute-start(f32[64,128]{1,0:T(8,128)S(1)} %get-tuple-element.64), channel_id=1, source_target_pairs={{1,2},{3,4},{5,6},{7,8},{9,10},{11,12},{13,14},{15,16},{17,18},{19... | collective-permute-start | bytes 98312 | tf_op jit(solution)/shard_map/ppermute | solution.py:204

commit v5 on v4

--- a/solution.py
+++ b/solution.py
@@ -13,8 +13,11 @@
 SLAB = ("x1", "x0", "z2", "z1")
 TILE = ("z0", "y2", "y1", "y0", "core")
 BRICK = ("x1", "x0", "core")
-NEAR = ("y2", "y1", "y0")
-FAR = ("z2", "z1", "z0")
+PLANE = ("z2", "z1", "z0", "y2", "y1", "y0", "core")
+ALONG_Y = [[[z * 16 + y * 2 + core for y in range(8)] for z in range(8)] for core in range(2)]
+ALONG_Z = [[[z * 16 + y * 2 + core for z in range(8)] for y in range(8)] for core in range(2)]
+NEAR = ALONG_Y[0] + ALONG_Z[1]
+FAR = ALONG_Z[0] + ALONG_Y[1]
 ROUND = (("y2", "y1", "y0", "core"), ("x1", "x0", "z2", "z1", "z0"))
 
 WIDTH = 128
@@ -385,6 +388,10 @@
     return lax.all_to_all(value, axes, 0, 0, tiled=True)
 
 
+def swap_lines(value, groups):
+    return lax.all_to_all(value, PLANE, 0, 0, axis_index_groups=groups, tiled=True)
+
+
 def shards(embed, tissue, whiten0, means0, weights0):
     count = whiten0.shape[0]
     f32 = jnp.float32
@@ -415,10 +422,10 @@
         [((8, PACKET, WIDTH), f32), ((8, WIDTH, CELLS), jnp.bfloat16), ((1, WIDTH), f32)],
         core, part, mine, theirs, scalars=1, flops=1 << 30,
     )
-    (packets,) = call(gather_kernel, [((8, PACKET, WIDTH), f32)], swap_all(packets, NEAR))
-    packets = swap_all(packets, FAR)
+    (packets,) = call(gather_kernel, [((8, PACKET, WIDTH), f32)], swap_lines(packets, NEAR))
+    packets = swap_lines(packets, FAR)
     (packets,) = call(factor_kernel, [((8, PACKET, WIDTH), f32)], packets, flops=1 << 27)
-    packets = swap_all(packets, NEAR)
+    packets = swap_lines(packets, NEAR)
     (part,) = call(
         second_kernel, [((8, 8, CELLS + WIDTH), f32)], packets, turned, flops=1 << 29
     )

time: 174 us -> 172 us (0.989)
  blocking collectives: 56.5 us -> 53.9 us
    all_to_all x4 -> x1, blocking collectives: 56.5 us -> 8.71 us  [swap_all(): return lax.all_to_all(value, axes, 0, 0, tiled=True)]
    all_to_all x0 -> x3, blocking collectives: none -> 45.2 us  [swap_lines(): lax.all_to_all(value, PLANE, 0, 0, axis_index_groups=groups, tiled=True)]
where the time goes in v5:
time: 172 us; the launch traced here: 170 us
  starting transfers between devices  84.3 us (49%)
  blocking collectives  53.9 us (31%)
  waiting for transfers between devices  15.7 us (9%)
  Pallas kernels  13.6 us (8%)
    ppermute x16, starting transfers between devices, swapped(): return lax.ppermute(part, axes, pairs + [(j, i) for i, j in pairs])  57.1 us
    all_to_all x3, blocking collectives, swap_lines(): lax.all_to_all(value, PLANE, 0, 0, axis_index_groups=groups, tiled=True)  45.2 us
    all_to_all x4, starting transfers between devices, swap_all(): return lax.all_to_all(value, axes, 0, 0, tiled=True)  25.3 us
    ppermute x16, waiting for transfers between devices, swapped(): return lax.ppermute(part, axes, pairs + [(j, i) for i, j in pairs])  10.7 us
    all_to_all x1, blocking collectives, swap_all(): return lax.all_to_all(value, axes, 0, 0, tiled=True)  8.71 us
    pallas_call x8, Pallas kernels, call(): pl.pallas_call(kernel, out_shape=out, in_specs=[SMEM] * scalars + [VMEM]...  8.69 us
    all_to_all x4, waiting for transfers between devices, swap_all(): return lax.all_to_all(value, axes, 0, 0, tiled=True)  5.01 us
    pallas_call x1, Pallas kernels, start(): pl.pallas_call(start_kernel, out_shape=[jax.ShapeDtypeStruct(shape, f32)...  4.12 us
  transfers between devices with their start and end apart: 21, of which 5 were waited for; matrix products, arithmetic and copies ran while one was open for 0% of the time, Pallas kernels for 0%

profile of v5, /device:TPU:1, one launch (start us, length us, event | category | flops | bytes accessed | tf_op | source)
XLA Modules:
  0.0 170.1 jit_solution(7772875109851861466)
XLA Ops:
  0.6 4.1 %shard_map.76 = (f32[136,256]{1,0:T(8,128)}, f32[64,256]{1,0:T(8,128)}, f32[64,128]{1,0:T(8,128)}, f32[64,128]{1,0:T(8,128)}, f32[4,256,128]{2,1,0:T(8,128)}) custom-call(s32[1]{0:T(128)} %bitcast.core, f32[1,64]{1,0:T(1,128)} %bitcast.15, bf16[256,128]{1,0:T(8,128)(2,1)} %bitcast.13, s32[2,128]{1,0:T(2,128)} %bitcast.14, f32[64,128]{1,0:T(8,128)} %means.1, ...), custom_call_target="tpu_custom_call" | custom-call | flops 536870912 | bytes 2097152 | tf_op jit(solution)/shard_map/pallas_call | solution.py:137
  4.8 4.9 %all-to-all-start = ((f32[4,256,128]{2,1,0:T(8,128)}), f32[4,256,128]{2,1,0:T(8,128)S(1)}, u32[]{:S(2)}, u32[]{:S(2)}) async-start(f32[4,256,128]{2,1,0:T(8,128)} %get-tuple-element.44), calls=%async_computation | async-start | bytes 1048576 | tf_op jit(solution)/shard_map/all_to_all | solution.py:388
  9.6 0.7 collective-permute-start.1
  10.3 12.2 %collective-permute-start = (f32[64,256]{1,0:T(8,128)}, f32[64,256]{1,0:T(8,128)S(1)}, u32[]{:S(2)}, u32[]{:S(2)}) collective-permute-start(f32[64,256]{1,0:T(8,128)} %get-tuple-element.37), channel_id=1, source_target_pairs={{0,32},{64,96},{128,160},{192,224},{256,288},{320,352},{384,416},{... | collective-permute-start | bytes 196616 | tf_op jit(solution)/shard_map/ppermute | solution.py:207
  22.5 3.4 %collective-permute-start.2 = (f32[64,128]{1,0:T(8,128)}, f32[64,128]{1,0:T(8,128)S(1)}, u32[]{:S(2)}, u32[]{:S(2)}) collective-permute-start(f32[64,128]{1,0:T(8,128)} %get-tuple-element.38), channel_id=1, source_target_pairs={{0,1},{2,3},{4,5},{6,7},{8,9},{10,11},{12,13},{14,15},{16,17},{18,... | collective-permute-start | bytes 98312 | tf_op jit(solution)/shard_map/ppermute | solution.py:207
  25.9 3.1 %collective-permute-start.3 = (f32[64,128]{1,0:T(8,128)}, f32[64,128]{1,0:T(8,128)S(1)}, u32[]{:S(2)}, u32[]{:S(2)}) collective-permute-start(f32[64,128]{1,0:T(8,128)} %get-tuple-element.39), channel_id=1, source_target_pairs={{1,2},{3,4},{5,6},{7,8},{9,10},{11,12},{13,14},{15,16},{17,18},{19... | collective-permute-start | bytes 98312 | tf_op jit(solution)/shard_map/ppermute | solution.py:207
  29.0 0.0 collective-permute-done.2.near_in
  29.0 2.3 %collective-permute-done.3.far_in = f32[64,128]{1,0:T(8,128)S(1)} collective-permute-done((f32[64,128]{1,0:T(8,128)}, f32[64,128]{1,0:T(8,128)S(1)}, u32[]{:S(2)}, u32[]{:S(2)}) %collective-permute-start.3) | collective-permute-done | bytes 32800 | tf_op jit(solution)/shard_map/ppermute | solution.py:207
  31.3 0.0 collective-permute-done.1.slab_odd
  31.3 0.0 collective-permute-done.slab_even
  31.3 0.0 copy-start
  31.3 0.9 copy-done
  32.2 0.1 shard_map.77
  32.4 0.0 all-to-all-done.mine
  32.4 1.9 %collective-permute-start.8 = (f32[4,256,128]{2,1,0:T(8,128)S(1)}, f32[4,256,128]{2,1,0:T(8,128)S(1)}, u32[]{:S(2)}, u32[]{:S(2)}) collective-permute-start(f32[4,256,128]{2,1,0:T(8,128)S(1)} %all-to-all-done.mine), channel_id=1, source_target_pairs={{0,1},{1,0},{2,3},{3,2},{4,5},{5,4},{6,7},{7,6},{8,9},{9,8},{10,11... | collective-permute-start | bytes 1572872 | tf_op jit(solution)/shard_map/ppermute | solution.py:413
  34.3 0.7 collective-permute-start.5
  35.0 6.1 %collective-permute-start.4 = (f32[64,256]{1,0:T(8,128)S(1)}, f32[64,256]{1,0:T(8,128)S(1)}, u32[]{:S(2)}, u32[]{:S(2)}) collective-permute-start(f32[64,256]{1,0:T(8,128)S(1)} %get-tuple-element.45.resp), channel_id=1, source_target_pairs={{0,32},{64,96},{128,160},{192,224},{256,288},{320,352},{384,416},{... | collective-permute-start | bytes 196616 | tf_op jit(solution)/shard_map/ppermute | solution.py:207
  41.1 3.0 %collective-permute-start.6 = (f32[64,128]{1,0:T(8,128)S(1)}, f32[64,128]{1,0:T(8,128)S(1)}, u32[]{:S(2)}, u32[]{:S(2)}) collective-permute-start(f32[64,128]{1,0:T(8,128)S(1)} %get-tuple-element.46), channel_id=1, source_target_pairs={{0,1},{2,3},{4,5},{6,7},{8,9},{10,11},{12,13},{14,15},{16,17},{18,... | collective-permute-start | bytes 98312 | tf_op jit(solution)/shard_map/ppermute | solution.py:207
  44.0 2.0 %collective-permute-start.7 = (f32[64,128]{1,0:T(8,128)S(1)}, f32[64,128]{1,0:T(8,128)S(1)}, u32[]{:S(2)}, u32[]{:S(2)}) collective-permute-start(f32[64,128]{1,0:T(8,128)S(1)} %get-tuple-element.47), channel_id=1, source_target_pairs={{1,2},{3,4},{5,6},{7,8},{9,10},{11,12},{13,14},{15,16},{17,18},{19... | collective-permute-start | bytes 98312 | tf_op jit(solution)/shard_map/ppermute | solution.py:207
  46.1 0.0 collective-permute-done.6.near_in
  46.1 3.2 %collective-permute-done.7.far_in = f32[64,128]{1,0:T(8,128)S(1)} collective-permute-done((f32[64,128]{1,0:T(8,128)S(1)}, f32[64,128]{1,0:T(8,128)S(1)}, u32[]{:S(2)}, u32[]{:S(2)}) %collective-permute-start.7) | collective-permute-done | bytes 32800 | tf_op jit(solution)/shard_map/ppermute | solution.py:207
  49.3 0.0 collective-permute-done.5.slab_odd
  49.3 0.0 collective-permute-done.4.slab_even
  49.3 0.1 shard_map.78
  49.4 0.0 collective-permute-done.8.theirs
  49.4 8.7 %all_to_all.40.resp = f32[8,8,256]{2,1,0:T(8,128)S(1)} all-to-all(f32[8,8,256]{2,1,0:T(8,128)S(1)} %bitcast.12), channel_id=1, replica_groups=mesh['x1'=2,'x0'=2,'z2'=2,'z1'=2,'z0'=2,'y2'=2,'y1'=2,'y0'=2,'core'=2] {..., dimensions={0} | all-to-all | bytes 131072 | tf_op jit(solution)/shard_map/all_to_all | solution.py:388
  58.2 1.6 shard_map.79
  59.7 19.1 %all_to_all.41.packets = f32[8,72,128]{2,1,0:T(8,128)S(1)} all-to-all(f32[8,72,128]{2,1,0:T(8,128)S(1)} %get-tuple-element.51), channel_id=1, replica_groups={{0,2,4,6,8,10,12,14},{16,18,20,22,24,26,28,30},{32,34,36,38,40,42,44,46..., dimensions={0} | all-to-all | bytes 589824 | tf_op jit(solution)/shard_map/all_to_all | solution.py:392
  78.9 14.0 %all_to_all.42.packets = f32[8,72,128]{2,1,0:T(8,128)S(1)} all-to-all(f32[8,72,128]{2,1,0:T(8,128)S(1)} %shard_map.80), channel_id=1, replica_groups={{0,16,32,48,64,80,96,112},{2,18,34,50,66,82,98,114},{4,20,36,52,68,84,1..., dimensions={0} | all-to-all | bytes 589824 | tf_op jit(solution)/shard_map/all_to_all | solution.py:392
  92.9 3.8 %shard_map.81 = f32[8,72,128]{2,1,0:T(8,128)S(1)} custom-call(f32[8,72,128]{2,1,0:T(8,128)S(1)} %all_to_all.42.packets), custom_call_target="tpu_custom_call" | custom-call | flops 134217728 | bytes 1048576 | tf_op jit(solution)/shard_map/pallas_call | solution.py:36
  96.7 12.0 %all_to_all.43.packets = f32[8,72,128]{2,1,0:T(8,128)S(1)} all-to-all(f32[8,72,128]{2,1,0:T(8,128)S(1)} %shard_map.81), channel_id=1, replica_groups={{0,2,4,6,8,10,12,14},{16,18,20,22,24,26,28,30},{32,34,36,38,40,42,44,46..., dimensions={0} | all-to-all | bytes 589824 | tf_op jit(solution)/shard_map/all_to_all | solution.py:392
  108.8 2.1 %shard_map.82 = f32[8,8,384]{2,1,0:T(8,128)} custom-call(f32[8,72,128]{2,1,0:T(8,128)S(1)} %all_to_all.43.packets, bf16[8,128,256]{2,1,0:T(8,128)(2,1)S(1)} %get-tuple-element.52.turned), custom_call_target="tpu_custom_call" | custom-call | flops 536870912 | bytes 1048576 | tf_op jit(solution)/shard_map/pallas_call | solution.py:36
  110.8 8.0 %all-to-all-start.5 = ((f32[8,8,384]{2,1,0:T(8,128)}), f32[8,8,384]{2,1,0:T(8,128)S(1)}, u32[]{:S(2)}, u32[]{:S(2)}) async-start(f32[8,8,384]{2,1,0:T(8,128)} %shard_map.82), calls=%async_computation.5 | async-start | bytes 196608 | tf_op jit(solution)/shard_map/all_to_all | solution.py:388
  118.9 5.0 %all-to-all-done.5 = f32[8,8,384]{2,1,0:T(8,128)S(1)} async-done(((f32[8,8,384]{2,1,0:T(8,128)}), f32[8,8,384]{2,1,0:T(8,128)S(1)}, u32[]{:S(2)}, u32[]{:S(2)}) %all-to-all-start.5) | async-done | bytes 98336 | tf_op jit(solution)/shard_map/all_to_all | solution.py:388
  123.9 0.8 shard_map.83
  124.7 4.1 %all-to-all-start.6 = ((f32[16,16,128]{2,1,0:T(8,128)}), f32[16,16,128]{2,1,0:T(8,128)S(1)}, u32[]{:S(2)}, u32[]{:S(2)}) async-start(f32[16,16,128]{2,1,0:T(8,128)} %get-tuple-element.55), calls=%async_computation.6 | async-start | bytes 262144 | tf_op jit(solution)/shard_map/all_to_all | solution.py:388
  128.8 0.7 collective-permute-start.10
  129.4 3.7 %collective-permute-start.9 = (f32[64,256]{1,0:T(8,128)S(1)}, f32[64,256]{1,0:T(8,128)S(1)}, u32[]{:S(2)}, u32[]{:S(2)}) collective-permute-start(f32[64,256]{1,0:T(8,128)S(1)} %get-tuple-element.56), channel_id=1, source_target_pairs={{0,32},{64,96},{128,160},{192,224},{256,288},{320,352},{384,416},{... | collective-permute-start | bytes 196616 | tf_op jit(solution)/shard_map/ppermute | solution.py:207
  133.2 2.7 %collective-permute-start.11 = (f32[64,128]{1,0:T(8,128)S(1)}, f32[64,128]{1,0:T(8,128)S(1)}, u32[]{:S(2)}, u32[]{:S(2)}) collective-permute-start(f32[64,128]{1,0:T(8,128)S(1)} %get-tuple-element.57), channel_id=1, source_target_pairs={{0,1},{2,3},{4,5},{6,7},{8,9},{10,11},{12,13},{14,15},{16,17},{18,... | collective-permute-start | bytes 98312 | tf_op jit(solution)/shard_map/ppermute | solution.py:207
  135.9 3.3 %collective-permute-start.12 = (f32[64,128]{1,0:T(8,128)S(1)}, f32[64,128]{1,0:T(8,128)S(1)}, u32[]{:S(2)}, u32[]{:S(2)}) collective-permute-start(f32[64,128]{1,0:T(8,128)S(1)} %get-tuple-element.58), channel_id=1, source_target_pairs={{1,2},{3,4},{5,6},{7,8},{9,10},{11,12},{13,14},{15,16},{17,18},{19... | collective-permute-start | bytes 98312 | tf_op jit(solution)/shard_map/ppermute | solution.py:207
  139.2 0.0 collective-permute-done.11.near_in
  139.2 1.9 %collective-permute-done.12.far_in = f32[64,128]{1,0:T(8,128)S(1)} collective-permute-done((f32[64,128]{1,0:T(8,128)S(1)}, f32[64,128]{1,0:T(8,128)S(1)}, u32[]{:S(2)}, u32[]{:S(2)}) %collective-permute-start.12) | collective-permute-done | bytes 32800 | tf_op jit(solution)/shard_map/ppermute | solution.py:207
  141.1 0.0 collective-permute-done.10.slab_odd
  141.1 0.0 collective-permute-done.9.slab_even
  141.1 0.1 shard_map.84
  141.3 0.0 all-to-all-done.6
  141.3 0.7 broadcast_in_dim.2
  142.0 8.2 %all-to-all-start.7 = ((f32[32,8,128]{2,1,0:T(8,128)}), f32[32,8,128]{2,1,0:T(8,128)S(1)}, u32[]{:S(2)}, u32[]{:S(2)}) async-start(f32[32,8,128]{2,1,0:T(8,128)} %broadcast_in_dim.2), calls=%async_computation.7 | async-start | bytes 262144 | tf_op jit(solution)/shard_map/all_to_all | solution.py:388
  150.2 0.7 collective-permute-start.14
  150.9 8.6 %collective-permute-start.13 = (f32[64,256]{1,0:T(8,128)S(1)}, f32[64,256]{1,0:T(8,128)S(1)}, u32[]{:S(2)}, u32[]{:S(2)}) collective-permute-start(f32[64,256]{1,0:T(8,128)S(1)} %get-tuple-element.62.resp), channel_id=1, source_target_pairs={{0,32},{64,96},{128,160},{192,224},{256,288},{320,352},{384,416},{... | collective-permute-start | bytes 196616 | tf_op jit(solution)/shard_map/ppermute | solution.py:207
  159.5 4.5 %collective-permute-start.15 = (f32[64,128]{1,0:T(8,128)S(1)}, f32[64,128]{1,0:T(8,128)S(1)}, u32[]{:S(2)}, u32[]{:S(2)}) collective-permute-start(f32[64,128]{1,0:T(8,128)S(1)} %get-tuple-element.63), channel_id=1, source_target_pairs={{0,1},{2,3},{4,5},{6,7},{8,9},{10,11},{12,13},{14,15},{16,17},{18,... | collective-permute-start | bytes 98312 | tf_op jit(solution)/shard_map/ppermute | solution.py:207
  164.0 1.9 %collective-permute-start.16 = (f32[64,128]{1,0:T(8,128)S(1)}, f32[64,128]{1,0:T(8,128)S(1)}, u32[]{:S(2)}, u32[]{:S(2)}) collective-permute-start(f32[64,128]{1,0:T(8,128)S(1)} %get-tuple-element.64), channel_id=1, source_target_pairs={{1,2},{3,4},{5,6},{7,8},{9,10},{11,12},{13,14},{15,16},{17,18},{19... | collective-permute-start | bytes 98312 | tf_op jit(solution)/shard_map/ppermute | solution.py:207
  165.9 0.0 collective-permute-done.15.near_in
  165.9 3.3 %collective-permute-done.16.far_in = f32[64,128]{1,0:T(8,128)S(1)} collective-permute-done((f32[64,128]{1,0:T(8,128)S(1)}, f32[64,128]{1,0:T(8,128)S(1)}, u32[]{:S(2)}, u32[]{:S(2)}) %collective-permute-start.16) | collective-permute-done | bytes 32800 | tf_op jit(solution)/shard_map/ppermute | solution.py:207
  169.2 0.0 collective-permute-done.14.slab_odd
  169.2 0.0 collective-permute-done.13.slab_even
  169.2 0.0 all-to-all-done.7.totals
  169.2 0.8 shard_map.85
  (3 shorter events, 0.1 us)
Async XLA Ops:
  4.8 27.6 %all-to-all-start = ((f32[4,256,128]{2,1,0:T(8,128)}), f32[4,256,128]{2,1,0:T(8,128)S(1)}, u32[]{:S(2)}, u32[]{:S(2)}) async-start(f32[4,256,128]{2,1,0:T(8,128)} %get-tuple-element.44), calls=%async_computation | async-start | bytes 1048576 | tf_op jit(solution)/shard_map/all_to_all | solution.py:388
  9.6 21.7 %collective-permute-start.1 = (f32[64,256]{1,0:T(8,128)}, f32[64,256]{1,0:T(8,128)S(1)}, u32[]{:S(2)}, u32[]{:S(2)}) collective-permute-start(f32[64,256]{1,0:T(8,128)} %get-tuple-element.37), channel_id=1, source_target_pairs={{32,64},{96,128},{160,192},{224,256},{288,320},{352,384},{416,448}... | collective-permute-start | bytes 196616 | tf_op jit(solution)/shard_map/ppermute | solution.py:207
  10.3 21.1 %collective-permute-start = (f32[64,256]{1,0:T(8,128)}, f32[64,256]{1,0:T(8,128)S(1)}, u32[]{:S(2)}, u32[]{:S(2)}) collective-permute-start(f32[64,256]{1,0:T(8,128)} %get-tuple-element.37), channel_id=1, source_target_pairs={{0,32},{64,96},{128,160},{192,224},{256,288},{320,352},{384,416},{... | collective-permute-start | bytes 196616 | tf_op jit(solution)/shard_map/ppermute | solution.py:207
  22.5 6.5 %collective-permute-start.2 = (f32[64,128]{1,0:T(8,128)}, f32[64,128]{1,0:T(8,128)S(1)}, u32[]{:S(2)}, u32[]{:S(2)}) collective-permute-start(f32[64,128]{1,0:T(8,128)} %get-tuple-element.38), channel_id=1, source_target_pairs={{0,1},{2,3},{4,5},{6,7},{8,9},{10,11},{12,13},{14,15},{16,17},{18,... | collective-permute-start | bytes 98312 | tf_op jit(solution)/shard_map/ppermute | solution.py:207
  25.9 5.4 %collective-permute-start.3 = (f32[64,128]{1,0:T(8,128)}, f32[64,128]{1,0:T(8,128)S(1)}, u32[]{:S(2)}, u32[]{:S(2)}) collective-permute-start(f32[64,128]{1,0:T(8,128)} %get-tuple-element.39), channel_id=1, source_target_pairs={{1,2},{3,4},{5,6},{7,8},{9,10},{11,12},{13,14},{15,16},{17,18},{19... | collective-permute-start | bytes 98312 | tf_op jit(solution)/shard_map/ppermute | solution.py:207
  31.3 0.9 copy-start
  32.4 17.0 %collective-permute-start.8 = (f32[4,256,128]{2,1,0:T(8,128)S(1)}, f32[4,256,128]{2,1,0:T(8,128)S(1)}, u32[]{:S(2)}, u32[]{:S(2)}) collective-permute-start(f32[4,256,128]{2,1,0:T(8,128)S(1)} %all-to-all-done.mine), channel_id=1, source_target_pairs={{0,1},{1,0},{2,3},{3,2},{4,5},{5,4},{6,7},{7,6},{8,9},{9,8},{10,11... | collective-permute-start | bytes 1572872 | tf_op jit(solution)/shard_map/ppermute | solution.py:413
  34.3 14.9 %collective-permute-start.5 = (f32[64,256]{1,0:T(8,128)S(1)}, f32[64,256]{1,0:T(8,128)S(1)}, u32[]{:S(2)}, u32[]{:S(2)}) collective-permute-start(f32[64,256]{1,0:T(8,128)S(1)} %get-tuple-element.45.resp), channel_id=1, source_target_pairs={{32,64},{96,128},{160,192},{224,256},{288,320},{352,384},{416,448}... | collective-permute-start | bytes 196616 | tf_op jit(solution)/shard_map/ppermute | solution.py:207
  35.0 14.3 %collective-permute-start.4 = (f32[64,256]{1,0:T(8,128)S(1)}, f32[64,256]{1,0:T(8,128)S(1)}, u32[]{:S(2)}, u32[]{:S(2)}) collective-permute-start(f32[64,256]{1,0:T(8,128)S(1)} %get-tuple-element.45.resp), channel_id=1, source_target_pairs={{0,32},{64,96},{128,160},{192,224},{256,288},{320,352},{384,416},{... | collective-permute-start | bytes 196616 | tf_op jit(solution)/shard_map/ppermute | solution.py:207
  41.1 5.0 %collective-permute-start.6 = (f32[64,128]{1,0:T(8,128)S(1)}, f32[64,128]{1,0:T(8,128)S(1)}, u32[]{:S(2)}, u32[]{:S(2)}) collective-permute-start(f32[64,128]{1,0:T(8,128)S(1)} %get-tuple-element.46), channel_id=1, source_target_pairs={{0,1},{2,3},{4,5},{6,7},{8,9},{10,11},{12,13},{14,15},{16,17},{18,... | collective-permute-start | bytes 98312 | tf_op jit(solution)/shard_map/ppermute | solution.py:207
  44.0 5.2 %collective-permute-start.7 = (f32[64,128]{1,0:T(8,128)S(1)}, f32[64,128]{1,0:T(8,128)S(1)}, u32[]{:S(2)}, u32[]{:S(2)}) collective-permute-start(f32[64,128]{1,0:T(8,128)S(1)} %get-tuple-element.47), channel_id=1, source_target_pairs={{1,2},{3,4},{5,6},{7,8},{9,10},{11,12},{13,14},{15,16},{17,18},{19... | collective-permute-start | bytes 98312 | tf_op jit(solution)/shard_map/ppermute | solution.py:207
  110.8 13.0 %all-to-all-start.5 = ((f32[8,8,384]{2,1,0:T(8,128)}), f32[8,8,384]{2,1,0:T(8,128)S(1)}, u32[]{:S(2)}, u32[]{:S(2)}) async-start(f32[8,8,384]{2,1,0:T(8,128)} %shard_map.82), calls=%async_computation.5 | async-start | bytes 196608 | tf_op jit(solution)/shard_map/all_to_all | solution.py:388
  124.7 16.6 %all-to-all-start.6 = ((f32[16,16,128]{2,1,0:T(8,128)}), f32[16,16,128]{2,1,0:T(8,128)S(1)}, u32[]{:S(2)}, u32[]{:S(2)}) async-start(f32[16,16,128]{2,1,0:T(8,128)} %get-tuple-element.55), calls=%async_computation.6 | async-start | bytes 262144 | tf_op jit(solution)/shard_map/all_to_all | solution.py:388
  128.8 12.3 %collective-permute-start.10 = (f32[64,256]{1,0:T(8,128)S(1)}, f32[64,256]{1,0:T(8,128)S(1)}, u32[]{:S(2)}, u32[]{:S(2)}) collective-permute-start(f32[64,256]{1,0:T(8,128)S(1)} %get-tuple-element.56), channel_id=1, source_target_pairs={{32,64},{96,128},{160,192},{224,256},{288,320},{352,384},{416,448}... | collective-permute-start | bytes 196616 | tf_op jit(solution)/shard_map/ppermute | solution.py:207
  129.4 11.7 %collective-permute-start.9 = (f32[64,256]{1,0:T(8,128)S(1)}, f32[64,256]{1,0:T(8,128)S(1)}, u32[]{:S(2)}, u32[]{:S(2)}) collective-permute-start(f32[64,256]{1,0:T(8,128)S(1)} %get-tuple-element.56), channel_id=1, source_target_pairs={{0,32},{64,96},{128,160},{192,224},{256,288},{320,352},{384,416},{... | collective-permute-start | bytes 196616 | tf_op jit(solution)/shard_map/ppermute | solution.py:207
  133.2 6.0 %collective-permute-start.11 = (f32[64,128]{1,0:T(8,128)S(1)}, f32[64,128]{1,0:T(8,128)S(1)}, u32[]{:S(2)}, u32[]{:S(2)}) collective-permute-start(f32[64,128]{1,0:T(8,128)S(1)} %get-tuple-element.57), channel_id=1, source_target_pairs={{0,1},{2,3},{4,5},{6,7},{8,9},{10,11},{12,13},{14,15},{16,17},{18,... | collective-permute-start | bytes 98312 | tf_op jit(solution)/shard_map/ppermute | solution.py:207
  135.9 5.2 %collective-permute-start.12 = (f32[64,128]{1,0:T(8,128)S(1)}, f32[64,128]{1,0:T(8,128)S(1)}, u32[]{:S(2)}, u32[]{:S(2)}) collective-permute-start(f32[64,128]{1,0:T(8,128)S(1)} %get-tuple-element.58), channel_id=1, source_target_pairs={{1,2},{3,4},{5,6},{7,8},{9,10},{11,12},{13,14},{15,16},{17,18},{19... | collective-permute-start | bytes 98312 | tf_op jit(solution)/shard_map/ppermute | solution.py:207
  142.0 27.3 %all-to-all-start.7 = ((f32[32,8,128]{2,1,0:T(8,128)}), f32[32,8,128]{2,1,0:T(8,128)S(1)}, u32[]{:S(2)}, u32[]{:S(2)}) async-start(f32[32,8,128]{2,1,0:T(8,128)} %broadcast_in_dim.2), calls=%async_computation.7 | async-start | bytes 262144 | tf_op jit(solution)/shard_map/all_to_all | solution.py:388
  150.2 19.0 %collective-permute-start.14 = (f32[64,256]{1,0:T(8,128)S(1)}, f32[64,256]{1,0:T(8,128)S(1)}, u32[]{:S(2)}, u32[]{:S(2)}) collective-permute-start(f32[64,256]{1,0:T(8,128)S(1)} %get-tuple-element.62.resp), channel_id=1, source_target_pairs={{32,64},{96,128},{160,192},{224,256},{288,320},{352,384},{416,448}... | collective-permute-start | bytes 196616 | tf_op jit(solution)/shard_map/ppermute | solution.py:207
  150.9 18.3 %collective-permute-start.13 = (f32[64,256]{1,0:T(8,128)S(1)}, f32[64,256]{1,0:T(8,128)S(1)}, u32[]{:S(2)}, u32[]{:S(2)}) collective-permute-start(f32[64,256]{1,0:T(8,128)S(1)} %get-tuple-element.62.resp), channel_id=1, source_target_pairs={{0,32},{64,96},{128,160},{192,224},{256,288},{320,352},{384,416},{... | collective-permute-start | bytes 196616 | tf_op jit(solution)/shard_map/ppermute | solution.py:207
  159.5 6.4 %collective-permute-start.15 = (f32[64,128]{1,0:T(8,128)S(1)}, f32[64,128]{1,0:T(8,128)S(1)}, u32[]{:S(2)}, u32[]{:S(2)}) collective-permute-start(f32[64,128]{1,0:T(8,128)S(1)} %get-tuple-element.63), channel_id=1, source_target_pairs={{0,1},{2,3},{4,5},{6,7},{8,9},{10,11},{12,13},{14,15},{16,17},{18,... | collective-permute-start | bytes 98312 | tf_op jit(solution)/shard_map/ppermute | solution.py:207
  164.0 5.2 %collective-permute-start.16 = (f32[64,128]{1,0:T(8,128)S(1)}, f32[64,128]{1,0:T(8,128)S(1)}, u32[]{:S(2)}, u32[]{:S(2)}) collective-permute-start(f32[64,128]{1,0:T(8,128)S(1)} %get-tuple-element.64), channel_id=1, source_target_pairs={{1,2},{3,4},{5,6},{7,8},{9,10},{11,12},{13,14},{15,16},{17,18},{19... | collective-permute-start | bytes 98312 | tf_op jit(solution)/shard_map/ppermute | solution.py:207

commit v6 on v5

--- a/solution.py
+++ b/solution.py
@@ -153,7 +153,7 @@
     )(core, weights, flat, tissue, means, whiten)
 
 
-def swept(core, state, resp, slab_even, slab_odd, near_in, far_in):
+def swept(core, state, resp, slab_even, slab_odd, far_in, near_in):
     count = resp.shape[0]
     lane = iotas((count, WIDTH))[1]
     rows = (resp[:, :WIDTH], resp[:, WIDTH:])
@@ -169,25 +169,36 @@
     return normalise(scores + BETA_POTTS * field) * mask
 
 
-def first_kernel(core, state, slab_even, slab_odd, near_in, far_in, out, near, far):
+def first_kernel(core, state, slab_even, slab_odd, far_in, near_in, out, near, far):
     count = out.shape[0]
     resp = state[count : 2 * count]
-    put(core[0], swept(core, state, resp, slab_even, slab_odd, near_in, far_in), out, near, far)
-
-
-def early_kernel(core, state, slab_even, slab_odd, near_in, far_in, out, near, far, kept):
+    put(core[0], swept(core, state, resp, slab_even, slab_odd, far_in, near_in), out, near, far)
+
+
+def early_kernel(core, state, slab_even, slab_odd, far_in, near_in, out, near, far, kept):
     count = out.shape[0]
     kept[:count] = state[:count]
     kept[count:] = state[2 * count :]
-    first_kernel(core, state, slab_even, slab_odd, near_in, far_in, out, near, far)
-
-
-def later_kernel(core, state, resp, slab_even, slab_odd, near_in, far_in, out):
-    out[...] = swept(core, state, resp[...], slab_even, slab_odd, near_in, far_in)
-
-
-def last_kernel(core, state, resp, slab_even, slab_odd, near_in, far_in, totals, out, score):
-    result = swept(core, state, resp[...], slab_even, slab_odd, near_in, far_in)
+    first_kernel(core, state, slab_even, slab_odd, far_in, near_in, out, near, far)
+
+
+def middle_kernel(
+    core, state, slab_even, slab_odd, far_in, near_in, totals, out, near, far, sums
+):
+    total = totals[0]
+    for n in range(1, totals.shape[0]):
+        total = total + totals[n]
+    for n in range(sums.shape[0]):
+        sums[n] = total[: sums.shape[1]]
+    first_kernel(core, state, slab_even, slab_odd, far_in, near_in, out, near, far)
+
+
+def later_kernel(core, state, resp, slab_even, slab_odd, far_in, near_in, out):
+    out[...] = swept(core, state, resp[...], slab_even, slab_odd, far_in, near_in)
+
+
+def last_kernel(core, state, resp, slab_even, slab_odd, far_in, near_in, totals, out, score):
+    result = swept(core, state, resp[...], slab_even, slab_odd, far_in, near_in)
     out[:, 0, :] = result[:, :WIDTH]
     out[:, 1, :] = result[:, WIDTH:]
     total = totals[0]
@@ -209,7 +220,7 @@
 
 def halos(resp, near, far):
     return (
-        swapped(resp, SLAB, 0), swapped(resp, SLAB, 1), swapped(near, TILE, 0), swapped(far, TILE, 1)
+        swapped(resp, SLAB, 0), swapped(resp, SLAB, 1), swapped(far, TILE, 1), swapped(near, TILE, 0)
     )
 
 
@@ -278,7 +289,8 @@
         ]
         scale = jnp.broadcast_to(cols[0][:1], (STEP, WIDTH))
         for j in range(STEP - 1):
-            inverse = 1.0 / cols[j][j : j + 1]
+            inverse = lax.rsqrt(cols[j][j : j + 1])
+            inverse = inverse * inverse
             mult = jnp.where(sub > j, cols[j] * inverse, 0.0)
             for l in range(j + 1, STEP):
                 cols[l] = cols[l] - mult * jnp.broadcast_to(cols[l][j : j + 1], (STEP, WIDTH))
@@ -438,11 +450,10 @@
         core, tile, part, kept, total, scalars=2,
     )
     totals = swap_all(totals, ROUND[0])
-    resp, near, far = call(
-        first_kernel, resp_shapes, core, state, *halos(resp, near, far), scalars=1
-    )
-    totals, resp, near, far = lax.optimization_barrier((totals, resp, near, far))
-    totals = jnp.broadcast_to(jnp.sum(totals, axis=0)[None, :8], (sizes[1], 8, WIDTH))
+    resp, near, far, totals = call(
+        middle_kernel, resp_shapes + [((sizes[1], 8, WIDTH), f32)],
+        core, state, *halos(resp, near, far), totals, scalars=1,
+    )
     totals = swap_all(totals, ROUND[1])
     sides = halos(resp, near, far)
     resp_final, score = pl.pallas_call(

time: 172 us -> 164 us (0.953)
  waiting for transfers between devices: 15.7 us -> 9.9 us
    ppermute x16, waiting for transfers between devices: 10.7 us -> 4.89 us  [swapped(): return lax.ppermute(part, axes, pairs + [(j, i) for i, j in pairs])]
    all_to_all x3, blocking collectives: 45.2 us -> 43.4 us  [swap_lines(): lax.all_to_all(value, PLANE, 0, 0, axis_index_groups=groups, tiled=True)]
where the time goes in v6:
time: 164 us; the launch traced here: 163 us
  starting transfers between devices  84.1 us (51%)
  blocking collectives  53 us (32%)
  Pallas kernels  14.3 us (9%)
  waiting for transfers between devices  9.9 us (6%)
    ppermute x16, starting transfers between devices, swapped(): return lax.ppermute(part, axes, pairs + [(j, i) for i, j in pairs])  56.2 us
    all_to_all x3, blocking collectives, swap_lines(): lax.all_to_all(value, PLANE, 0, 0, axis_index_groups=groups, tiled=True)  43.4 us
    all_to_all x4, starting transfers between devices, swap_all(): return lax.all_to_all(value, axes, 0, 0, tiled=True)  25.8 us
    all_to_all x1, blocking collectives, swap_all(): return lax.all_to_all(value, axes, 0, 0, tiled=True)  9.61 us
    pallas_call x8, Pallas kernels, call(): pl.pallas_call(kernel, out_shape=out, in_specs=[SMEM] * scalars + [VMEM]...  9.31 us
    all_to_all x4, waiting for transfers between devices, swap_all(): return lax.all_to_all(value, axes, 0, 0, tiled=True)  5.01 us
    ppermute x16, waiting for transfers between devices, swapped(): return lax.ppermute(part, axes, pairs + [(j, i) for i, j in pairs])  4.89 us
    pallas_call x1, Pallas kernels, start(): pl.pallas_call(start_kernel, out_shape=[jax.ShapeDtypeStruct(shape, f32)...  4.12 us
  transfers between devices with their start and end apart: 21, of which 5 were waited for; matrix products, arithmetic and copies ran while one was open for 0% of the time, Pallas kernels for 0%

profile of v6, /device:TPU:1, one launch (start us, length us, event | category | flops | bytes accessed | tf_op | source)
XLA Modules:
  0.0 163.0 jit_solution(13392836595568770872)
XLA Ops:
  0.6 4.1 %shard_map.76 = (f32[136,256]{1,0:T(8,128)}, f32[64,256]{1,0:T(8,128)}, f32[64,128]{1,0:T(8,128)}, f32[64,128]{1,0:T(8,128)}, f32[4,256,128]{2,1,0:T(8,128)}) custom-call(s32[1]{0:T(128)} %bitcast.core, f32[1,64]{1,0:T(1,128)} %bitcast.15, bf16[256,128]{1,0:T(8,128)(2,1)} %bitcast.13, s32[2,128]{1,0:T(2,128)} %bitcast.14, f32[64,128]{1,0:T(8,128)} %means.1, ...), custom_call_target="tpu_custom_call" | custom-call | flops 536870912 | bytes 2097152 | tf_op jit(solution)/shard_map/pallas_call | solution.py:137
  4.8 4.9 %all-to-all-start = ((f32[4,256,128]{2,1,0:T(8,128)}), f32[4,256,128]{2,1,0:T(8,128)S(1)}, u32[]{:S(2)}, u32[]{:S(2)}) async-start(f32[4,256,128]{2,1,0:T(8,128)} %get-tuple-element.41), calls=%async_computation | async-start | bytes 1048576 | tf_op jit(solution)/shard_map/all_to_all | solution.py:400
  9.6 0.7 collective-permute-start.1
  10.3 12.2 %collective-permute-start = (f32[64,256]{1,0:T(8,128)}, f32[64,256]{1,0:T(8,128)S(1)}, u32[]{:S(2)}, u32[]{:S(2)}) collective-permute-start(f32[64,256]{1,0:T(8,128)} %get-tuple-element.34), channel_id=1, source_target_pairs={{0,32},{64,96},{128,160},{192,224},{256,288},{320,352},{384,416},{... | collective-permute-start | bytes 196616 | tf_op jit(solution)/shard_map/ppermute | solution.py:218
  22.5 4.6 %collective-permute-start.2 = (f32[64,128]{1,0:T(8,128)}, f32[64,128]{1,0:T(8,128)S(1)}, u32[]{:S(2)}, u32[]{:S(2)}) collective-permute-start(f32[64,128]{1,0:T(8,128)} %get-tuple-element.35), channel_id=1, source_target_pairs={{1,2},{3,4},{5,6},{7,8},{9,10},{11,12},{13,14},{15,16},{17,18},{19... | collective-permute-start | bytes 98312 | tf_op jit(solution)/shard_map/ppermute | solution.py:218
  27.1 1.9 %collective-permute-start.3 = (f32[64,128]{1,0:T(8,128)}, f32[64,128]{1,0:T(8,128)S(1)}, u32[]{:S(2)}, u32[]{:S(2)}) collective-permute-start(f32[64,128]{1,0:T(8,128)} %get-tuple-element.36), channel_id=1, source_target_pairs={{0,1},{2,3},{4,5},{6,7},{8,9},{10,11},{12,13},{14,15},{16,17},{18,... | collective-permute-start | bytes 98312 | tf_op jit(solution)/shard_map/ppermute | solution.py:218
  29.0 0.0 collective-permute-done.2.far_in
  29.0 1.4 collective-permute-done.3.near_in
  30.4 0.0 collective-permute-done.1.slab_odd
  30.4 0.0 collective-permute-done.slab_even
  30.4 0.0 copy-start
  30.4 0.9 copy-done
  31.3 0.1 shard_map.77
  31.4 0.0 all-to-all-done.mine
  31.5 2.1 %collective-permute-start.8 = (f32[4,256,128]{2,1,0:T(8,128)S(1)}, f32[4,256,128]{2,1,0:T(8,128)S(1)}, u32[]{:S(2)}, u32[]{:S(2)}) collective-permute-start(f32[4,256,128]{2,1,0:T(8,128)S(1)} %all-to-all-done.mine), channel_id=1, source_target_pairs={{0,1},{1,0},{2,3},{3,2},{4,5},{5,4},{6,7},{7,6},{8,9},{9,8},{10,11... | collective-permute-start | bytes 1572872 | tf_op jit(solution)/shard_map/ppermute | solution.py:425
  33.5 0.7 collective-permute-start.5
  34.2 5.0 %collective-permute-start.4 = (f32[64,256]{1,0:T(8,128)S(1)}, f32[64,256]{1,0:T(8,128)S(1)}, u32[]{:S(2)}, u32[]{:S(2)}) collective-permute-start(f32[64,256]{1,0:T(8,128)S(1)} %get-tuple-element.42.resp), channel_id=1, source_target_pairs={{0,32},{64,96},{128,160},{192,224},{256,288},{320,352},{384,416},{... | collective-permute-start | bytes 196616 | tf_op jit(solution)/shard_map/ppermute | solution.py:218
  39.2 4.0 %collective-permute-start.6 = (f32[64,128]{1,0:T(8,128)S(1)}, f32[64,128]{1,0:T(8,128)S(1)}, u32[]{:S(2)}, u32[]{:S(2)}) collective-permute-start(f32[64,128]{1,0:T(8,128)S(1)} %get-tuple-element.43), channel_id=1, source_target_pairs={{1,2},{3,4},{5,6},{7,8},{9,10},{11,12},{13,14},{15,16},{17,18},{19... | collective-permute-start | bytes 98312 | tf_op jit(solution)/shard_map/ppermute | solution.py:218
  43.2 1.9 %collective-permute-start.7 = (f32[64,128]{1,0:T(8,128)S(1)}, f32[64,128]{1,0:T(8,128)S(1)}, u32[]{:S(2)}, u32[]{:S(2)}) collective-permute-start(f32[64,128]{1,0:T(8,128)S(1)} %get-tuple-element.44), channel_id=1, source_target_pairs={{0,1},{2,3},{4,5},{6,7},{8,9},{10,11},{12,13},{14,15},{16,17},{18,... | collective-permute-start | bytes 98312 | tf_op jit(solution)/shard_map/ppermute | solution.py:218
  45.1 0.0 collective-permute-done.6.far_in
  45.1 1.2 collective-permute-done.7.near_in
  46.3 0.0 collective-permute-done.5.slab_odd
  46.3 0.0 collective-permute-done.4.slab_even
  46.3 0.1 shard_map.78
  46.5 0.0 collective-permute-done.8.theirs
  46.5 9.6 %all_to_all.40.resp = f32[8,8,256]{2,1,0:T(8,128)S(1)} all-to-all(f32[8,8,256]{2,1,0:T(8,128)S(1)} %bitcast.12), channel_id=1, replica_groups=mesh['x1'=2,'x0'=2,'z2'=2,'z1'=2,'z0'=2,'y2'=2,'y1'=2,'y0'=2,'core'=2] {..., dimensions={0} | all-to-all | bytes 131072 | tf_op jit(solution)/shard_map/all_to_all | solution.py:400
  56.1 1.6 shard_map.79
  57.7 17.1 %all_to_all.41.packets = f32[8,72,128]{2,1,0:T(8,128)S(1)} all-to-all(f32[8,72,128]{2,1,0:T(8,128)S(1)} %get-tuple-element.48), channel_id=1, replica_groups={{0,2,4,6,8,10,12,14},{16,18,20,22,24,26,28,30},{32,34,36,38,40,42,44,46..., dimensions={0} | all-to-all | bytes 589824 | tf_op jit(solution)/shard_map/all_to_all | solution.py:404
  74.8 14.2 %all_to_all.42.packets = f32[8,72,128]{2,1,0:T(8,128)S(1)} all-to-all(f32[8,72,128]{2,1,0:T(8,128)S(1)} %shard_map.80), channel_id=1, replica_groups={{0,16,32,48,64,80,96,112},{2,18,34,50,66,82,98,114},{4,20,36,52,68,84,1..., dimensions={0} | all-to-all | bytes 589824 | tf_op jit(solution)/shard_map/all_to_all | solution.py:404
  89.0 3.9 %shard_map.81 = f32[8,72,128]{2,1,0:T(8,128)S(1)} custom-call(f32[8,72,128]{2,1,0:T(8,128)S(1)} %all_to_all.42.packets), custom_call_target="tpu_custom_call" | custom-call | flops 134217728 | bytes 1048576 | tf_op jit(solution)/shard_map/pallas_call | solution.py:36
  92.9 12.0 %all_to_all.43.packets = f32[8,72,128]{2,1,0:T(8,128)S(1)} all-to-all(f32[8,72,128]{2,1,0:T(8,128)S(1)} %shard_map.81), channel_id=1, replica_groups={{0,2,4,6,8,10,12,14},{16,18,20,22,24,26,28,30},{32,34,36,38,40,42,44,46..., dimensions={0} | all-to-all | bytes 589824 | tf_op jit(solution)/shard_map/all_to_all | solution.py:404
  105.0 2.1 %shard_map.82 = f32[8,8,384]{2,1,0:T(8,128)} custom-call(f32[8,72,128]{2,1,0:T(8,128)S(1)} %all_to_all.43.packets, bf16[8,128,256]{2,1,0:T(8,128)(2,1)S(1)} %get-tuple-element.49.turned), custom_call_target="tpu_custom_call" | custom-call | flops 536870912 | bytes 1048576 | tf_op jit(solution)/shard_map/pallas_call | solution.py:36
  107.0 8.0 %all-to-all-start.5 = ((f32[8,8,384]{2,1,0:T(8,128)}), f32[8,8,384]{2,1,0:T(8,128)S(1)}, u32[]{:S(2)}, u32[]{:S(2)}) async-start(f32[8,8,384]{2,1,0:T(8,128)} %shard_map.82), calls=%async_computation.5 | async-start | bytes 196608 | tf_op jit(solution)/shard_map/all_to_all | solution.py:400
  115.1 5.0 %all-to-all-done.5 = f32[8,8,384]{2,1,0:T(8,128)S(1)} async-done(((f32[8,8,384]{2,1,0:T(8,128)}), f32[8,8,384]{2,1,0:T(8,128)S(1)}, u32[]{:S(2)}, u32[]{:S(2)}) %all-to-all-start.5) | async-done | bytes 98336 | tf_op jit(solution)/shard_map/all_to_all | solution.py:400
  120.1 0.8 shard_map.83
  120.9 4.1 %all-to-all-start.6 = ((f32[16,16,128]{2,1,0:T(8,128)}), f32[16,16,128]{2,1,0:T(8,128)S(1)}, u32[]{:S(2)}, u32[]{:S(2)}) async-start(f32[16,16,128]{2,1,0:T(8,128)} %get-tuple-element.55), calls=%async_computation.6 | async-start | bytes 262144 | tf_op jit(solution)/shard_map/all_to_all | solution.py:400
  125.0 0.7 collective-permute-start.10
  125.6 3.7 %collective-permute-start.9 = (f32[64,256]{1,0:T(8,128)S(1)}, f32[64,256]{1,0:T(8,128)S(1)}, u32[]{:S(2)}, u32[]{:S(2)}) collective-permute-start(f32[64,256]{1,0:T(8,128)S(1)} %get-tuple-element.52), channel_id=1, source_target_pairs={{0,32},{64,96},{128,160},{192,224},{256,288},{320,352},{384,416},{... | collective-permute-start | bytes 196616 | tf_op jit(solution)/shard_map/ppermute | solution.py:218
  129.4 4.1 %collective-permute-start.11 = (f32[64,128]{1,0:T(8,128)S(1)}, f32[64,128]{1,0:T(8,128)S(1)}, u32[]{:S(2)}, u32[]{:S(2)}) collective-permute-start(f32[64,128]{1,0:T(8,128)S(1)} %get-tuple-element.53), channel_id=1, source_target_pairs={{1,2},{3,4},{5,6},{7,8},{9,10},{11,12},{13,14},{15,16},{17,18},{19... | collective-permute-start | bytes 98312 | tf_op jit(solution)/shard_map/ppermute | solution.py:218
  133.5 1.9 %collective-permute-start.12 = (f32[64,128]{1,0:T(8,128)S(1)}, f32[64,128]{1,0:T(8,128)S(1)}, u32[]{:S(2)}, u32[]{:S(2)}) collective-permute-start(f32[64,128]{1,0:T(8,128)S(1)} %get-tuple-element.54), channel_id=1, source_target_pairs={{0,1},{2,3},{4,5},{6,7},{8,9},{10,11},{12,13},{14,15},{16,17},{18,... | collective-permute-start | bytes 98312 | tf_op jit(solution)/shard_map/ppermute | solution.py:218
  135.4 0.0 collective-permute-done.11.far_in
  135.4 1.2 collective-permute-done.12.near_in
  136.6 0.0 collective-permute-done.10.slab_odd
  136.6 0.0 collective-permute-done.9.slab_even
  136.6 0.0 all-to-all-done.6.totals
  136.6 0.7 shard_map.84
  137.3 8.8 %all-to-all-start.7 = ((f32[32,8,128]{2,1,0:T(8,128)}), f32[32,8,128]{2,1,0:T(8,128)S(1)}, u32[]{:S(2)}, u32[]{:S(2)}) async-start(f32[32,8,128]{2,1,0:T(8,128)} %get-tuple-element.59), calls=%async_computation.7 | async-start | bytes 262144 | tf_op jit(solution)/shard_map/all_to_all | solution.py:400
  146.1 0.7 collective-permute-start.14
  146.8 8.6 %collective-permute-start.13 = (f32[64,256]{1,0:T(8,128)S(1)}, f32[64,256]{1,0:T(8,128)S(1)}, u32[]{:S(2)}, u32[]{:S(2)}) collective-permute-start(f32[64,256]{1,0:T(8,128)S(1)} %get-tuple-element.56.resp), channel_id=1, source_target_pairs={{0,32},{64,96},{128,160},{192,224},{256,288},{320,352},{384,416},{... | collective-permute-start | bytes 196616 | tf_op jit(solution)/shard_map/ppermute | solution.py:218
  155.3 3.7 %collective-permute-start.15 = (f32[64,128]{1,0:T(8,128)S(1)}, f32[64,128]{1,0:T(8,128)S(1)}, u32[]{:S(2)}, u32[]{:S(2)}) collective-permute-start(f32[64,128]{1,0:T(8,128)S(1)} %get-tuple-element.57), channel_id=1, source_target_pairs={{1,2},{3,4},{5,6},{7,8},{9,10},{11,12},{13,14},{15,16},{17,18},{19... | collective-permute-start | bytes 98312 | tf_op jit(solution)/shard_map/ppermute | solution.py:218
  159.1 1.9 %collective-permute-start.16 = (f32[64,128]{1,0:T(8,128)S(1)}, f32[64,128]{1,0:T(8,128)S(1)}, u32[]{:S(2)}, u32[]{:S(2)}) collective-permute-start(f32[64,128]{1,0:T(8,128)S(1)} %get-tuple-element.58), channel_id=1, source_target_pairs={{0,1},{2,3},{4,5},{6,7},{8,9},{10,11},{12,13},{14,15},{16,17},{18,... | collective-permute-start | bytes 98312 | tf_op jit(solution)/shard_map/ppermute | solution.py:218
  161.0 0.0 collective-permute-done.15.far_in
  161.0 1.2 collective-permute-done.16.near_in
  162.2 0.0 collective-permute-done.14.slab_odd
  162.2 0.0 collective-permute-done.13.slab_even
  162.2 0.0 all-to-all-done.7.totals
  162.2 0.8 shard_map.85
  (1 shorter events, 0.0 us)
Async XLA Ops:
  4.8 26.7 %all-to-all-start = ((f32[4,256,128]{2,1,0:T(8,128)}), f32[4,256,128]{2,1,0:T(8,128)S(1)}, u32[]{:S(2)}, u32[]{:S(2)}) async-start(f32[4,256,128]{2,1,0:T(8,128)} %get-tuple-element.41), calls=%async_computation | async-start | bytes 1048576 | tf_op jit(solution)/shard_map/all_to_all | solution.py:400
  9.6 20.8 %collective-permute-start.1 = (f32[64,256]{1,0:T(8,128)}, f32[64,256]{1,0:T(8,128)S(1)}, u32[]{:S(2)}, u32[]{:S(2)}) collective-permute-start(f32[64,256]{1,0:T(8,128)} %get-tuple-element.34), channel_id=1, source_target_pairs={{32,64},{96,128},{160,192},{224,256},{288,320},{352,384},{416,448}... | collective-permute-start | bytes 196616 | tf_op jit(solution)/shard_map/ppermute | solution.py:218
  10.3 20.1 %collective-permute-start = (f32[64,256]{1,0:T(8,128)}, f32[64,256]{1,0:T(8,128)S(1)}, u32[]{:S(2)}, u32[]{:S(2)}) collective-permute-start(f32[64,256]{1,0:T(8,128)} %get-tuple-element.34), channel_id=1, source_target_pairs={{0,32},{64,96},{128,160},{192,224},{256,288},{320,352},{384,416},{... | collective-permute-start | bytes 196616 | tf_op jit(solution)/shard_map/ppermute | solution.py:218
  22.5 6.5 %collective-permute-start.2 = (f32[64,128]{1,0:T(8,128)}, f32[64,128]{1,0:T(8,128)S(1)}, u32[]{:S(2)}, u32[]{:S(2)}) collective-permute-start(f32[64,128]{1,0:T(8,128)} %get-tuple-element.35), channel_id=1, source_target_pairs={{1,2},{3,4},{5,6},{7,8},{9,10},{11,12},{13,14},{15,16},{17,18},{19... | collective-permute-start | bytes 98312 | tf_op jit(solution)/shard_map/ppermute | solution.py:218
  27.1 3.3 %collective-permute-start.3 = (f32[64,128]{1,0:T(8,128)}, f32[64,128]{1,0:T(8,128)S(1)}, u32[]{:S(2)}, u32[]{:S(2)}) collective-permute-start(f32[64,128]{1,0:T(8,128)} %get-tuple-element.36), channel_id=1, source_target_pairs={{0,1},{2,3},{4,5},{6,7},{8,9},{10,11},{12,13},{14,15},{16,17},{18,... | collective-permute-start | bytes 98312 | tf_op jit(solution)/shard_map/ppermute | solution.py:218
  30.4 0.9 copy-start
  31.5 15.0 %collective-permute-start.8 = (f32[4,256,128]{2,1,0:T(8,128)S(1)}, f32[4,256,128]{2,1,0:T(8,128)S(1)}, u32[]{:S(2)}, u32[]{:S(2)}) collective-permute-start(f32[4,256,128]{2,1,0:T(8,128)S(1)} %all-to-all-done.mine), channel_id=1, source_target_pairs={{0,1},{1,0},{2,3},{3,2},{4,5},{5,4},{6,7},{7,6},{8,9},{9,8},{10,11... | collective-permute-start | bytes 1572872 | tf_op jit(solution)/shard_map/ppermute | solution.py:425
  33.5 12.8 %collective-permute-start.5 = (f32[64,256]{1,0:T(8,128)S(1)}, f32[64,256]{1,0:T(8,128)S(1)}, u32[]{:S(2)}, u32[]{:S(2)}) collective-permute-start(f32[64,256]{1,0:T(8,128)S(1)} %get-tuple-element.42.resp), channel_id=1, source_target_pairs={{32,64},{96,128},{160,192},{224,256},{288,320},{352,384},{416,448}... | collective-permute-start | bytes 196616 | tf_op jit(solution)/shard_map/ppermute | solution.py:218
  34.2 12.1 %collective-permute-start.4 = (f32[64,256]{1,0:T(8,128)S(1)}, f32[64,256]{1,0:T(8,128)S(1)}, u32[]{:S(2)}, u32[]{:S(2)}) collective-permute-start(f32[64,256]{1,0:T(8,128)S(1)} %get-tuple-element.42.resp), channel_id=1, source_target_pairs={{0,32},{64,96},{128,160},{192,224},{256,288},{320,352},{384,416},{... | collective-permute-start | bytes 196616 | tf_op jit(solution)/shard_map/ppermute | solution.py:218
  39.2 5.9 %collective-permute-start.6 = (f32[64,128]{1,0:T(8,128)S(1)}, f32[64,128]{1,0:T(8,128)S(1)}, u32[]{:S(2)}, u32[]{:S(2)}) collective-permute-start(f32[64,128]{1,0:T(8,128)S(1)} %get-tuple-element.43), channel_id=1, source_target_pairs={{1,2},{3,4},{5,6},{7,8},{9,10},{11,12},{13,14},{15,16},{17,18},{19... | collective-permute-start | bytes 98312 | tf_op jit(solution)/shard_map/ppermute | solution.py:218
  43.2 3.1 %collective-permute-start.7 = (f32[64,128]{1,0:T(8,128)S(1)}, f32[64,128]{1,0:T(8,128)S(1)}, u32[]{:S(2)}, u32[]{:S(2)}) collective-permute-start(f32[64,128]{1,0:T(8,128)S(1)} %get-tuple-element.44), channel_id=1, source_target_pairs={{0,1},{2,3},{4,5},{6,7},{8,9},{10,11},{12,13},{14,15},{16,17},{18,... | collective-permute-start | bytes 98312 | tf_op jit(solution)/shard_map/ppermute | solution.py:218
  107.0 13.0 %all-to-all-start.5 = ((f32[8,8,384]{2,1,0:T(8,128)}), f32[8,8,384]{2,1,0:T(8,128)S(1)}, u32[]{:S(2)}, u32[]{:S(2)}) async-start(f32[8,8,384]{2,1,0:T(8,128)} %shard_map.82), calls=%async_computation.5 | async-start | bytes 196608 | tf_op jit(solution)/shard_map/all_to_all | solution.py:400
  120.9 15.7 %all-to-all-start.6 = ((f32[16,16,128]{2,1,0:T(8,128)}), f32[16,16,128]{2,1,0:T(8,128)S(1)}, u32[]{:S(2)}, u32[]{:S(2)}) async-start(f32[16,16,128]{2,1,0:T(8,128)} %get-tuple-element.55), calls=%async_computation.6 | async-start | bytes 262144 | tf_op jit(solution)/shard_map/all_to_all | solution.py:400
  125.0 11.6 %collective-permute-start.10 = (f32[64,256]{1,0:T(8,128)S(1)}, f32[64,256]{1,0:T(8,128)S(1)}, u32[]{:S(2)}, u32[]{:S(2)}) collective-permute-start(f32[64,256]{1,0:T(8,128)S(1)} %get-tuple-element.52), channel_id=1, source_target_pairs={{32,64},{96,128},{160,192},{224,256},{288,320},{352,384},{416,448}... | collective-permute-start | bytes 196616 | tf_op jit(solution)/shard_map/ppermute | solution.py:218
  125.6 11.0 %collective-permute-start.9 = (f32[64,256]{1,0:T(8,128)S(1)}, f32[64,256]{1,0:T(8,128)S(1)}, u32[]{:S(2)}, u32[]{:S(2)}) collective-permute-start(f32[64,256]{1,0:T(8,128)S(1)} %get-tuple-element.52), channel_id=1, source_target_pairs={{0,32},{64,96},{128,160},{192,224},{256,288},{320,352},{384,416},{... | collective-permute-start | bytes 196616 | tf_op jit(solution)/shard_map/ppermute | solution.py:218
  129.4 6.0 %collective-permute-start.11 = (f32[64,128]{1,0:T(8,128)S(1)}, f32[64,128]{1,0:T(8,128)S(1)}, u32[]{:S(2)}, u32[]{:S(2)}) collective-permute-start(f32[64,128]{1,0:T(8,128)S(1)} %get-tuple-element.53), channel_id=1, source_target_pairs={{1,2},{3,4},{5,6},{7,8},{9,10},{11,12},{13,14},{15,16},{17,18},{19... | collective-permute-start | bytes 98312 | tf_op jit(solution)/shard_map/ppermute | solution.py:218
  133.5 3.1 %collective-permute-start.12 = (f32[64,128]{1,0:T(8,128)S(1)}, f32[64,128]{1,0:T(8,128)S(1)}, u32[]{:S(2)}, u32[]{:S(2)}) collective-permute-start(f32[64,128]{1,0:T(8,128)S(1)} %get-tuple-element.54), channel_id=1, source_target_pairs={{0,1},{2,3},{4,5},{6,7},{8,9},{10,11},{12,13},{14,15},{16,17},{18,... | collective-permute-start | bytes 98312 | tf_op jit(solution)/shard_map/ppermute | solution.py:218
  137.3 24.9 %all-to-all-start.7 = ((f32[32,8,128]{2,1,0:T(8,128)}), f32[32,8,128]{2,1,0:T(8,128)S(1)}, u32[]{:S(2)}, u32[]{:S(2)}) async-start(f32[32,8,128]{2,1,0:T(8,128)} %get-tuple-element.59), calls=%async_computation.7 | async-start | bytes 262144 | tf_op jit(solution)/shard_map/all_to_all | solution.py:400
  146.1 16.1 %collective-permute-start.14 = (f32[64,256]{1,0:T(8,128)S(1)}, f32[64,256]{1,0:T(8,128)S(1)}, u32[]{:S(2)}, u32[]{:S(2)}) collective-permute-start(f32[64,256]{1,0:T(8,128)S(1)} %get-tuple-element.56.resp), channel_id=1, source_target_pairs={{32,64},{96,128},{160,192},{224,256},{288,320},{352,384},{416,448}... | collective-permute-start | bytes 196616 | tf_op jit(solution)/shard_map/ppermute | solution.py:218
  146.8 15.4 %collective-permute-start.13 = (f32[64,256]{1,0:T(8,128)S(1)}, f32[64,256]{1,0:T(8,128)S(1)}, u32[]{:S(2)}, u32[]{:S(2)}) collective-permute-start(f32[64,256]{1,0:T(8,128)S(1)} %get-tuple-element.56.resp), channel_id=1, source_target_pairs={{0,32},{64,96},{128,160},{192,224},{256,288},{320,352},{384,416},{... | collective-permute-start | bytes 196616 | tf_op jit(solution)/shard_map/ppermute | solution.py:218
  155.3 5.7 %collective-permute-start.15 = (f32[64,128]{1,0:T(8,128)S(1)}, f32[64,128]{1,0:T(8,128)S(1)}, u32[]{:S(2)}, u32[]{:S(2)}) collective-permute-start(f32[64,128]{1,0:T(8,128)S(1)} %get-tuple-element.57), channel_id=1, source_target_pairs={{1,2},{3,4},{5,6},{7,8},{9,10},{11,12},{13,14},{15,16},{17,18},{19... | collective-permute-start | bytes 98312 | tf_op jit(solution)/shard_map/ppermute | solution.py:218
  159.1 3.1 %collective-permute-start.16 = (f32[64,128]{1,0:T(8,128)S(1)}, f32[64,128]{1,0:T(8,128)S(1)}, u32[]{:S(2)}, u32[]{:S(2)}) collective-permute-start(f32[64,128]{1,0:T(8,128)S(1)} %get-tuple-element.58), channel_id=1, source_target_pairs={{0,1},{2,3},{4,5},{6,7},{8,9},{10,11},{12,13},{14,15},{16,17},{18,... | collective-permute-start | bytes 98312 | tf_op jit(solution)/shard_map/ppermute | solution.py:218

commit v7 on v6

--- a/solution.py
+++ b/solution.py
@@ -133,7 +133,7 @@
     count = whiten.shape[0]
     f32 = jnp.float32
     shapes = [(2 * count + 8, CELLS), (count, CELLS), (count, WIDTH), (count, WIDTH)]
-    shapes += [(4, CELLS, WIDTH)]
+    shapes += [(8, CELLS, WIDTH)]
     return pl.pallas_call(
         start_kernel,
         out_shape=[jax.ShapeDtypeStruct(shape, f32) for shape in shapes],
@@ -224,15 +224,13 @@
     )
 
 
-def moments_kernel(core, resp, mine, theirs, packet, turned, total):
+def moments_kernel(resp, shared, packet, turned, total):
     blocks, count = resp.shape[:2]
     row_at, col_at = iotas((WIDTH, WIDTH))
     ones = jnp.ones((CELLS, WIDTH), jnp.bfloat16)
     acc = [jnp.zeros((WIDTH, 2 * WIDTH), jnp.float32) for _ in range(count)]
-    for n in range(blocks):
-        cells = mine[n // 2] if n % 2 == 0 else theirs[n // 2]
-        block = n + core[0] if n % 2 == 0 else n - core[0]
-        weight = resp[block]
+    for block in range(blocks):
+        cells, weight = shared[block], resp[block]
         flipped = cells.T
         turned[block] = flipped.astype(jnp.bfloat16)
         wide = jnp.concatenate([cells.astype(jnp.bfloat16), ones], axis=1)
@@ -416,23 +414,21 @@
     before, resp, near, far, spread = start(
         core, weights0.reshape(1, count), flat, tissue.reshape(2, WIDTH), means0, whiten0
     )
-    mine = swap_all(spread, BRICK[:2])
+    shared = swap_all(spread, BRICK)
     kept_shape = ((count + 8, CELLS), f32)
     resp, near, far, kept = call(
         early_kernel, resp_shapes + [kept_shape], core, before, *halos(resp, near, far), scalars=1
     )
-    resp, near, far, mine = lax.optimization_barrier((resp, near, far, mine))
-    theirs = lax.ppermute(mine, "core", [(0, 1), (1, 0)])
+    resp, near, far, shared = lax.optimization_barrier((resp, near, far, shared))
     (resp,) = call(
         later_kernel, resp_shapes[:1], core, kept, resp, *halos(resp, near, far), scalars=1
     )
-    resp, theirs = lax.optimization_barrier((resp, theirs))
 
     part = swap_all(resp.reshape(8, 8, CELLS), BRICK)
     packets, turned, total = call(
         moments_kernel,
         [((8, PACKET, WIDTH), f32), ((8, WIDTH, CELLS), jnp.bfloat16), ((1, WIDTH), f32)],
-        core, part, mine, theirs, scalars=1, flops=1 << 30,
+        part, shared, flops=1 << 30,
     )
     (packets,) = call(gather_kernel, [((8, PACKET, WIDTH), f32)], swap_lines(packets, NEAR))
     packets = swap_lines(packets, FAR)

time: 164 us -> 162 us (0.988)
  the two profiles are of different devices: /device:TPU:1 before, /device:TPU:31 now
where the time goes in v7:
time: 162 us; the launch traced here: 161 us
  starting transfers between devices  89.7 us (55%)
  blocking collectives  47.6 us (29%)
  Pallas kernels  14.4 us (9%)
  waiting for transfers between devices  7.95 us (5%)
    ppermute x16, starting transfers between devices, swapped(): return lax.ppermute(part, axes, pairs + [(j, i) for i, j in pairs])  58.7 us
    all_to_all x3, blocking collectives, swap_lines(): lax.all_to_all(value, PLANE, 0, 0, axis_index_groups=groups, tiled=True)  37.8 us
    all_to_all x4, starting transfers between devices, swap_all(): return lax.all_to_all(value, axes, 0, 0, tiled=True)  31 us
    all_to_all x1, blocking collectives, swap_all(): return lax.all_to_all(value, axes, 0, 0, tiled=True)  9.75 us
    pallas_call x8, Pallas kernels, call(): pl.pallas_call(kernel, out_shape=out, in_specs=[SMEM] * scalars + [VMEM]...  9.32 us
    ppermute x16, waiting for transfers between devices, swapped(): return lax.ppermute(part, axes, pairs + [(j, i) for i, j in pairs])  4.7 us
    pallas_call x1, Pallas kernels, start(): pl.pallas_call(start_kernel, out_shape=[jax.ShapeDtypeStruct(shape, f32)...  4.28 us
    all_to_all x4, waiting for transfers between devices, swap_all(): return lax.all_to_all(value, axes, 0, 0, tiled=True)  3.25 us
  transfers between devices with their start and end apart: 20, of which 6 were waited for; matrix products, arithmetic and copies ran while one was open for 0% of the time, Pallas kernels for 0%

profile of v7, /device:TPU:31, one launch (start us, length us, event | category | flops | bytes accessed | tf_op | source)
XLA Modules:
  0.0 160.6 jit_solution(98501976513458505)
XLA Ops:
  0.6 4.3 %shard_map.76 = (f32[136,256]{1,0:T(8,128)}, f32[64,256]{1,0:T(8,128)}, f32[64,128]{1,0:T(8,128)}, f32[64,128]{1,0:T(8,128)}, f32[8,256,128]{2,1,0:T(8,128)}) custom-call(s32[1]{0:T(128)} %bitcast.core, f32[1,64]{1,0:T(1,128)} %bitcast.15, bf16[256,128]{1,0:T(8,128)(2,1)} %bitcast.13, s32[2,128]{1,0:T(2,128)} %bitcast.14, f32[64,128]{1,0:T(8,128)} %means.1, ...), custom_call_target="tpu_custom_call" | custom-call | flops 536870912 | bytes 2097152 | tf_op jit(solution)/shard_map/pallas_call | solution.py:137
  4.9 0.0 copy-start.1
  4.9 0.0 copy-start.3
  4.9 0.0 copy-start.2
  5.0 0.0 copy-start
  5.0 5.2 %all-to-all-start = ((f32[8,256,128]{2,1,0:T(8,128)}), f32[8,256,128]{2,1,0:T(8,128)S(1)}, u32[]{:S(2)}, u32[]{:S(2)}) async-start(f32[8,256,128]{2,1,0:T(8,128)} %get-tuple-element.39), calls=%async_computation | async-start | bytes 2097152 | tf_op jit(solution)/shard_map/all_to_all | solution.py:398
  10.2 0.0 copy-done.1
  10.2 5.8 %collective-permute-start = (f32[64,256]{1,0:T(8,128)S(1)}, f32[64,256]{1,0:T(8,128)S(1)}, u32[]{:S(2)}, u32[]{:S(2)}) collective-permute-start(f32[64,256]{1,0:T(8,128)S(1)} %copy-done.1), channel_id=1, source_target_pairs={{0,32},{64,96},{128,160},{192,224},{256,288},{320,352},{384,416},{... | collective-permute-start | bytes 196616 | tf_op jit(solution)/shard_map/ppermute | solution.py:218
  16.0 7.3 %collective-permute-start.1 = (f32[64,256]{1,0:T(8,128)S(1)}, f32[64,256]{1,0:T(8,128)S(1)}, u32[]{:S(2)}, u32[]{:S(2)}) collective-permute-start(f32[64,256]{1,0:T(8,128)S(1)} %copy-done.1), channel_id=1, source_target_pairs={{32,64},{96,128},{160,192},{224,256},{288,320},{352,384},{416,448}... | collective-permute-start | bytes 196616 | tf_op jit(solution)/shard_map/ppermute | solution.py:218
  23.3 0.0 copy-done.3
  23.3 5.2 %collective-permute-start.2 = (f32[64,128]{1,0:T(8,128)S(1)}, f32[64,128]{1,0:T(8,128)S(1)}, u32[]{:S(2)}, u32[]{:S(2)}) collective-permute-start(f32[64,128]{1,0:T(8,128)S(1)} %copy-done.3), channel_id=1, source_target_pairs={{1,2},{3,4},{5,6},{7,8},{9,10},{11,12},{13,14},{15,16},{17,18},{19... | collective-permute-start | bytes 98312 | tf_op jit(solution)/shard_map/ppermute | solution.py:218
  28.6 0.0 copy-done.2
  28.6 1.9 %collective-permute-start.3 = (f32[64,128]{1,0:T(8,128)S(1)}, f32[64,128]{1,0:T(8,128)S(1)}, u32[]{:S(2)}, u32[]{:S(2)}) collective-permute-start(f32[64,128]{1,0:T(8,128)S(1)} %copy-done.2), channel_id=1, source_target_pairs={{0,1},{2,3},{4,5},{6,7},{8,9},{10,11},{12,13},{14,15},{16,17},{18,... | collective-permute-start | bytes 98312 | tf_op jit(solution)/shard_map/ppermute | solution.py:218
  30.5 0.0 collective-permute-done.2.far_in
  30.5 1.2 collective-permute-done.3.near_in
  31.7 0.0 collective-permute-done.slab_even
  31.7 0.0 collective-permute-done.1.slab_odd
  31.7 0.0 copy-done
  31.7 0.2 shard_map.77
  31.9 0.0 all-to-all-done.shared
  31.9 3.7 %collective-permute-start.4 = (f32[64,256]{1,0:T(8,128)S(1)}, f32[64,256]{1,0:T(8,128)S(1)}, u32[]{:S(2)}, u32[]{:S(2)}) collective-permute-start(f32[64,256]{1,0:T(8,128)S(1)} %get-tuple-element.40.resp), channel_id=1, source_target_pairs={{0,32},{64,96},{128,160},{192,224},{256,288},{320,352},{384,416},{... | collective-permute-start | bytes 196616 | tf_op jit(solution)/shard_map/ppermute | solution.py:218
  35.6 1.9 %collective-permute-start.5 = (f32[64,256]{1,0:T(8,128)S(1)}, f32[64,256]{1,0:T(8,128)S(1)}, u32[]{:S(2)}, u32[]{:S(2)}) collective-permute-start(f32[64,256]{1,0:T(8,128)S(1)} %get-tuple-element.40.resp), channel_id=1, source_target_pairs={{32,64},{96,128},{160,192},{224,256},{288,320},{352,384},{416,448}... | collective-permute-start | bytes 196616 | tf_op jit(solution)/shard_map/ppermute | solution.py:218
  37.5 3.9 %collective-permute-start.6 = (f32[64,128]{1,0:T(8,128)S(1)}, f32[64,128]{1,0:T(8,128)S(1)}, u32[]{:S(2)}, u32[]{:S(2)}) collective-permute-start(f32[64,128]{1,0:T(8,128)S(1)} %get-tuple-element.41), channel_id=1, source_target_pairs={{1,2},{3,4},{5,6},{7,8},{9,10},{11,12},{13,14},{15,16},{17,18},{19... | collective-permute-start | bytes 98312 | tf_op jit(solution)/shard_map/ppermute | solution.py:218
  41.4 1.9 %collective-permute-start.7 = (f32[64,128]{1,0:T(8,128)S(1)}, f32[64,128]{1,0:T(8,128)S(1)}, u32[]{:S(2)}, u32[]{:S(2)}) collective-permute-start(f32[64,128]{1,0:T(8,128)S(1)} %get-tuple-element.42), channel_id=1, source_target_pairs={{0,1},{2,3},{4,5},{6,7},{8,9},{10,11},{12,13},{14,15},{16,17},{18,... | collective-permute-start | bytes 98312 | tf_op jit(solution)/shard_map/ppermute | solution.py:218
  43.4 0.9 collective-permute-done.6.far_in
  44.3 0.3 collective-permute-done.7.near_in
  44.5 0.0 collective-permute-done.4.slab_even
  44.5 0.0 collective-permute-done.5.slab_odd
  44.5 0.1 shard_map.78
  44.7 9.8 %all_to_all.40.resp = f32[8,8,256]{2,1,0:T(8,128)S(1)} all-to-all(f32[8,8,256]{2,1,0:T(8,128)S(1)} %bitcast.12), channel_id=1, replica_groups=mesh['x1'=2,'x0'=2,'z2'=2,'z1'=2,'z0'=2,'y2'=2,'y1'=2,'y0'=2,'core'=2] {..., dimensions={0} | all-to-all | bytes 131072 | tf_op jit(solution)/shard_map/all_to_all | solution.py:398
  54.4 1.6 shard_map.79
  56.0 13.6 %all_to_all.41.packets = f32[8,72,128]{2,1,0:T(8,128)S(1)} all-to-all(f32[8,72,128]{2,1,0:T(8,128)S(1)} %get-tuple-element.44), channel_id=1, replica_groups={{0,2,4,6,8,10,12,14},{16,18,20,22,24,26,28,30},{32,34,36,38,40,42,44,46..., dimensions={0} | all-to-all | bytes 589824 | tf_op jit(solution)/shard_map/all_to_all | solution.py:402
  69.7 12.2 %all_to_all.42.packets = f32[8,72,128]{2,1,0:T(8,128)S(1)} all-to-all(f32[8,72,128]{2,1,0:T(8,128)S(1)} %shard_map.80), channel_id=1, replica_groups={{0,16,32,48,64,80,96,112},{2,18,34,50,66,82,98,114},{4,20,36,52,68,84,1..., dimensions={0} | all-to-all | bytes 589824 | tf_op jit(solution)/shard_map/all_to_all | solution.py:402
  81.8 3.9 %shard_map.81 = f32[8,72,128]{2,1,0:T(8,128)S(1)} custom-call(f32[8,72,128]{2,1,0:T(8,128)S(1)} %all_to_all.42.packets), custom_call_target="tpu_custom_call" | custom-call | flops 134217728 | bytes 1048576 | tf_op jit(solution)/shard_map/pallas_call | solution.py:36
  85.7 12.0 %all_to_all.43.packets = f32[8,72,128]{2,1,0:T(8,128)S(1)} all-to-all(f32[8,72,128]{2,1,0:T(8,128)S(1)} %shard_map.81), channel_id=1, replica_groups={{0,2,4,6,8,10,12,14},{16,18,20,22,24,26,28,30},{32,34,36,38,40,42,44,46..., dimensions={0} | all-to-all | bytes 589824 | tf_op jit(solution)/shard_map/all_to_all | solution.py:402
  97.8 2.1 %shard_map.82 = f32[8,8,384]{2,1,0:T(8,128)} custom-call(f32[8,72,128]{2,1,0:T(8,128)S(1)} %all_to_all.43.packets, bf16[8,128,256]{2,1,0:T(8,128)(2,1)S(1)} %get-tuple-element.45.turned), custom_call_target="tpu_custom_call" | custom-call | flops 536870912 | bytes 1048576 | tf_op jit(solution)/shard_map/pallas_call | solution.py:36
  99.8 9.5 %all-to-all-start.5 = ((f32[8,8,384]{2,1,0:T(8,128)}), f32[8,8,384]{2,1,0:T(8,128)S(1)}, u32[]{:S(2)}, u32[]{:S(2)}) async-start(f32[8,8,384]{2,1,0:T(8,128)} %shard_map.82), calls=%async_computation.5 | async-start | bytes 196608 | tf_op jit(solution)/shard_map/all_to_all | solution.py:398
  109.4 3.2 %all-to-all-done.5 = f32[8,8,384]{2,1,0:T(8,128)S(1)} async-done(((f32[8,8,384]{2,1,0:T(8,128)}), f32[8,8,384]{2,1,0:T(8,128)S(1)}, u32[]{:S(2)}, u32[]{:S(2)}) %all-to-all-start.5) | async-done | bytes 98336 | tf_op jit(solution)/shard_map/all_to_all | solution.py:398
  112.6 0.8 shard_map.83
  113.4 7.1 %all-to-all-start.6 = ((f32[16,16,128]{2,1,0:T(8,128)}), f32[16,16,128]{2,1,0:T(8,128)S(1)}, u32[]{:S(2)}, u32[]{:S(2)}) async-start(f32[16,16,128]{2,1,0:T(8,128)} %get-tuple-element.51), calls=%async_computation.6 | async-start | bytes 262144 | tf_op jit(solution)/shard_map/all_to_all | solution.py:398
  120.5 2.1 %collective-permute-start.8 = (f32[64,256]{1,0:T(8,128)S(1)}, f32[64,256]{1,0:T(8,128)S(1)}, u32[]{:S(2)}, u32[]{:S(2)}) collective-permute-start(f32[64,256]{1,0:T(8,128)S(1)} %get-tuple-element.48), channel_id=1, source_target_pairs={{0,32},{64,96},{128,160},{192,224},{256,288},{320,352},{384,416},{... | collective-permute-start | bytes 196616 | tf_op jit(solution)/shard_map/ppermute | solution.py:218
  122.6 2.0 %collective-permute-start.9 = (f32[64,256]{1,0:T(8,128)S(1)}, f32[64,256]{1,0:T(8,128)S(1)}, u32[]{:S(2)}, u32[]{:S(2)}) collective-permute-start(f32[64,256]{1,0:T(8,128)S(1)} %get-tuple-element.48), channel_id=1, source_target_pairs={{32,64},{96,128},{160,192},{224,256},{288,320},{352,384},{416,448}... | collective-permute-start | bytes 196616 | tf_op jit(solution)/shard_map/ppermute | solution.py:218
  124.6 5.1 %collective-permute-start.10 = (f32[64,128]{1,0:T(8,128)S(1)}, f32[64,128]{1,0:T(8,128)S(1)}, u32[]{:S(2)}, u32[]{:S(2)}) collective-permute-start(f32[64,128]{1,0:T(8,128)S(1)} %get-tuple-element.49), channel_id=1, source_target_pairs={{1,2},{3,4},{5,6},{7,8},{9,10},{11,12},{13,14},{15,16},{17,18},{19... | collective-permute-start | bytes 98312 | tf_op jit(solution)/shard_map/ppermute | solution.py:218
  129.7 1.9 %collective-permute-start.11 = (f32[64,128]{1,0:T(8,128)S(1)}, f32[64,128]{1,0:T(8,128)S(1)}, u32[]{:S(2)}, u32[]{:S(2)}) collective-permute-start(f32[64,128]{1,0:T(8,128)S(1)} %get-tuple-element.50), channel_id=1, source_target_pairs={{0,1},{2,3},{4,5},{6,7},{8,9},{10,11},{12,13},{14,15},{16,17},{18,... | collective-permute-start | bytes 98312 | tf_op jit(solution)/shard_map/ppermute | solution.py:218
  131.7 0.0 collective-permute-done.10.far_in
  131.7 1.2 collective-permute-done.11.near_in
  132.9 0.0 collective-permute-done.8.slab_even
  132.9 0.0 collective-permute-done.9.slab_odd
  132.9 0.0 all-to-all-done.6.totals
  132.9 0.7 shard_map.84
  133.6 9.2 %all-to-all-start.7 = ((f32[32,8,128]{2,1,0:T(8,128)}), f32[32,8,128]{2,1,0:T(8,128)S(1)}, u32[]{:S(2)}, u32[]{:S(2)}) async-start(f32[32,8,128]{2,1,0:T(8,128)} %get-tuple-element.55), calls=%async_computation.7 | async-start | bytes 262144 | tf_op jit(solution)/shard_map/all_to_all | solution.py:398
  142.7 4.0 %collective-permute-start.12 = (f32[64,256]{1,0:T(8,128)S(1)}, f32[64,256]{1,0:T(8,128)S(1)}, u32[]{:S(2)}, u32[]{:S(2)}) collective-permute-start(f32[64,256]{1,0:T(8,128)S(1)} %get-tuple-element.52.resp), channel_id=1, source_target_pairs={{0,32},{64,96},{128,160},{192,224},{256,288},{320,352},{384,416},{... | collective-permute-start | bytes 196616 | tf_op jit(solution)/shard_map/ppermute | solution.py:218
  146.8 5.5 %collective-permute-start.13 = (f32[64,256]{1,0:T(8,128)S(1)}, f32[64,256]{1,0:T(8,128)S(1)}, u32[]{:S(2)}, u32[]{:S(2)}) collective-permute-start(f32[64,256]{1,0:T(8,128)S(1)} %get-tuple-element.52.resp), channel_id=1, source_target_pairs={{32,64},{96,128},{160,192},{224,256},{288,320},{352,384},{416,448}... | collective-permute-start | bytes 196616 | tf_op jit(solution)/shard_map/ppermute | solution.py:218
  152.2 4.5 %collective-permute-start.14 = (f32[64,128]{1,0:T(8,128)S(1)}, f32[64,128]{1,0:T(8,128)S(1)}, u32[]{:S(2)}, u32[]{:S(2)}) collective-permute-start(f32[64,128]{1,0:T(8,128)S(1)} %get-tuple-element.53), channel_id=1, source_target_pairs={{1,2},{3,4},{5,6},{7,8},{9,10},{11,12},{13,14},{15,16},{17,18},{19... | collective-permute-start | bytes 98312 | tf_op jit(solution)/shard_map/ppermute | solution.py:218
  156.7 1.9 %collective-permute-start.15 = (f32[64,128]{1,0:T(8,128)S(1)}, f32[64,128]{1,0:T(8,128)S(1)}, u32[]{:S(2)}, u32[]{:S(2)}) collective-permute-start(f32[64,128]{1,0:T(8,128)S(1)} %get-tuple-element.54), channel_id=1, source_target_pairs={{0,1},{2,3},{4,5},{6,7},{8,9},{10,11},{12,13},{14,15},{16,17},{18,... | collective-permute-start | bytes 98312 | tf_op jit(solution)/shard_map/ppermute | solution.py:218
  158.6 0.0 collective-permute-done.14.far_in
  158.7 1.1 collective-permute-done.15.near_in
  159.8 0.0 collective-permute-done.12.slab_even
  159.8 0.0 collective-permute-done.13.slab_odd
  159.8 0.0 all-to-all-done.7.totals
  159.8 0.8 shard_map.85
  (1 shorter events, 0.0 us)
Async XLA Ops:
  4.9 5.3 %copy-start.1 = (f32[64,256]{1,0:T(8,128)S(1)}, f32[64,256]{1,0:T(8,128)}, u32[]{:S(2)}) copy-start(f32[64,256]{1,0:T(8,128)} %get-tuple-element.32) | copy-start | bytes 196612
  4.9 18.4 %copy-start.3 = (f32[64,128]{1,0:T(8,128)S(1)}, f32[64,128]{1,0:T(8,128)}, u32[]{:S(2)}) copy-start(f32[64,128]{1,0:T(8,128)} %get-tuple-element.33) | copy-start | bytes 98308
  4.9 23.6 %copy-start.2 = (f32[64,128]{1,0:T(8,128)S(1)}, f32[64,128]{1,0:T(8,128)}, u32[]{:S(2)}) copy-start(f32[64,128]{1,0:T(8,128)} %get-tuple-element.34) | copy-start | bytes 98308
  5.0 26.7 %copy-start = (f32[136,256]{1,0:T(8,128)S(1)}, f32[136,256]{1,0:T(8,128)}, u32[]{:S(2)}) copy-start(f32[136,256]{1,0:T(8,128)} %get-tuple-element.31.state) | copy-start | bytes 417796
  5.0 26.9 %all-to-all-start = ((f32[8,256,128]{2,1,0:T(8,128)}), f32[8,256,128]{2,1,0:T(8,128)S(1)}, u32[]{:S(2)}, u32[]{:S(2)}) async-start(f32[8,256,128]{2,1,0:T(8,128)} %get-tuple-element.39), calls=%async_computation | async-start | bytes 2097152 | tf_op jit(solution)/shard_map/all_to_all | solution.py:398
  10.2 21.5 %collective-permute-start = (f32[64,256]{1,0:T(8,128)S(1)}, f32[64,256]{1,0:T(8,128)S(1)}, u32[]{:S(2)}, u32[]{:S(2)}) collective-permute-start(f32[64,256]{1,0:T(8,128)S(1)} %copy-done.1), channel_id=1, source_target_pairs={{0,32},{64,96},{128,160},{192,224},{256,288},{320,352},{384,416},{... | collective-permute-start | bytes 196616 | tf_op jit(solution)/shard_map/ppermute | solution.py:218
  16.0 15.7 %collective-permute-start.1 = (f32[64,256]{1,0:T(8,128)S(1)}, f32[64,256]{1,0:T(8,128)S(1)}, u32[]{:S(2)}, u32[]{:S(2)}) collective-permute-start(f32[64,256]{1,0:T(8,128)S(1)} %copy-done.1), channel_id=1, source_target_pairs={{32,64},{96,128},{160,192},{224,256},{288,320},{352,384},{416,448}... | collective-permute-start | bytes 196616 | tf_op jit(solution)/shard_map/ppermute | solution.py:218
  23.3 7.2 %collective-permute-start.2 = (f32[64,128]{1,0:T(8,128)S(1)}, f32[64,128]{1,0:T(8,128)S(1)}, u32[]{:S(2)}, u32[]{:S(2)}) collective-permute-start(f32[64,128]{1,0:T(8,128)S(1)} %copy-done.3), channel_id=1, source_target_pairs={{1,2},{3,4},{5,6},{7,8},{9,10},{11,12},{13,14},{15,16},{17,18},{19... | collective-permute-start | bytes 98312 | tf_op jit(solution)/shard_map/ppermute | solution.py:218
  28.6 3.1 %collective-permute-start.3 = (f32[64,128]{1,0:T(8,128)S(1)}, f32[64,128]{1,0:T(8,128)S(1)}, u32[]{:S(2)}, u32[]{:S(2)}) collective-permute-start(f32[64,128]{1,0:T(8,128)S(1)} %copy-done.2), channel_id=1, source_target_pairs={{0,1},{2,3},{4,5},{6,7},{8,9},{10,11},{12,13},{14,15},{16,17},{18,... | collective-permute-start | bytes 98312 | tf_op jit(solution)/shard_map/ppermute | solution.py:218
  31.9 12.7 %collective-permute-start.4 = (f32[64,256]{1,0:T(8,128)S(1)}, f32[64,256]{1,0:T(8,128)S(1)}, u32[]{:S(2)}, u32[]{:S(2)}) collective-permute-start(f32[64,256]{1,0:T(8,128)S(1)} %get-tuple-element.40.resp), channel_id=1, source_target_pairs={{0,32},{64,96},{128,160},{192,224},{256,288},{320,352},{384,416},{... | collective-permute-start | bytes 196616 | tf_op jit(solution)/shard_map/ppermute | solution.py:218
  35.6 9.0 %collective-permute-start.5 = (f32[64,256]{1,0:T(8,128)S(1)}, f32[64,256]{1,0:T(8,128)S(1)}, u32[]{:S(2)}, u32[]{:S(2)}) collective-permute-start(f32[64,256]{1,0:T(8,128)S(1)} %get-tuple-element.40.resp), channel_id=1, source_target_pairs={{32,64},{96,128},{160,192},{224,256},{288,320},{352,384},{416,448}... | collective-permute-start | bytes 196616 | tf_op jit(solution)/shard_map/ppermute | solution.py:218
  37.5 6.7 %collective-permute-start.6 = (f32[64,128]{1,0:T(8,128)S(1)}, f32[64,128]{1,0:T(8,128)S(1)}, u32[]{:S(2)}, u32[]{:S(2)}) collective-permute-start(f32[64,128]{1,0:T(8,128)S(1)} %get-tuple-element.41), channel_id=1, source_target_pairs={{1,2},{3,4},{5,6},{7,8},{9,10},{11,12},{13,14},{15,16},{17,18},{19... | collective-permute-start | bytes 98312 | tf_op jit(solution)/shard_map/ppermute | solution.py:218
  41.4 3.1 %collective-permute-start.7 = (f32[64,128]{1,0:T(8,128)S(1)}, f32[64,128]{1,0:T(8,128)S(1)}, u32[]{:S(2)}, u32[]{:S(2)}) collective-permute-start(f32[64,128]{1,0:T(8,128)S(1)} %get-tuple-element.42), channel_id=1, source_target_pairs={{0,1},{2,3},{4,5},{6,7},{8,9},{10,11},{12,13},{14,15},{16,17},{18,... | collective-permute-start | bytes 98312 | tf_op jit(solution)/shard_map/ppermute | solution.py:218
  99.8 12.8 %all-to-all-start.5 = ((f32[8,8,384]{2,1,0:T(8,128)}), f32[8,8,384]{2,1,0:T(8,128)S(1)}, u32[]{:S(2)}, u32[]{:S(2)}) async-start(f32[8,8,384]{2,1,0:T(8,128)} %shard_map.82), calls=%async_computation.5 | async-start | bytes 196608 | tf_op jit(solution)/shard_map/all_to_all | solution.py:398
  113.4 19.5 %all-to-all-start.6 = ((f32[16,16,128]{2,1,0:T(8,128)}), f32[16,16,128]{2,1,0:T(8,128)S(1)}, u32[]{:S(2)}, u32[]{:S(2)}) async-start(f32[16,16,128]{2,1,0:T(8,128)} %get-tuple-element.51), calls=%async_computation.6 | async-start | bytes 262144 | tf_op jit(solution)/shard_map/all_to_all | solution.py:398
  120.5 12.4 %collective-permute-start.8 = (f32[64,256]{1,0:T(8,128)S(1)}, f32[64,256]{1,0:T(8,128)S(1)}, u32[]{:S(2)}, u32[]{:S(2)}) collective-permute-start(f32[64,256]{1,0:T(8,128)S(1)} %get-tuple-element.48), channel_id=1, source_target_pairs={{0,32},{64,96},{128,160},{192,224},{256,288},{320,352},{384,416},{... | collective-permute-start | bytes 196616 | tf_op jit(solution)/shard_map/ppermute | solution.py:218
  122.6 10.3 %collective-permute-start.9 = (f32[64,256]{1,0:T(8,128)S(1)}, f32[64,256]{1,0:T(8,128)S(1)}, u32[]{:S(2)}, u32[]{:S(2)}) collective-permute-start(f32[64,256]{1,0:T(8,128)S(1)} %get-tuple-element.48), channel_id=1, source_target_pairs={{32,64},{96,128},{160,192},{224,256},{288,320},{352,384},{416,448}... | collective-permute-start | bytes 196616 | tf_op jit(solution)/shard_map/ppermute | solution.py:218
  124.6 7.1 %collective-permute-start.10 = (f32[64,128]{1,0:T(8,128)S(1)}, f32[64,128]{1,0:T(8,128)S(1)}, u32[]{:S(2)}, u32[]{:S(2)}) collective-permute-start(f32[64,128]{1,0:T(8,128)S(1)} %get-tuple-element.49), channel_id=1, source_target_pairs={{1,2},{3,4},{5,6},{7,8},{9,10},{11,12},{13,14},{15,16},{17,18},{19... | collective-permute-start | bytes 98312 | tf_op jit(solution)/shard_map/ppermute | solution.py:218
  129.7 3.1 %collective-permute-start.11 = (f32[64,128]{1,0:T(8,128)S(1)}, f32[64,128]{1,0:T(8,128)S(1)}, u32[]{:S(2)}, u32[]{:S(2)}) collective-permute-start(f32[64,128]{1,0:T(8,128)S(1)} %get-tuple-element.50), channel_id=1, source_target_pairs={{0,1},{2,3},{4,5},{6,7},{8,9},{10,11},{12,13},{14,15},{16,17},{18,... | collective-permute-start | bytes 98312 | tf_op jit(solution)/shard_map/ppermute | solution.py:218
  133.6 26.2 %all-to-all-start.7 = ((f32[32,8,128]{2,1,0:T(8,128)}), f32[32,8,128]{2,1,0:T(8,128)S(1)}, u32[]{:S(2)}, u32[]{:S(2)}) async-start(f32[32,8,128]{2,1,0:T(8,128)} %get-tuple-element.55), calls=%async_computation.7 | async-start | bytes 262144 | tf_op jit(solution)/shard_map/all_to_all | solution.py:398
  142.7 17.1 %collective-permute-start.12 = (f32[64,256]{1,0:T(8,128)S(1)}, f32[64,256]{1,0:T(8,128)S(1)}, u32[]{:S(2)}, u32[]{:S(2)}) collective-permute-start(f32[64,256]{1,0:T(8,128)S(1)} %get-tuple-element.52.resp), channel_id=1, source_target_pairs={{0,32},{64,96},{128,160},{192,224},{256,288},{320,352},{384,416},{... | collective-permute-start | bytes 196616 | tf_op jit(solution)/shard_map/ppermute | solution.py:218
  146.8 13.0 %collective-permute-start.13 = (f32[64,256]{1,0:T(8,128)S(1)}, f32[64,256]{1,0:T(8,128)S(1)}, u32[]{:S(2)}, u32[]{:S(2)}) collective-permute-start(f32[64,256]{1,0:T(8,128)S(1)} %get-tuple-element.52.resp), channel_id=1, source_target_pairs={{32,64},{96,128},{160,192},{224,256},{288,320},{352,384},{416,448}... | collective-permute-start | bytes 196616 | tf_op jit(solution)/shard_map/ppermute | solution.py:218
  152.2 6.4 %collective-permute-start.14 = (f32[64,128]{1,0:T(8,128)S(1)}, f32[64,128]{1,0:T(8,128)S(1)}, u32[]{:S(2)}, u32[]{:S(2)}) collective-permute-start(f32[64,128]{1,0:T(8,128)S(1)} %get-tuple-element.53), channel_id=1, source_target_pairs={{1,2},{3,4},{5,6},{7,8},{9,10},{11,12},{13,14},{15,16},{17,18},{19... | collective-permute-start | bytes 98312 | tf_op jit(solution)/shard_map/ppermute | solution.py:218
  156.7 3.1 %collective-permute-start.15 = (f32[64,128]{1,0:T(8,128)S(1)}, f32[64,128]{1,0:T(8,128)S(1)}, u32[]{:S(2)}, u32[]{:S(2)}) collective-permute-start(f32[64,128]{1,0:T(8,128)S(1)} %get-tuple-element.54), channel_id=1, source_target_pairs={{0,1},{2,3},{4,5},{6,7},{8,9},{10,11},{12,13},{14,15},{16,17},{18,... | collective-permute-start | bytes 98312 | tf_op jit(solution)/shard_map/ppermute | solution.py:218

commit v8 on v7

--- a/solution.py
+++ b/solution.py
@@ -18,12 +18,12 @@
 ALONG_Z = [[[z * 16 + y * 2 + core for z in range(8)] for y in range(8)] for core in range(2)]
 NEAR = ALONG_Y[0] + ALONG_Z[1]
 FAR = ALONG_Z[0] + ALONG_Y[1]
-ROUND = (("y2", "y1", "y0", "core"), ("x1", "x0", "z2", "z1", "z0"))
 
 WIDTH = 128
 CELLS = 256
 DEVICES = 512
 HALF = 64
+PARTS = CELLS + WIDTH
 PACKET = HALF + 8
 VMEM = pl.BlockSpec(memory_space=pltpu.VMEM)
 SMEM = pl.BlockSpec(memory_space=pltpu.SMEM)
@@ -100,9 +100,13 @@
     full = flat_in[...].astype(jnp.float32)
     cells = full.T.astype(jnp.bfloat16)
     for n in range(spread.shape[0]):
-        spread[n] = full
+        spread[n, :CELLS] = full
     for copy in copies[1:]:
         copy.wait()
+    tissue_f = tissue_in[...].astype(jnp.float32)
+    rows = jnp.concatenate([tissue_f, jnp.zeros((6, WIDTH), jnp.float32)], axis=0)
+    for n in range(spread.shape[0]):
+        spread[n, CELLS:] = rows
     for n, block in enumerate(blocks):
         block.wait()
         for own in range(n * CHUNK, (n + 1) * CHUNK):
@@ -122,7 +126,6 @@
         jnp.log(diag[...]), axis=1, keepdims=True
     )
     result = offset - 0.5 * state[:count]
-    tissue_f = tissue_in[...].astype(jnp.float32)
     tissue_f = jnp.concatenate([tissue_f[:1], tissue_f[1:]], axis=1)
     first = normalise(result) * tissue_f
     keep(result, first, tissue_f, state)
@@ -133,7 +136,7 @@
     count = whiten.shape[0]
     f32 = jnp.float32
     shapes = [(2 * count + 8, CELLS), (count, CELLS), (count, WIDTH), (count, WIDTH)]
-    shapes += [(8, CELLS, WIDTH)]
+    shapes += [(8, CELLS + 8, WIDTH)]
     return pl.pallas_call(
         start_kernel,
         out_shape=[jax.ShapeDtypeStruct(shape, f32) for shape in shapes],
@@ -207,7 +210,7 @@
     total = total[:1]
     lane = iotas((1, WIDTH))[1]
     lse = jnp.sum(jnp.where(lane == 0, total, 0.0))
-    level = jnp.sum(jnp.where(lane == 2, jnp.log(total), 0.0))
+    level = jnp.sum(jnp.where(lane == 1, jnp.log(total), 0.0))
     cells = jnp.sum(jnp.where(lane == 1, total, 0.0))
     score[0, 0] = (lse - cells * level) / (CELLS * DEVICES)
 
@@ -224,13 +227,15 @@
     )
 
 
-def moments_kernel(resp, shared, packet, turned, total):
+def moments_kernel(resp, shared, packet, turned, cover):
     blocks, count = resp.shape[:2]
     row_at, col_at = iotas((WIDTH, WIDTH))
     ones = jnp.ones((CELLS, WIDTH), jnp.bfloat16)
     acc = [jnp.zeros((WIDTH, 2 * WIDTH), jnp.float32) for _ in range(count)]
     for block in range(blocks):
-        cells, weight = shared[block], resp[block]
+        cells, weight = shared[block, :CELLS], resp[block]
+        tissue_f = shared[block, CELLS:]
+        cover[block : block + 1] = jnp.concatenate([tissue_f[:1], tissue_f[1:2]], axis=1)
         flipped = cells.T
         turned[block] = flipped.astype(jnp.bfloat16)
         wide = jnp.concatenate([cells.astype(jnp.bfloat16), ones], axis=1)
@@ -243,7 +248,6 @@
     firsts = firsts.T
     counts = jnp.sum(jnp.sum(resp[...], axis=0), axis=1, keepdims=True)
     counts = jnp.broadcast_to(counts, (count, WIDTH))
-    total[...] = jnp.sum(counts, axis=0, keepdims=True)
     fold_row, fold_col = iotas((HALF, WIDTH))
     for k in range(count):
         sym = acc[k][:, :WIDTH]
@@ -362,6 +366,7 @@
     offsets = jnp.concatenate(offsets, axis=0)
     offsets = jnp.concatenate([offsets, offsets], axis=1)
     centres = jnp.concatenate(centres, axis=0)
+    tops, weights = [], []
     for block in range(turned.shape[0]):
         proj = matmul(halves, turned[block])
         quads = []
@@ -369,27 +374,41 @@
             shift = jnp.concatenate([shifts[k], shifts[k]], axis=1)
             off = proj[k * WIDTH : (k + 1) * WIDTH] - shift
             quads.append(jnp.sum(off * off, axis=0, keepdims=True))
-        scores[block, :, :CELLS] = offsets - 0.5 * jnp.concatenate(quads, axis=0)
-        scores[block, :, CELLS:] = centres
-
-
-def likely_kernel(core, tile, part, mask, total, state, resp, near, far, means, totals):
+        values = offsets - 0.5 * jnp.concatenate(quads, axis=0)
+        scores[block, :, :CELLS] = values
+        scores[block, :, CELLS:PARTS] = centres
+        tops.append(jnp.max(values, axis=0, keepdims=True))
+        weights.append(jnp.sum(jnp.exp(values - tops[-1]), axis=0, keepdims=True))
+    tops = jnp.concatenate(tops, axis=0)
+    weights = jnp.concatenate(weights, axis=0)
+    for block in range(turned.shape[0]):
+        scores[block, :, PARTS : PARTS + CELLS] = tops
+        scores[block, :, PARTS + CELLS :] = weights
+
+
+def likely_kernel(core, tile, part, mask, cover, state, resp, near, far, means, totals):
     values = part[:, :CELLS]
-    row = iotas((part.shape[0], WIDTH))[0]
+    count = values.shape[0]
+    row = iotas((count, WIDTH))[0]
     for n in range(2):
-        own = jnp.where(row == 2 * tile[0] + n, part[:, CELLS:], 0.0)
+        own = jnp.where(row == 2 * tile[0] + n, part[:, CELLS:PARTS], 0.0)
         means[n : n + 1] = jnp.sum(own, axis=0, keepdims=True)
     tissue_f = mask[mask.shape[0] - 1 :]
-    top = jnp.max(values, axis=0, keepdims=True)
-    expon = jnp.exp(values - top)
-    weight = jnp.sum(expon, axis=0, keepdims=True)
-    first = expon / weight * tissue_f
+    first = normalise(values) * tissue_f
     keep(values, first, tissue_f, state)
     put(core[0], first, resp, near, far)
-    lse = jnp.sum((top + jnp.log(weight)) * tissue_f, axis=1, keepdims=True)
-    cells = jnp.sum(tissue_f, axis=1, keepdims=True)
+    parts = [part[n : n + 8, PARTS:] for n in range(0, count, 8)]
+    top = parts[0][:, :CELLS]
+    for one in parts[1:]:
+        top = jnp.maximum(top, one[:, :CELLS])
+    weight = jnp.zeros(top.shape, jnp.float32)
+    for one in parts:
+        weight = weight + one[:, CELLS:] * jnp.exp(one[:, :CELLS] - top)
+    lse = jnp.sum((top + jnp.log(weight)) * cover[...], axis=0, keepdims=True)
+    lse = jnp.sum(lse, axis=1, keepdims=True)
+    cells = jnp.sum(jnp.sum(cover[...], axis=0, keepdims=True), axis=1, keepdims=True)
     lane = iotas((1, WIDTH))[1]
-    result = jnp.where(lane == 0, lse, jnp.where(lane == 1, cells, total[...]))
+    result = jnp.where(lane == 0, lse, cells)
     for n in range(totals.shape[0]):
         totals[n] = jnp.broadcast_to(result, totals.shape[1:])
 
@@ -425,9 +444,9 @@
     )
 
     part = swap_all(resp.reshape(8, 8, CELLS), BRICK)
-    packets, turned, total = call(
+    packets, turned, cover = call(
         moments_kernel,
-        [((8, PACKET, WIDTH), f32), ((8, WIDTH, CELLS), jnp.bfloat16), ((1, WIDTH), f32)],
+        [((8, PACKET, WIDTH), f32), ((8, WIDTH, CELLS), jnp.bfloat16), ((8, CELLS), f32)],
         part, shared, flops=1 << 30,
     )
     (packets,) = call(gather_kernel, [((8, PACKET, WIDTH), f32)], swap_lines(packets, NEAR))
@@ -435,22 +454,22 @@
     (packets,) = call(factor_kernel, [((8, PACKET, WIDTH), f32)], packets, flops=1 << 27)
     packets = swap_lines(packets, NEAR)
     (part,) = call(
-        second_kernel, [((8, 8, CELLS + WIDTH), f32)], packets, turned, flops=1 << 29
-    )
-    part = swap_all(part, BRICK).reshape(count, CELLS + WIDTH)
-
-    sizes = [lax.axis_size(axes) for axes in ROUND]
+        second_kernel, [((8, 8, PARTS + 2 * CELLS), f32)], packets, turned, flops=1 << 29
+    )
+    part = swap_all(part, BRICK).reshape(count, PARTS + 2 * CELLS)
+
+    sum_shape = ((8, 32, WIDTH), f32)
     state, resp, near, far, means_out, totals = call(
         likely_kernel,
-        [state_shape] + resp_shapes + [((2, WIDTH), f32), ((sizes[0], 16, WIDTH), f32)],
-        core, tile, part, kept, total, scalars=2,
-    )
-    totals = swap_all(totals, ROUND[0])
+        [state_shape] + resp_shapes + [((2, WIDTH), f32), sum_shape],
+        core, tile, part, kept, cover, scalars=2,
+    )
+    totals = swap_lines(totals, NEAR)
     resp, near, far, totals = call(
-        middle_kernel, resp_shapes + [((sizes[1], 8, WIDTH), f32)],
+        middle_kernel, resp_shapes + [sum_shape],
         core, state, *halos(resp, near, far), totals, scalars=1,
     )
-    totals = swap_all(totals, ROUND[1])
+    totals = swap_lines(totals, FAR)
     sides = halos(resp, near, far)
     resp_final, score = pl.pallas_call(
         last_kernel,

time: 162 us -> 162 us (level)
  the two profiles are of different devices: /device:TPU:31 before, /device:TPU:27 now
where the time goes in v8:
time: 162 us; the launch traced here: 161 us
  starting transfers between devices  90.2 us (56%)
  blocking collectives  46 us (28%)
  Pallas kernels  14.5 us (9%)
  waiting for transfers between devices  9.82 us (6%)
    ppermute x16, starting transfers between devices, swapped(): return lax.ppermute(part, axes, pairs + [(j, i) for i, j in pairs])  67.7 us
    all_to_all x3, blocking collectives, swap_lines(): lax.all_to_all(value, PLANE, 0, 0, axis_index_groups=groups, tiled=True)  37.8 us
    all_to_all x2, starting transfers between devices, swap_all(): return lax.all_to_all(value, axes, 0, 0, tiled=True)  14.2 us
    pallas_call x8, Pallas kernels, call(): pl.pallas_call(kernel, out_shape=out, in_specs=[SMEM] * scalars + [VMEM]...  9.36 us
    all_to_all x2, starting transfers between devices, swap_lines(): lax.all_to_all(value, PLANE, 0, 0, axis_index_groups=groups, tiled=True)  8.31 us
    all_to_all x1, blocking collectives, swap_all(): return lax.all_to_all(value, axes, 0, 0, tiled=True)  8.12 us
    all_to_all x2, waiting for transfers between devices, swap_all(): return lax.all_to_all(value, axes, 0, 0, tiled=True)  5.12 us
    ppermute x16, waiting for transfers between devices, swapped(): return lax.ppermute(part, axes, pairs + [(j, i) for i, j in pairs])  4.69 us
  transfers between devices with their start and end apart: 20, of which 6 were waited for; matrix products, arithmetic and copies ran while one was open for 0% of the time, Pallas kernels for 0%

profile of v8, /device:TPU:27, one launch (start us, length us, event | category | flops | bytes accessed | tf_op | source)
XLA Modules:
  0.0 161.4 jit_solution(12865199201401494124)
XLA Ops:
  0.6 4.3 %shard_map.76 = (f32[136,256]{1,0:T(8,128)}, f32[64,256]{1,0:T(8,128)}, f32[64,128]{1,0:T(8,128)}, f32[64,128]{1,0:T(8,128)}, f32[8,264,128]{2,1,0:T(8,128)}) custom-call(s32[1]{0:T(128)} %bitcast.core, f32[1,64]{1,0:T(1,128)} %bitcast.15, bf16[256,128]{1,0:T(8,128)(2,1)} %bitcast.13, s32[2,128]{1,0:T(2,128)} %bitcast.14, f32[64,128]{1,0:T(8,128)} %means.1, ...), custom_call_target="tpu_custom_call" | custom-call | flops 536870912 | bytes 2097152 | tf_op jit(solution)/shard_map/pallas_call | solution.py:140
  4.9 0.0 copy-start.1
  5.0 0.0 copy-start.3
  5.0 0.0 copy-start.2
  5.0 0.0 copy-start
  5.0 5.3 %all-to-all-start = ((f32[8,264,128]{2,1,0:T(8,128)}), f32[8,264,128]{2,1,0:T(8,128)S(1)}, u32[]{:S(2)}, u32[]{:S(2)}) async-start(f32[8,264,128]{2,1,0:T(8,128)} %get-tuple-element.39), calls=%async_computation | async-start | bytes 2162688 | tf_op jit(solution)/shard_map/all_to_all | solution.py:417
  10.3 0.0 copy-done.1
  10.3 5.8 %collective-permute-start = (f32[64,256]{1,0:T(8,128)S(1)}, f32[64,256]{1,0:T(8,128)S(1)}, u32[]{:S(2)}, u32[]{:S(2)}) collective-permute-start(f32[64,256]{1,0:T(8,128)S(1)} %copy-done.1), channel_id=1, source_target_pairs={{0,32},{64,96},{128,160},{192,224},{256,288},{320,352},{384,416},{... | collective-permute-start | bytes 196616 | tf_op jit(solution)/shard_map/ppermute | solution.py:221
  16.1 6.8 %collective-permute-start.1 = (f32[64,256]{1,0:T(8,128)S(1)}, f32[64,256]{1,0:T(8,128)S(1)}, u32[]{:S(2)}, u32[]{:S(2)}) collective-permute-start(f32[64,256]{1,0:T(8,128)S(1)} %copy-done.1), channel_id=1, source_target_pairs={{32,64},{96,128},{160,192},{224,256},{288,320},{352,384},{416,448}... | collective-permute-start | bytes 196616 | tf_op jit(solution)/shard_map/ppermute | solution.py:221
  22.9 0.0 copy-done.3
  22.9 4.9 %collective-permute-start.2 = (f32[64,128]{1,0:T(8,128)S(1)}, f32[64,128]{1,0:T(8,128)S(1)}, u32[]{:S(2)}, u32[]{:S(2)}) collective-permute-start(f32[64,128]{1,0:T(8,128)S(1)} %copy-done.3), channel_id=1, source_target_pairs={{1,2},{3,4},{5,6},{7,8},{9,10},{11,12},{13,14},{15,16},{17,18},{19... | collective-permute-start | bytes 98312 | tf_op jit(solution)/shard_map/ppermute | solution.py:221
  27.8 0.0 copy-done.2
  27.8 1.9 %collective-permute-start.3 = (f32[64,128]{1,0:T(8,128)S(1)}, f32[64,128]{1,0:T(8,128)S(1)}, u32[]{:S(2)}, u32[]{:S(2)}) collective-permute-start(f32[64,128]{1,0:T(8,128)S(1)} %copy-done.2), channel_id=1, source_target_pairs={{0,1},{2,3},{4,5},{6,7},{8,9},{10,11},{12,13},{14,15},{16,17},{18,... | collective-permute-start | bytes 98312 | tf_op jit(solution)/shard_map/ppermute | solution.py:221
  29.7 0.0 collective-permute-done.2.far_in
  29.8 1.2 collective-permute-done.3.near_in
  30.9 0.0 collective-permute-done.slab_even
  30.9 0.0 collective-permute-done.1.slab_odd
  30.9 0.0 copy-done
  30.9 0.1 shard_map.77
  31.1 0.0 all-to-all-done.shared
  31.1 4.6 %collective-permute-start.4 = (f32[64,256]{1,0:T(8,128)S(1)}, f32[64,256]{1,0:T(8,128)S(1)}, u32[]{:S(2)}, u32[]{:S(2)}) collective-permute-start(f32[64,256]{1,0:T(8,128)S(1)} %get-tuple-element.40.resp), channel_id=1, source_target_pairs={{0,32},{64,96},{128,160},{192,224},{256,288},{320,352},{384,416},{... | collective-permute-start | bytes 196616 | tf_op jit(solution)/shard_map/ppermute | solution.py:221
  35.7 2.7 %collective-permute-start.5 = (f32[64,256]{1,0:T(8,128)S(1)}, f32[64,256]{1,0:T(8,128)S(1)}, u32[]{:S(2)}, u32[]{:S(2)}) collective-permute-start(f32[64,256]{1,0:T(8,128)S(1)} %get-tuple-element.40.resp), channel_id=1, source_target_pairs={{32,64},{96,128},{160,192},{224,256},{288,320},{352,384},{416,448}... | collective-permute-start | bytes 196616 | tf_op jit(solution)/shard_map/ppermute | solution.py:221
  38.4 5.7 %collective-permute-start.6 = (f32[64,128]{1,0:T(8,128)S(1)}, f32[64,128]{1,0:T(8,128)S(1)}, u32[]{:S(2)}, u32[]{:S(2)}) collective-permute-start(f32[64,128]{1,0:T(8,128)S(1)} %get-tuple-element.41), channel_id=1, source_target_pairs={{1,2},{3,4},{5,6},{7,8},{9,10},{11,12},{13,14},{15,16},{17,18},{19... | collective-permute-start | bytes 98312 | tf_op jit(solution)/shard_map/ppermute | solution.py:221
  44.1 1.9 %collective-permute-start.7 = (f32[64,128]{1,0:T(8,128)S(1)}, f32[64,128]{1,0:T(8,128)S(1)}, u32[]{:S(2)}, u32[]{:S(2)}) collective-permute-start(f32[64,128]{1,0:T(8,128)S(1)} %get-tuple-element.42), channel_id=1, source_target_pairs={{0,1},{2,3},{4,5},{6,7},{8,9},{10,11},{12,13},{14,15},{16,17},{18,... | collective-permute-start | bytes 98312 | tf_op jit(solution)/shard_map/ppermute | solution.py:221
  46.0 0.0 collective-permute-done.6.far_in
  46.0 1.2 collective-permute-done.7.near_in
  47.2 0.0 collective-permute-done.4.slab_even
  47.2 0.0 collective-permute-done.5.slab_odd
  47.2 0.1 shard_map.78
  47.4 8.1 %all_to_all.40.resp = f32[8,8,256]{2,1,0:T(8,128)S(1)} all-to-all(f32[8,8,256]{2,1,0:T(8,128)S(1)} %bitcast.12), channel_id=1, replica_groups=mesh['x1'=2,'x0'=2,'z2'=2,'z1'=2,'z0'=2,'y2'=2,'y1'=2,'y0'=2,'core'=2] {..., dimensions={0} | all-to-all | bytes 131072 | tf_op jit(solution)/shard_map/all_to_all | solution.py:417
  55.5 1.6 shard_map.79
  57.0 13.6 %all_to_all.41.packets = f32[8,72,128]{2,1,0:T(8,128)S(1)} all-to-all(f32[8,72,128]{2,1,0:T(8,128)S(1)} %get-tuple-element.44), channel_id=1, replica_groups={{0,2,4,6,8,10,12,14},{16,18,20,22,24,26,28,30},{32,34,36,38,40,42,44,46..., dimensions={0} | all-to-all | bytes 589824 | tf_op jit(solution)/shard_map/all_to_all | solution.py:421
  70.7 12.2 %all_to_all.42.packets = f32[8,72,128]{2,1,0:T(8,128)S(1)} all-to-all(f32[8,72,128]{2,1,0:T(8,128)S(1)} %shard_map.80), channel_id=1, replica_groups={{0,16,32,48,64,80,96,112},{2,18,34,50,66,82,98,114},{4,20,36,52,68,84,1..., dimensions={0} | all-to-all | bytes 589824 | tf_op jit(solution)/shard_map/all_to_all | solution.py:421
  82.9 3.9 %shard_map.81 = f32[8,72,128]{2,1,0:T(8,128)S(1)} custom-call(f32[8,72,128]{2,1,0:T(8,128)S(1)} %all_to_all.42.packets), custom_call_target="tpu_custom_call" | custom-call | flops 134217728 | bytes 1048576 | tf_op jit(solution)/shard_map/pallas_call | solution.py:36
  86.8 12.0 %all_to_all.43.packets = f32[8,72,128]{2,1,0:T(8,128)S(1)} all-to-all(f32[8,72,128]{2,1,0:T(8,128)S(1)} %shard_map.81), channel_id=1, replica_groups={{0,2,4,6,8,10,12,14},{16,18,20,22,24,26,28,30},{32,34,36,38,40,42,44,46..., dimensions={0} | all-to-all | bytes 589824 | tf_op jit(solution)/shard_map/all_to_all | solution.py:421
  98.8 2.1 %shard_map.82 = f32[8,8,896]{2,1,0:T(8,128)} custom-call(f32[8,72,128]{2,1,0:T(8,128)S(1)} %all_to_all.43.packets, bf16[8,128,256]{2,1,0:T(8,128)(2,1)S(1)} %get-tuple-element.45.turned), custom_call_target="tpu_custom_call" | custom-call | flops 536870912 | bytes 1048576 | tf_op jit(solution)/shard_map/pallas_call | solution.py:36
  100.9 8.9 %all-to-all-start.5 = ((f32[8,8,896]{2,1,0:T(8,128)}), f32[8,8,896]{2,1,0:T(8,128)S(1)}, u32[]{:S(2)}, u32[]{:S(2)}) async-start(f32[8,8,896]{2,1,0:T(8,128)} %shard_map.82), calls=%async_computation.5 | async-start | bytes 458752 | tf_op jit(solution)/shard_map/all_to_all | solution.py:417
  109.9 5.1 %all-to-all-done.5 = f32[8,8,896]{2,1,0:T(8,128)S(1)} async-done(((f32[8,8,896]{2,1,0:T(8,128)}), f32[8,8,896]{2,1,0:T(8,128)S(1)}, u32[]{:S(2)}, u32[]{:S(2)}) %all-to-all-start.5) | async-done | bytes 229408 | tf_op jit(solution)/shard_map/all_to_all | solution.py:417
  115.0 0.8 shard_map.83
  115.8 3.4 %all-to-all-start.6 = ((f32[8,32,128]{2,1,0:T(8,128)}), f32[8,32,128]{2,1,0:T(8,128)S(1)}, u32[]{:S(2)}, u32[]{:S(2)}) async-start(f32[8,32,128]{2,1,0:T(8,128)} %get-tuple-element.51), calls=%async_computation.6 | async-start | bytes 262144 | tf_op jit(solution)/shard_map/all_to_all | solution.py:421
  119.1 4.2 %collective-permute-start.8 = (f32[64,256]{1,0:T(8,128)S(1)}, f32[64,256]{1,0:T(8,128)S(1)}, u32[]{:S(2)}, u32[]{:S(2)}) collective-permute-start(f32[64,256]{1,0:T(8,128)S(1)} %get-tuple-element.48), channel_id=1, source_target_pairs={{0,32},{64,96},{128,160},{192,224},{256,288},{320,352},{384,416},{... | collective-permute-start | bytes 196616 | tf_op jit(solution)/shard_map/ppermute | solution.py:221
  123.3 6.1 %collective-permute-start.9 = (f32[64,256]{1,0:T(8,128)S(1)}, f32[64,256]{1,0:T(8,128)S(1)}, u32[]{:S(2)}, u32[]{:S(2)}) collective-permute-start(f32[64,256]{1,0:T(8,128)S(1)} %get-tuple-element.48), channel_id=1, source_target_pairs={{32,64},{96,128},{160,192},{224,256},{288,320},{352,384},{416,448}... | collective-permute-start | bytes 196616 | tf_op jit(solution)/shard_map/ppermute | solution.py:221
  129.4 3.9 %collective-permute-start.10 = (f32[64,128]{1,0:T(8,128)S(1)}, f32[64,128]{1,0:T(8,128)S(1)}, u32[]{:S(2)}, u32[]{:S(2)}) collective-permute-start(f32[64,128]{1,0:T(8,128)S(1)} %get-tuple-element.49), channel_id=1, source_target_pairs={{1,2},{3,4},{5,6},{7,8},{9,10},{11,12},{13,14},{15,16},{17,18},{19... | collective-permute-start | bytes 98312 | tf_op jit(solution)/shard_map/ppermute | solution.py:221
  133.4 1.9 %collective-permute-start.11 = (f32[64,128]{1,0:T(8,128)S(1)}, f32[64,128]{1,0:T(8,128)S(1)}, u32[]{:S(2)}, u32[]{:S(2)}) collective-permute-start(f32[64,128]{1,0:T(8,128)S(1)} %get-tuple-element.50), channel_id=1, source_target_pairs={{0,1},{2,3},{4,5},{6,7},{8,9},{10,11},{12,13},{14,15},{16,17},{18,... | collective-permute-start | bytes 98312 | tf_op jit(solution)/shard_map/ppermute | solution.py:221
  135.3 0.6 collective-permute-done.10.far_in
  135.9 0.6 collective-permute-done.11.near_in
  136.5 0.0 collective-permute-done.8.slab_even
  136.5 0.0 collective-permute-done.9.slab_odd
  136.5 0.0 all-to-all-done.6.totals
  136.5 0.7 shard_map.84
  137.2 4.9 %all-to-all-start.7 = ((f32[8,32,128]{2,1,0:T(8,128)}), f32[8,32,128]{2,1,0:T(8,128)S(1)}, u32[]{:S(2)}, u32[]{:S(2)}) async-start(f32[8,32,128]{2,1,0:T(8,128)} %get-tuple-element.55), calls=%async_computation.7 | async-start | bytes 262144 | tf_op jit(solution)/shard_map/all_to_all | solution.py:421
  142.1 2.6 %collective-permute-start.12 = (f32[64,256]{1,0:T(8,128)S(1)}, f32[64,256]{1,0:T(8,128)S(1)}, u32[]{:S(2)}, u32[]{:S(2)}) collective-permute-start(f32[64,256]{1,0:T(8,128)S(1)} %get-tuple-element.52.resp), channel_id=1, source_target_pairs={{0,32},{64,96},{128,160},{192,224},{256,288},{320,352},{384,416},{... | collective-permute-start | bytes 196616 | tf_op jit(solution)/shard_map/ppermute | solution.py:221
  144.7 6.2 %collective-permute-start.13 = (f32[64,256]{1,0:T(8,128)S(1)}, f32[64,256]{1,0:T(8,128)S(1)}, u32[]{:S(2)}, u32[]{:S(2)}) collective-permute-start(f32[64,256]{1,0:T(8,128)S(1)} %get-tuple-element.52.resp), channel_id=1, source_target_pairs={{32,64},{96,128},{160,192},{224,256},{288,320},{352,384},{416,448}... | collective-permute-start | bytes 196616 | tf_op jit(solution)/shard_map/ppermute | solution.py:221
  150.9 6.6 %collective-permute-start.14 = (f32[64,128]{1,0:T(8,128)S(1)}, f32[64,128]{1,0:T(8,128)S(1)}, u32[]{:S(2)}, u32[]{:S(2)}) collective-permute-start(f32[64,128]{1,0:T(8,128)S(1)} %get-tuple-element.53), channel_id=1, source_target_pairs={{1,2},{3,4},{5,6},{7,8},{9,10},{11,12},{13,14},{15,16},{17,18},{19... | collective-permute-start | bytes 98312 | tf_op jit(solution)/shard_map/ppermute | solution.py:221
  157.5 1.9 %collective-permute-start.15 = (f32[64,128]{1,0:T(8,128)S(1)}, f32[64,128]{1,0:T(8,128)S(1)}, u32[]{:S(2)}, u32[]{:S(2)}) collective-permute-start(f32[64,128]{1,0:T(8,128)S(1)} %get-tuple-element.54), channel_id=1, source_target_pairs={{0,1},{2,3},{4,5},{6,7},{8,9},{10,11},{12,13},{14,15},{16,17},{18,... | collective-permute-start | bytes 98312 | tf_op jit(solution)/shard_map/ppermute | solution.py:221
  159.4 0.0 collective-permute-done.14.far_in
  159.4 1.2 collective-permute-done.15.near_in
  160.6 0.0 collective-permute-done.12.slab_even
  160.6 0.0 collective-permute-done.13.slab_odd
  160.6 0.0 all-to-all-done.7.totals
  160.6 0.8 shard_map.85
  (1 shorter events, 0.0 us)
Async XLA Ops:
  4.9 5.3 %copy-start.1 = (f32[64,256]{1,0:T(8,128)S(1)}, f32[64,256]{1,0:T(8,128)}, u32[]{:S(2)}) copy-start(f32[64,256]{1,0:T(8,128)} %get-tuple-element.32) | copy-start | bytes 196612
  5.0 17.9 %copy-start.3 = (f32[64,128]{1,0:T(8,128)S(1)}, f32[64,128]{1,0:T(8,128)}, u32[]{:S(2)}) copy-start(f32[64,128]{1,0:T(8,128)} %get-tuple-element.33) | copy-start | bytes 98308
  5.0 22.8 %copy-start.2 = (f32[64,128]{1,0:T(8,128)S(1)}, f32[64,128]{1,0:T(8,128)}, u32[]{:S(2)}) copy-start(f32[64,128]{1,0:T(8,128)} %get-tuple-element.34) | copy-start | bytes 98308
  5.0 25.9 %copy-start = (f32[136,256]{1,0:T(8,128)S(1)}, f32[136,256]{1,0:T(8,128)}, u32[]{:S(2)}) copy-start(f32[136,256]{1,0:T(8,128)} %get-tuple-element.31.state) | copy-start | bytes 417796
  5.0 26.1 %all-to-all-start = ((f32[8,264,128]{2,1,0:T(8,128)}), f32[8,264,128]{2,1,0:T(8,128)S(1)}, u32[]{:S(2)}, u32[]{:S(2)}) async-start(f32[8,264,128]{2,1,0:T(8,128)} %get-tuple-element.39), calls=%async_computation | async-start | bytes 2162688 | tf_op jit(solution)/shard_map/all_to_all | solution.py:417
  10.3 20.6 %collective-permute-start = (f32[64,256]{1,0:T(8,128)S(1)}, f32[64,256]{1,0:T(8,128)S(1)}, u32[]{:S(2)}, u32[]{:S(2)}) collective-permute-start(f32[64,256]{1,0:T(8,128)S(1)} %copy-done.1), channel_id=1, source_target_pairs={{0,32},{64,96},{128,160},{192,224},{256,288},{320,352},{384,416},{... | collective-permute-start | bytes 196616 | tf_op jit(solution)/shard_map/ppermute | solution.py:221
  16.1 14.8 %collective-permute-start.1 = (f32[64,256]{1,0:T(8,128)S(1)}, f32[64,256]{1,0:T(8,128)S(1)}, u32[]{:S(2)}, u32[]{:S(2)}) collective-permute-start(f32[64,256]{1,0:T(8,128)S(1)} %copy-done.1), channel_id=1, source_target_pairs={{32,64},{96,128},{160,192},{224,256},{288,320},{352,384},{416,448}... | collective-permute-start | bytes 196616 | tf_op jit(solution)/shard_map/ppermute | solution.py:221
  22.9 6.8 %collective-permute-start.2 = (f32[64,128]{1,0:T(8,128)S(1)}, f32[64,128]{1,0:T(8,128)S(1)}, u32[]{:S(2)}, u32[]{:S(2)}) collective-permute-start(f32[64,128]{1,0:T(8,128)S(1)} %copy-done.3), channel_id=1, source_target_pairs={{1,2},{3,4},{5,6},{7,8},{9,10},{11,12},{13,14},{15,16},{17,18},{19... | collective-permute-start | bytes 98312 | tf_op jit(solution)/shard_map/ppermute | solution.py:221
  27.8 3.1 %collective-permute-start.3 = (f32[64,128]{1,0:T(8,128)S(1)}, f32[64,128]{1,0:T(8,128)S(1)}, u32[]{:S(2)}, u32[]{:S(2)}) collective-permute-start(f32[64,128]{1,0:T(8,128)S(1)} %copy-done.2), channel_id=1, source_target_pairs={{0,1},{2,3},{4,5},{6,7},{8,9},{10,11},{12,13},{14,15},{16,17},{18,... | collective-permute-start | bytes 98312 | tf_op jit(solution)/shard_map/ppermute | solution.py:221
  31.1 16.1 %collective-permute-start.4 = (f32[64,256]{1,0:T(8,128)S(1)}, f32[64,256]{1,0:T(8,128)S(1)}, u32[]{:S(2)}, u32[]{:S(2)}) collective-permute-start(f32[64,256]{1,0:T(8,128)S(1)} %get-tuple-element.40.resp), channel_id=1, source_target_pairs={{0,32},{64,96},{128,160},{192,224},{256,288},{320,352},{384,416},{... | collective-permute-start | bytes 196616 | tf_op jit(solution)/shard_map/ppermute | solution.py:221
  35.7 11.5 %collective-permute-start.5 = (f32[64,256]{1,0:T(8,128)S(1)}, f32[64,256]{1,0:T(8,128)S(1)}, u32[]{:S(2)}, u32[]{:S(2)}) collective-permute-start(f32[64,256]{1,0:T(8,128)S(1)} %get-tuple-element.40.resp), channel_id=1, source_target_pairs={{32,64},{96,128},{160,192},{224,256},{288,320},{352,384},{416,448}... | collective-permute-start | bytes 196616 | tf_op jit(solution)/shard_map/ppermute | solution.py:221
  38.4 7.7 %collective-permute-start.6 = (f32[64,128]{1,0:T(8,128)S(1)}, f32[64,128]{1,0:T(8,128)S(1)}, u32[]{:S(2)}, u32[]{:S(2)}) collective-permute-start(f32[64,128]{1,0:T(8,128)S(1)} %get-tuple-element.41), channel_id=1, source_target_pairs={{1,2},{3,4},{5,6},{7,8},{9,10},{11,12},{13,14},{15,16},{17,18},{19... | collective-permute-start | bytes 98312 | tf_op jit(solution)/shard_map/ppermute | solution.py:221
  44.1 3.1 %collective-permute-start.7 = (f32[64,128]{1,0:T(8,128)S(1)}, f32[64,128]{1,0:T(8,128)S(1)}, u32[]{:S(2)}, u32[]{:S(2)}) collective-permute-start(f32[64,128]{1,0:T(8,128)S(1)} %get-tuple-element.42), channel_id=1, source_target_pairs={{0,1},{2,3},{4,5},{6,7},{8,9},{10,11},{12,13},{14,15},{16,17},{18,... | collective-permute-start | bytes 98312 | tf_op jit(solution)/shard_map/ppermute | solution.py:221
  100.9 14.0 %all-to-all-start.5 = ((f32[8,8,896]{2,1,0:T(8,128)}), f32[8,8,896]{2,1,0:T(8,128)S(1)}, u32[]{:S(2)}, u32[]{:S(2)}) async-start(f32[8,8,896]{2,1,0:T(8,128)} %shard_map.82), calls=%async_computation.5 | async-start | bytes 458752 | tf_op jit(solution)/shard_map/all_to_all | solution.py:417
  115.8 20.7 %all-to-all-start.6 = ((f32[8,32,128]{2,1,0:T(8,128)}), f32[8,32,128]{2,1,0:T(8,128)S(1)}, u32[]{:S(2)}, u32[]{:S(2)}) async-start(f32[8,32,128]{2,1,0:T(8,128)} %get-tuple-element.51), calls=%async_computation.6 | async-start | bytes 262144 | tf_op jit(solution)/shard_map/all_to_all | solution.py:421
  119.1 17.3 %collective-permute-start.8 = (f32[64,256]{1,0:T(8,128)S(1)}, f32[64,256]{1,0:T(8,128)S(1)}, u32[]{:S(2)}, u32[]{:S(2)}) collective-permute-start(f32[64,256]{1,0:T(8,128)S(1)} %get-tuple-element.48), channel_id=1, source_target_pairs={{0,32},{64,96},{128,160},{192,224},{256,288},{320,352},{384,416},{... | collective-permute-start | bytes 196616 | tf_op jit(solution)/shard_map/ppermute | solution.py:221
  123.3 13.2 %collective-permute-start.9 = (f32[64,256]{1,0:T(8,128)S(1)}, f32[64,256]{1,0:T(8,128)S(1)}, u32[]{:S(2)}, u32[]{:S(2)}) collective-permute-start(f32[64,256]{1,0:T(8,128)S(1)} %get-tuple-element.48), channel_id=1, source_target_pairs={{32,64},{96,128},{160,192},{224,256},{288,320},{352,384},{416,448}... | collective-permute-start | bytes 196616 | tf_op jit(solution)/shard_map/ppermute | solution.py:221
  129.4 6.4 %collective-permute-start.10 = (f32[64,128]{1,0:T(8,128)S(1)}, f32[64,128]{1,0:T(8,128)S(1)}, u32[]{:S(2)}, u32[]{:S(2)}) collective-permute-start(f32[64,128]{1,0:T(8,128)S(1)} %get-tuple-element.49), channel_id=1, source_target_pairs={{1,2},{3,4},{5,6},{7,8},{9,10},{11,12},{13,14},{15,16},{17,18},{19... | collective-permute-start | bytes 98312 | tf_op jit(solution)/shard_map/ppermute | solution.py:221
  133.4 3.1 %collective-permute-start.11 = (f32[64,128]{1,0:T(8,128)S(1)}, f32[64,128]{1,0:T(8,128)S(1)}, u32[]{:S(2)}, u32[]{:S(2)}) collective-permute-start(f32[64,128]{1,0:T(8,128)S(1)} %get-tuple-element.50), channel_id=1, source_target_pairs={{0,1},{2,3},{4,5},{6,7},{8,9},{10,11},{12,13},{14,15},{16,17},{18,... | collective-permute-start | bytes 98312 | tf_op jit(solution)/shard_map/ppermute | solution.py:221
  137.2 23.4 %all-to-all-start.7 = ((f32[8,32,128]{2,1,0:T(8,128)}), f32[8,32,128]{2,1,0:T(8,128)S(1)}, u32[]{:S(2)}, u32[]{:S(2)}) async-start(f32[8,32,128]{2,1,0:T(8,128)} %get-tuple-element.55), calls=%async_computation.7 | async-start | bytes 262144 | tf_op jit(solution)/shard_map/all_to_all | solution.py:421
  142.1 18.5 %collective-permute-start.12 = (f32[64,256]{1,0:T(8,128)S(1)}, f32[64,256]{1,0:T(8,128)S(1)}, u32[]{:S(2)}, u32[]{:S(2)}) collective-permute-start(f32[64,256]{1,0:T(8,128)S(1)} %get-tuple-element.52.resp), channel_id=1, source_target_pairs={{0,32},{64,96},{128,160},{192,224},{256,288},{320,352},{384,416},{... | collective-permute-start | bytes 196616 | tf_op jit(solution)/shard_map/ppermute | solution.py:221
  144.7 15.9 %collective-permute-start.13 = (f32[64,256]{1,0:T(8,128)S(1)}, f32[64,256]{1,0:T(8,128)S(1)}, u32[]{:S(2)}, u32[]{:S(2)}) collective-permute-start(f32[64,256]{1,0:T(8,128)S(1)} %get-tuple-element.52.resp), channel_id=1, source_target_pairs={{32,64},{96,128},{160,192},{224,256},{288,320},{352,384},{416,448}... | collective-permute-start | bytes 196616 | tf_op jit(solution)/shard_map/ppermute | solution.py:221
  150.9 8.5 %collective-permute-start.14 = (f32[64,128]{1,0:T(8,128)S(1)}, f32[64,128]{1,0:T(8,128)S(1)}, u32[]{:S(2)}, u32[]{:S(2)}) collective-permute-start(f32[64,128]{1,0:T(8,128)S(1)} %get-tuple-element.53), channel_id=1, source_target_pairs={{1,2},{3,4},{5,6},{7,8},{9,10},{11,12},{13,14},{15,16},{17,18},{19... | collective-permute-start | bytes 98312 | tf_op jit(solution)/shard_map/ppermute | solution.py:221
  157.5 3.1 %collective-permute-start.15 = (f32[64,128]{1,0:T(8,128)S(1)}, f32[64,128]{1,0:T(8,128)S(1)}, u32[]{:S(2)}, u32[]{:S(2)}) collective-permute-start(f32[64,128]{1,0:T(8,128)S(1)} %get-tuple-element.54), channel_id=1, source_target_pairs={{0,1},{2,3},{4,5},{6,7},{8,9},{10,11},{12,13},{14,15},{16,17},{18,... | collective-permute-start | bytes 98312 | tf_op jit(solution)/shard_map/ppermute | solution.py:221

commit v9 on v7

--- a/solution.py
+++ b/solution.py
@@ -442,7 +442,7 @@
     sizes = [lax.axis_size(axes) for axes in ROUND]
     state, resp, near, far, means_out, totals = call(
         likely_kernel,
-        [state_shape] + resp_shapes + [((2, WIDTH), f32), ((sizes[0], 16, WIDTH), f32)],
+        [state_shape] + resp_shapes + [((2, WIDTH), f32), ((sizes[0], 8, WIDTH), f32)],
         core, tile, part, kept, total, scalars=2,
     )
     totals = swap_all(totals, ROUND[0])

time: 162 us -> 162 us (level)
  no operation moved by 1% of the time
where the time goes in v9:
time: 162 us; the launch traced here: 161 us
  starting transfers between devices  89.7 us (55%)
  blocking collectives  47.6 us (29%)
  Pallas kernels  14.4 us (9%)
  waiting for transfers between devices  7.95 us (5%)
    ppermute x16, starting transfers between devices, swapped(): return lax.ppermute(part, axes, pairs + [(j, i) for i, j in pairs])  58.7 us
    all_to_all x3, blocking collectives, swap_lines(): lax.all_to_all(value, PLANE, 0, 0, axis_index_groups=groups, tiled=True)  37.8 us
    all_to_all x4, starting transfers between devices, swap_all(): return lax.all_to_all(value, axes, 0, 0, tiled=True)  31 us
    all_to_all x1, blocking collectives, swap_all(): return lax.all_to_all(value, axes, 0, 0, tiled=True)  9.75 us
    pallas_call x8, Pallas kernels, call(): pl.pallas_call(kernel, out_shape=out, in_specs=[SMEM] * scalars + [VMEM]...  9.29 us
    ppermute x16, waiting for transfers between devices, swapped(): return lax.ppermute(part, axes, pairs + [(j, i) for i, j in pairs])  4.7 us
    pallas_call x1, Pallas kernels, start(): pl.pallas_call(start_kernel, out_shape=[jax.ShapeDtypeStruct(shape, f32)...  4.28 us
    all_to_all x4, waiting for transfers between devices, swap_all(): return lax.all_to_all(value, axes, 0, 0, tiled=True)  3.25 us
  transfers between devices with their start and end apart: 20, of which 6 were waited for; matrix products, arithmetic and copies ran while one was open for 0% of the time, Pallas kernels for 0%

profile of v9, /device:TPU:31, one launch (start us, length us, event | category | flops | bytes accessed | tf_op | source)
XLA Modules:
  0.0 160.6 jit_solution(10910086197389070051)
XLA Ops:
  0.6 4.3 %shard_map.76 = (f32[136,256]{1,0:T(8,128)}, f32[64,256]{1,0:T(8,128)}, f32[64,128]{1,0:T(8,128)}, f32[64,128]{1,0:T(8,128)}, f32[8,256,128]{2,1,0:T(8,128)}) custom-call(s32[1]{0:T(128)} %bitcast.core, f32[1,64]{1,0:T(1,128)} %bitcast.15, bf16[256,128]{1,0:T(8,128)(2,1)} %bitcast.13, s32[2,128]{1,0:T(2,128)} %bitcast.14, f32[64,128]{1,0:T(8,128)} %means.1, ...), custom_call_target="tpu_custom_call" | custom-call | flops 536870912 | bytes 2097152 | tf_op jit(solution)/shard_map/pallas_call | solution.py:137
  4.9 0.0 copy-start.1
  4.9 0.0 copy-start.3
  4.9 0.0 copy-start.2
  5.0 0.0 copy-start
  5.0 5.2 %all-to-all-start = ((f32[8,256,128]{2,1,0:T(8,128)}), f32[8,256,128]{2,1,0:T(8,128)S(1)}, u32[]{:S(2)}, u32[]{:S(2)}) async-start(f32[8,256,128]{2,1,0:T(8,128)} %get-tuple-element.39), calls=%async_computation | async-start | bytes 2097152 | tf_op jit(solution)/shard_map/all_to_all | solution.py:398
  10.2 0.0 copy-done.1
  10.2 5.8 %collective-permute-start = (f32[64,256]{1,0:T(8,128)S(1)}, f32[64,256]{1,0:T(8,128)S(1)}, u32[]{:S(2)}, u32[]{:S(2)}) collective-permute-start(f32[64,256]{1,0:T(8,128)S(1)} %copy-done.1), channel_id=1, source_target_pairs={{0,32},{64,96},{128,160},{192,224},{256,288},{320,352},{384,416},{... | collective-permute-start | bytes 196616 | tf_op jit(solution)/shard_map/ppermute | solution.py:218
  16.0 7.3 %collective-permute-start.1 = (f32[64,256]{1,0:T(8,128)S(1)}, f32[64,256]{1,0:T(8,128)S(1)}, u32[]{:S(2)}, u32[]{:S(2)}) collective-permute-start(f32[64,256]{1,0:T(8,128)S(1)} %copy-done.1), channel_id=1, source_target_pairs={{32,64},{96,128},{160,192},{224,256},{288,320},{352,384},{416,448}... | collective-permute-start | bytes 196616 | tf_op jit(solution)/shard_map/ppermute | solution.py:218
  23.3 0.0 copy-done.3
  23.3 5.2 %collective-permute-start.2 = (f32[64,128]{1,0:T(8,128)S(1)}, f32[64,128]{1,0:T(8,128)S(1)}, u32[]{:S(2)}, u32[]{:S(2)}) collective-permute-start(f32[64,128]{1,0:T(8,128)S(1)} %copy-done.3), channel_id=1, source_target_pairs={{1,2},{3,4},{5,6},{7,8},{9,10},{11,12},{13,14},{15,16},{17,18},{19... | collective-permute-start | bytes 98312 | tf_op jit(solution)/shard_map/ppermute | solution.py:218
  28.6 0.0 copy-done.2
  28.6 1.9 %collective-permute-start.3 = (f32[64,128]{1,0:T(8,128)S(1)}, f32[64,128]{1,0:T(8,128)S(1)}, u32[]{:S(2)}, u32[]{:S(2)}) collective-permute-start(f32[64,128]{1,0:T(8,128)S(1)} %copy-done.2), channel_id=1, source_target_pairs={{0,1},{2,3},{4,5},{6,7},{8,9},{10,11},{12,13},{14,15},{16,17},{18,... | collective-permute-start | bytes 98312 | tf_op jit(solution)/shard_map/ppermute | solution.py:218
  30.5 0.0 collective-permute-done.2.far_in
  30.5 1.2 collective-permute-done.3.near_in
  31.7 0.0 collective-permute-done.slab_even
  31.7 0.0 collective-permute-done.1.slab_odd
  31.7 0.0 copy-done
  31.7 0.2 shard_map.77
  31.9 0.0 all-to-all-done.shared
  31.9 3.7 %collective-permute-start.4 = (f32[64,256]{1,0:T(8,128)S(1)}, f32[64,256]{1,0:T(8,128)S(1)}, u32[]{:S(2)}, u32[]{:S(2)}) collective-permute-start(f32[64,256]{1,0:T(8,128)S(1)} %get-tuple-element.40.resp), channel_id=1, source_target_pairs={{0,32},{64,96},{128,160},{192,224},{256,288},{320,352},{384,416},{... | collective-permute-start | bytes 196616 | tf_op jit(solution)/shard_map/ppermute | solution.py:218
  35.6 1.9 %collective-permute-start.5 = (f32[64,256]{1,0:T(8,128)S(1)}, f32[64,256]{1,0:T(8,128)S(1)}, u32[]{:S(2)}, u32[]{:S(2)}) collective-permute-start(f32[64,256]{1,0:T(8,128)S(1)} %get-tuple-element.40.resp), channel_id=1, source_target_pairs={{32,64},{96,128},{160,192},{224,256},{288,320},{352,384},{416,448}... | collective-permute-start | bytes 196616 | tf_op jit(solution)/shard_map/ppermute | solution.py:218
  37.5 3.9 %collective-permute-start.6 = (f32[64,128]{1,0:T(8,128)S(1)}, f32[64,128]{1,0:T(8,128)S(1)}, u32[]{:S(2)}, u32[]{:S(2)}) collective-permute-start(f32[64,128]{1,0:T(8,128)S(1)} %get-tuple-element.41), channel_id=1, source_target_pairs={{1,2},{3,4},{5,6},{7,8},{9,10},{11,12},{13,14},{15,16},{17,18},{19... | collective-permute-start | bytes 98312 | tf_op jit(solution)/shard_map/ppermute | solution.py:218
  41.4 1.9 %collective-permute-start.7 = (f32[64,128]{1,0:T(8,128)S(1)}, f32[64,128]{1,0:T(8,128)S(1)}, u32[]{:S(2)}, u32[]{:S(2)}) collective-permute-start(f32[64,128]{1,0:T(8,128)S(1)} %get-tuple-element.42), channel_id=1, source_target_pairs={{0,1},{2,3},{4,5},{6,7},{8,9},{10,11},{12,13},{14,15},{16,17},{18,... | collective-permute-start | bytes 98312 | tf_op jit(solution)/shard_map/ppermute | solution.py:218
  43.4 0.9 collective-permute-done.6.far_in
  44.3 0.3 collective-permute-done.7.near_in
  44.5 0.0 collective-permute-done.4.slab_even
  44.5 0.0 collective-permute-done.5.slab_odd
  44.5 0.1 shard_map.78
  44.7 9.8 %all_to_all.40.resp = f32[8,8,256]{2,1,0:T(8,128)S(1)} all-to-all(f32[8,8,256]{2,1,0:T(8,128)S(1)} %bitcast.12), channel_id=1, replica_groups=mesh['x1'=2,'x0'=2,'z2'=2,'z1'=2,'z0'=2,'y2'=2,'y1'=2,'y0'=2,'core'=2] {..., dimensions={0} | all-to-all | bytes 131072 | tf_op jit(solution)/shard_map/all_to_all | solution.py:398
  54.4 1.6 shard_map.79
  56.0 13.6 %all_to_all.41.packets = f32[8,72,128]{2,1,0:T(8,128)S(1)} all-to-all(f32[8,72,128]{2,1,0:T(8,128)S(1)} %get-tuple-element.44), channel_id=1, replica_groups={{0,2,4,6,8,10,12,14},{16,18,20,22,24,26,28,30},{32,34,36,38,40,42,44,46..., dimensions={0} | all-to-all | bytes 589824 | tf_op jit(solution)/shard_map/all_to_all | solution.py:402
  69.7 12.2 %all_to_all.42.packets = f32[8,72,128]{2,1,0:T(8,128)S(1)} all-to-all(f32[8,72,128]{2,1,0:T(8,128)S(1)} %shard_map.80), channel_id=1, replica_groups={{0,16,32,48,64,80,96,112},{2,18,34,50,66,82,98,114},{4,20,36,52,68,84,1..., dimensions={0} | all-to-all | bytes 589824 | tf_op jit(solution)/shard_map/all_to_all | solution.py:402
  81.8 3.9 %shard_map.81 = f32[8,72,128]{2,1,0:T(8,128)S(1)} custom-call(f32[8,72,128]{2,1,0:T(8,128)S(1)} %all_to_all.42.packets), custom_call_target="tpu_custom_call" | custom-call | flops 134217728 | bytes 1048576 | tf_op jit(solution)/shard_map/pallas_call | solution.py:36
  85.7 12.0 %all_to_all.43.packets = f32[8,72,128]{2,1,0:T(8,128)S(1)} all-to-all(f32[8,72,128]{2,1,0:T(8,128)S(1)} %shard_map.81), channel_id=1, replica_groups={{0,2,4,6,8,10,12,14},{16,18,20,22,24,26,28,30},{32,34,36,38,40,42,44,46..., dimensions={0} | all-to-all | bytes 589824 | tf_op jit(solution)/shard_map/all_to_all | solution.py:402
  97.8 2.1 %shard_map.82 = f32[8,8,384]{2,1,0:T(8,128)} custom-call(f32[8,72,128]{2,1,0:T(8,128)S(1)} %all_to_all.43.packets, bf16[8,128,256]{2,1,0:T(8,128)(2,1)S(1)} %get-tuple-element.45.turned), custom_call_target="tpu_custom_call" | custom-call | flops 536870912 | bytes 1048576 | tf_op jit(solution)/shard_map/pallas_call | solution.py:36
  99.8 9.5 %all-to-all-start.5 = ((f32[8,8,384]{2,1,0:T(8,128)}), f32[8,8,384]{2,1,0:T(8,128)S(1)}, u32[]{:S(2)}, u32[]{:S(2)}) async-start(f32[8,8,384]{2,1,0:T(8,128)} %shard_map.82), calls=%async_computation.5 | async-start | bytes 196608 | tf_op jit(solution)/shard_map/all_to_all | solution.py:398
  109.4 3.2 %all-to-all-done.5 = f32[8,8,384]{2,1,0:T(8,128)S(1)} async-done(((f32[8,8,384]{2,1,0:T(8,128)}), f32[8,8,384]{2,1,0:T(8,128)S(1)}, u32[]{:S(2)}, u32[]{:S(2)}) %all-to-all-start.5) | async-done | bytes 98336 | tf_op jit(solution)/shard_map/all_to_all | solution.py:398
  112.6 0.8 shard_map.83
  113.4 7.1 %all-to-all-start.6 = ((f32[16,8,128]{2,1,0:T(8,128)}), f32[16,8,128]{2,1,0:T(8,128)S(1)}, u32[]{:S(2)}, u32[]{:S(2)}) async-start(f32[16,8,128]{2,1,0:T(8,128)} %get-tuple-element.51), calls=%async_computation.6 | async-start | bytes 131072 | tf_op jit(solution)/shard_map/all_to_all | solution.py:398
  120.4 2.1 %collective-permute-start.8 = (f32[64,256]{1,0:T(8,128)S(1)}, f32[64,256]{1,0:T(8,128)S(1)}, u32[]{:S(2)}, u32[]{:S(2)}) collective-permute-start(f32[64,256]{1,0:T(8,128)S(1)} %get-tuple-element.48), channel_id=1, source_target_pairs={{0,32},{64,96},{128,160},{192,224},{256,288},{320,352},{384,416},{... | collective-permute-start | bytes 196616 | tf_op jit(solution)/shard_map/ppermute | solution.py:218
  122.6 2.0 %collective-permute-start.9 = (f32[64,256]{1,0:T(8,128)S(1)}, f32[64,256]{1,0:T(8,128)S(1)}, u32[]{:S(2)}, u32[]{:S(2)}) collective-permute-start(f32[64,256]{1,0:T(8,128)S(1)} %get-tuple-element.48), channel_id=1, source_target_pairs={{32,64},{96,128},{160,192},{224,256},{288,320},{352,384},{416,448}... | collective-permute-start | bytes 196616 | tf_op jit(solution)/shard_map/ppermute | solution.py:218
  124.6 5.1 %collective-permute-start.10 = (f32[64,128]{1,0:T(8,128)S(1)}, f32[64,128]{1,0:T(8,128)S(1)}, u32[]{:S(2)}, u32[]{:S(2)}) collective-permute-start(f32[64,128]{1,0:T(8,128)S(1)} %get-tuple-element.49), channel_id=1, source_target_pairs={{1,2},{3,4},{5,6},{7,8},{9,10},{11,12},{13,14},{15,16},{17,18},{19... | collective-permute-start | bytes 98312 | tf_op jit(solution)/shard_map/ppermute | solution.py:218
  129.7 1.9 %collective-permute-start.11 = (f32[64,128]{1,0:T(8,128)S(1)}, f32[64,128]{1,0:T(8,128)S(1)}, u32[]{:S(2)}, u32[]{:S(2)}) collective-permute-start(f32[64,128]{1,0:T(8,128)S(1)} %get-tuple-element.50), channel_id=1, source_target_pairs={{0,1},{2,3},{4,5},{6,7},{8,9},{10,11},{12,13},{14,15},{16,17},{18,... | collective-permute-start | bytes 98312 | tf_op jit(solution)/shard_map/ppermute | solution.py:218
  131.6 0.0 collective-permute-done.10.far_in
  131.7 1.2 collective-permute-done.11.near_in
  132.8 0.0 collective-permute-done.8.slab_even
  132.8 0.0 collective-permute-done.9.slab_odd
  132.8 0.0 all-to-all-done.6.totals
  132.8 0.7 shard_map.84
  133.5 9.2 %all-to-all-start.7 = ((f32[32,8,128]{2,1,0:T(8,128)}), f32[32,8,128]{2,1,0:T(8,128)S(1)}, u32[]{:S(2)}, u32[]{:S(2)}) async-start(f32[32,8,128]{2,1,0:T(8,128)} %get-tuple-element.55), calls=%async_computation.7 | async-start | bytes 262144 | tf_op jit(solution)/shard_map/all_to_all | solution.py:398
  142.7 4.0 %collective-permute-start.12 = (f32[64,256]{1,0:T(8,128)S(1)}, f32[64,256]{1,0:T(8,128)S(1)}, u32[]{:S(2)}, u32[]{:S(2)}) collective-permute-start(f32[64,256]{1,0:T(8,128)S(1)} %get-tuple-element.52.resp), channel_id=1, source_target_pairs={{0,32},{64,96},{128,160},{192,224},{256,288},{320,352},{384,416},{... | collective-permute-start | bytes 196616 | tf_op jit(solution)/shard_map/ppermute | solution.py:218
  146.7 5.5 %collective-permute-start.13 = (f32[64,256]{1,0:T(8,128)S(1)}, f32[64,256]{1,0:T(8,128)S(1)}, u32[]{:S(2)}, u32[]{:S(2)}) collective-permute-start(f32[64,256]{1,0:T(8,128)S(1)} %get-tuple-element.52.resp), channel_id=1, source_target_pairs={{32,64},{96,128},{160,192},{224,256},{288,320},{352,384},{416,448}... | collective-permute-start | bytes 196616 | tf_op jit(solution)/shard_map/ppermute | solution.py:218
  152.2 4.5 %collective-permute-start.14 = (f32[64,128]{1,0:T(8,128)S(1)}, f32[64,128]{1,0:T(8,128)S(1)}, u32[]{:S(2)}, u32[]{:S(2)}) collective-permute-start(f32[64,128]{1,0:T(8,128)S(1)} %get-tuple-element.53), channel_id=1, source_target_pairs={{1,2},{3,4},{5,6},{7,8},{9,10},{11,12},{13,14},{15,16},{17,18},{19... | collective-permute-start | bytes 98312 | tf_op jit(solution)/shard_map/ppermute | solution.py:218
  156.7 1.9 %collective-permute-start.15 = (f32[64,128]{1,0:T(8,128)S(1)}, f32[64,128]{1,0:T(8,128)S(1)}, u32[]{:S(2)}, u32[]{:S(2)}) collective-permute-start(f32[64,128]{1,0:T(8,128)S(1)} %get-tuple-element.54), channel_id=1, source_target_pairs={{0,1},{2,3},{4,5},{6,7},{8,9},{10,11},{12,13},{14,15},{16,17},{18,... | collective-permute-start | bytes 98312 | tf_op jit(solution)/shard_map/ppermute | solution.py:218
  158.6 0.0 collective-permute-done.14.far_in
  158.6 1.1 collective-permute-done.15.near_in
  159.8 0.0 collective-permute-done.12.slab_even
  159.8 0.0 collective-permute-done.13.slab_odd
  159.8 0.0 all-to-all-done.7.totals
  159.8 0.8 shard_map.85
  (1 shorter events, 0.0 us)
Async XLA Ops:
  4.9 5.3 %copy-start.1 = (f32[64,256]{1,0:T(8,128)S(1)}, f32[64,256]{1,0:T(8,128)}, u32[]{:S(2)}) copy-start(f32[64,256]{1,0:T(8,128)} %get-tuple-element.32) | copy-start | bytes 196612
  4.9 18.4 %copy-start.3 = (f32[64,128]{1,0:T(8,128)S(1)}, f32[64,128]{1,0:T(8,128)}, u32[]{:S(2)}) copy-start(f32[64,128]{1,0:T(8,128)} %get-tuple-element.33) | copy-start | bytes 98308
  4.9 23.6 %copy-start.2 = (f32[64,128]{1,0:T(8,128)S(1)}, f32[64,128]{1,0:T(8,128)}, u32[]{:S(2)}) copy-start(f32[64,128]{1,0:T(8,128)} %get-tuple-element.34) | copy-start | bytes 98308
  5.0 26.7 %copy-start = (f32[136,256]{1,0:T(8,128)S(1)}, f32[136,256]{1,0:T(8,128)}, u32[]{:S(2)}) copy-start(f32[136,256]{1,0:T(8,128)} %get-tuple-element.31.state) | copy-start | bytes 417796
  5.0 26.9 %all-to-all-start = ((f32[8,256,128]{2,1,0:T(8,128)}), f32[8,256,128]{2,1,0:T(8,128)S(1)}, u32[]{:S(2)}, u32[]{:S(2)}) async-start(f32[8,256,128]{2,1,0:T(8,128)} %get-tuple-element.39), calls=%async_computation | async-start | bytes 2097152 | tf_op jit(solution)/shard_map/all_to_all | solution.py:398
  10.2 21.5 %collective-permute-start = (f32[64,256]{1,0:T(8,128)S(1)}, f32[64,256]{1,0:T(8,128)S(1)}, u32[]{:S(2)}, u32[]{:S(2)}) collective-permute-start(f32[64,256]{1,0:T(8,128)S(1)} %copy-done.1), channel_id=1, source_target_pairs={{0,32},{64,96},{128,160},{192,224},{256,288},{320,352},{384,416},{... | collective-permute-start | bytes 196616 | tf_op jit(solution)/shard_map/ppermute | solution.py:218
  16.0 15.7 %collective-permute-start.1 = (f32[64,256]{1,0:T(8,128)S(1)}, f32[64,256]{1,0:T(8,128)S(1)}, u32[]{:S(2)}, u32[]{:S(2)}) collective-permute-start(f32[64,256]{1,0:T(8,128)S(1)} %copy-done.1), channel_id=1, source_target_pairs={{32,64},{96,128},{160,192},{224,256},{288,320},{352,384},{416,448}... | collective-permute-start | bytes 196616 | tf_op jit(solution)/shard_map/ppermute | solution.py:218
  23.3 7.2 %collective-permute-start.2 = (f32[64,128]{1,0:T(8,128)S(1)}, f32[64,128]{1,0:T(8,128)S(1)}, u32[]{:S(2)}, u32[]{:S(2)}) collective-permute-start(f32[64,128]{1,0:T(8,128)S(1)} %copy-done.3), channel_id=1, source_target_pairs={{1,2},{3,4},{5,6},{7,8},{9,10},{11,12},{13,14},{15,16},{17,18},{19... | collective-permute-start | bytes 98312 | tf_op jit(solution)/shard_map/ppermute | solution.py:218
  28.6 3.1 %collective-permute-start.3 = (f32[64,128]{1,0:T(8,128)S(1)}, f32[64,128]{1,0:T(8,128)S(1)}, u32[]{:S(2)}, u32[]{:S(2)}) collective-permute-start(f32[64,128]{1,0:T(8,128)S(1)} %copy-done.2), channel_id=1, source_target_pairs={{0,1},{2,3},{4,5},{6,7},{8,9},{10,11},{12,13},{14,15},{16,17},{18,... | collective-permute-start | bytes 98312 | tf_op jit(solution)/shard_map/ppermute | solution.py:218
  31.9 12.7 %collective-permute-start.4 = (f32[64,256]{1,0:T(8,128)S(1)}, f32[64,256]{1,0:T(8,128)S(1)}, u32[]{:S(2)}, u32[]{:S(2)}) collective-permute-start(f32[64,256]{1,0:T(8,128)S(1)} %get-tuple-element.40.resp), channel_id=1, source_target_pairs={{0,32},{64,96},{128,160},{192,224},{256,288},{320,352},{384,416},{... | collective-permute-start | bytes 196616 | tf_op jit(solution)/shard_map/ppermute | solution.py:218
  35.6 9.0 %collective-permute-start.5 = (f32[64,256]{1,0:T(8,128)S(1)}, f32[64,256]{1,0:T(8,128)S(1)}, u32[]{:S(2)}, u32[]{:S(2)}) collective-permute-start(f32[64,256]{1,0:T(8,128)S(1)} %get-tuple-element.40.resp), channel_id=1, source_target_pairs={{32,64},{96,128},{160,192},{224,256},{288,320},{352,384},{416,448}... | collective-permute-start | bytes 196616 | tf_op jit(solution)/shard_map/ppermute | solution.py:218
  37.5 6.7 %collective-permute-start.6 = (f32[64,128]{1,0:T(8,128)S(1)}, f32[64,128]{1,0:T(8,128)S(1)}, u32[]{:S(2)}, u32[]{:S(2)}) collective-permute-start(f32[64,128]{1,0:T(8,128)S(1)} %get-tuple-element.41), channel_id=1, source_target_pairs={{1,2},{3,4},{5,6},{7,8},{9,10},{11,12},{13,14},{15,16},{17,18},{19... | collective-permute-start | bytes 98312 | tf_op jit(solution)/shard_map/ppermute | solution.py:218
  41.4 3.1 %collective-permute-start.7 = (f32[64,128]{1,0:T(8,128)S(1)}, f32[64,128]{1,0:T(8,128)S(1)}, u32[]{:S(2)}, u32[]{:S(2)}) collective-permute-start(f32[64,128]{1,0:T(8,128)S(1)} %get-tuple-element.42), channel_id=1, source_target_pairs={{0,1},{2,3},{4,5},{6,7},{8,9},{10,11},{12,13},{14,15},{16,17},{18,... | collective-permute-start | bytes 98312 | tf_op jit(solution)/shard_map/ppermute | solution.py:218
  99.8 12.8 %all-to-all-start.5 = ((f32[8,8,384]{2,1,0:T(8,128)}), f32[8,8,384]{2,1,0:T(8,128)S(1)}, u32[]{:S(2)}, u32[]{:S(2)}) async-start(f32[8,8,384]{2,1,0:T(8,128)} %shard_map.82), calls=%async_computation.5 | async-start | bytes 196608 | tf_op jit(solution)/shard_map/all_to_all | solution.py:398
  113.4 19.5 %all-to-all-start.6 = ((f32[16,8,128]{2,1,0:T(8,128)}), f32[16,8,128]{2,1,0:T(8,128)S(1)}, u32[]{:S(2)}, u32[]{:S(2)}) async-start(f32[16,8,128]{2,1,0:T(8,128)} %get-tuple-element.51), calls=%async_computation.6 | async-start | bytes 131072 | tf_op jit(solution)/shard_map/all_to_all | solution.py:398
  120.4 12.4 %collective-permute-start.8 = (f32[64,256]{1,0:T(8,128)S(1)}, f32[64,256]{1,0:T(8,128)S(1)}, u32[]{:S(2)}, u32[]{:S(2)}) collective-permute-start(f32[64,256]{1,0:T(8,128)S(1)} %get-tuple-element.48), channel_id=1, source_target_pairs={{0,32},{64,96},{128,160},{192,224},{256,288},{320,352},{384,416},{... | collective-permute-start | bytes 196616 | tf_op jit(solution)/shard_map/ppermute | solution.py:218
  122.6 10.3 %collective-permute-start.9 = (f32[64,256]{1,0:T(8,128)S(1)}, f32[64,256]{1,0:T(8,128)S(1)}, u32[]{:S(2)}, u32[]{:S(2)}) collective-permute-start(f32[64,256]{1,0:T(8,128)S(1)} %get-tuple-element.48), channel_id=1, source_target_pairs={{32,64},{96,128},{160,192},{224,256},{288,320},{352,384},{416,448}... | collective-permute-start | bytes 196616 | tf_op jit(solution)/shard_map/ppermute | solution.py:218
  124.6 7.1 %collective-permute-start.10 = (f32[64,128]{1,0:T(8,128)S(1)}, f32[64,128]{1,0:T(8,128)S(1)}, u32[]{:S(2)}, u32[]{:S(2)}) collective-permute-start(f32[64,128]{1,0:T(8,128)S(1)} %get-tuple-element.49), channel_id=1, source_target_pairs={{1,2},{3,4},{5,6},{7,8},{9,10},{11,12},{13,14},{15,16},{17,18},{19... | collective-permute-start | bytes 98312 | tf_op jit(solution)/shard_map/ppermute | solution.py:218
  129.7 3.1 %collective-permute-start.11 = (f32[64,128]{1,0:T(8,128)S(1)}, f32[64,128]{1,0:T(8,128)S(1)}, u32[]{:S(2)}, u32[]{:S(2)}) collective-permute-start(f32[64,128]{1,0:T(8,128)S(1)} %get-tuple-element.50), channel_id=1, source_target_pairs={{0,1},{2,3},{4,5},{6,7},{8,9},{10,11},{12,13},{14,15},{16,17},{18,... | collective-permute-start | bytes 98312 | tf_op jit(solution)/shard_map/ppermute | solution.py:218
  133.5 26.2 %all-to-all-start.7 = ((f32[32,8,128]{2,1,0:T(8,128)}), f32[32,8,128]{2,1,0:T(8,128)S(1)}, u32[]{:S(2)}, u32[]{:S(2)}) async-start(f32[32,8,128]{2,1,0:T(8,128)} %get-tuple-element.55), calls=%async_computation.7 | async-start | bytes 262144 | tf_op jit(solution)/shard_map/all_to_all | solution.py:398
  142.7 17.1 %collective-permute-start.12 = (f32[64,256]{1,0:T(8,128)S(1)}, f32[64,256]{1,0:T(8,128)S(1)}, u32[]{:S(2)}, u32[]{:S(2)}) collective-permute-start(f32[64,256]{1,0:T(8,128)S(1)} %get-tuple-element.52.resp), channel_id=1, source_target_pairs={{0,32},{64,96},{128,160},{192,224},{256,288},{320,352},{384,416},{... | collective-permute-start | bytes 196616 | tf_op jit(solution)/shard_map/ppermute | solution.py:218
  146.7 13.0 %collective-permute-start.13 = (f32[64,256]{1,0:T(8,128)S(1)}, f32[64,256]{1,0:T(8,128)S(1)}, u32[]{:S(2)}, u32[]{:S(2)}) collective-permute-start(f32[64,256]{1,0:T(8,128)S(1)} %get-tuple-element.52.resp), channel_id=1, source_target_pairs={{32,64},{96,128},{160,192},{224,256},{288,320},{352,384},{416,448}... | collective-permute-start | bytes 196616 | tf_op jit(solution)/shard_map/ppermute | solution.py:218
  152.2 6.4 %collective-permute-start.14 = (f32[64,128]{1,0:T(8,128)S(1)}, f32[64,128]{1,0:T(8,128)S(1)}, u32[]{:S(2)}, u32[]{:S(2)}) collective-permute-start(f32[64,128]{1,0:T(8,128)S(1)} %get-tuple-element.53), channel_id=1, source_target_pairs={{1,2},{3,4},{5,6},{7,8},{9,10},{11,12},{13,14},{15,16},{17,18},{19... | collective-permute-start | bytes 98312 | tf_op jit(solution)/shard_map/ppermute | solution.py:218
  156.7 3.1 %collective-permute-start.15 = (f32[64,128]{1,0:T(8,128)S(1)}, f32[64,128]{1,0:T(8,128)S(1)}, u32[]{:S(2)}, u32[]{:S(2)}) collective-permute-start(f32[64,128]{1,0:T(8,128)S(1)} %get-tuple-element.54), channel_id=1, source_target_pairs={{0,1},{2,3},{4,5},{6,7},{8,9},{10,11},{12,13},{14,15},{16,17},{18,... | collective-permute-start | bytes 98312 | tf_op jit(solution)/shard_map/ppermute | solution.py:218
